TPU v7x, 256 devices: a whole 4x4x8 slice. The times are simulated.
256 devices in a mesh: dap: 8 (over z_lo, core), dp: 32 (over y, x, z_hi).
Axes of the slice: x: 4, y: 4, z: 8 (z_hi: 2, z_lo: 4; z = z_hi * 4 + z_lo), core: 2. Of those that a mesh axis runs over, the one named last changes fastest.
Arguments:
- pair_rep: bfloat16 [3072, 96, 128], P(('dp', 'dap')), parts along dimension 0, may hold values from -6 to 6
- cotangent: bfloat16 [3072, 96, 128], P(('dp', 'dap')), parts along dimension 0, may hold values from -6 to 6
- residue_mask: int32 [3072], P('dp'), parts along dimension 0, may hold values from 0 to 1, as said below
- ln_gain: float32 [2, 128], replicated, may hold values from 0.5 to 1.5
- ln_shift: float32 [2, 128], replicated, may hold values from -3 to 3
- w_proj: bfloat16 [2, 128, 512], replicated, may hold values from -2.828427 to 2.828427
- w_bias: bfloat16 [2, 128, 4], replicated, may hold values from -0.5 to 0.5
- gate_bias: float32 [2, 128], replicated, may hold values from -4 to 4
- w_out: bfloat16 [2, 128, 128], replicated, may hold values from -0.5 to 0.5
- out_bias: float32 [2, 128], replicated, may hold values from -3 to 3
Outputs:
- grad_pair: bfloat16 [3072, 96, 128], P(('dp', 'dap')), parts along dimension 0
- grad_gain: float32 [64, 128], P('dp'), parts along dimension 0
- grad_shift: float32 [64, 128], P('dp'), parts along dimension 0
- grad_proj: float32 [64, 128, 512], P('dp'), parts along dimension 0
- grad_bias_w: float32 [64, 128, 4], P('dp'), parts along dimension 0
- grad_gate: float32 [64, 128], P('dp'), parts along dimension 0
- grad_out_w: float32 [64, 128, 128], P('dp'), parts along dimension 0
- grad_out_bias: float32 [64, 128], P('dp'), parts along dimension 0
There are 32 independent parts, one for each index of `dp`. A program takes and returns all parts, laid end to end along the dimension named above; an argument that names none is the same for every part. Nothing has to cross between parts.
Inputs may be any that keep to these rules, and one draw needn't show every extreme that they name: residue_mask is 1 below a crop length of at least 48 and 0 from there on; the last position is always 0.
All inputs are finite; a program needn't handle non-finite values.
Results may differ from a plain program's by a relative error of at most 0.029.
The roundings to bfloat16 on the way count: a program that leaves them out, or rounds other values in their place, can miss the bound.
Values may be sent and summed in bfloat16 or wider, within the bound.
No kernel may reach another device: no remote copies, remote signals or barrier semaphores. Data moves between devices by JAX's collectives and lax.ppermute only.
A program may use at most 128 MiB of HBM per device.

v0:
```python
import jax
import jax.numpy as jnp
from jax import lax
from jax.sharding import PartitionSpec as P

HEAD_COUNT = 4
HEAD_WIDTH = 32
RESIDUES = 96


EPSILON = 1e-05


def layer_norm(inputs, gain, shift):
    floats = inputs.astype(jnp.float32)
    center = jnp.mean(floats, axis=-1, keepdims=True)
    spread = jnp.mean(jnp.square(floats - center), axis=-1, keepdims=True)
    inverse = lax.rsqrt(spread + EPSILON)
    normed = (floats - center) * inverse
    return ((normed * gain + shift).astype(jnp.bfloat16), normed, inverse)


def head_part(tensor, head_index):
    return tensor[..., head_index * HEAD_WIDTH : (head_index + 1) * HEAD_WIDTH]


def prepare(inputs, gain, shift, w_proj, w_bias, gate_bias):
    width = HEAD_COUNT * HEAD_WIDTH
    normed_x, normed, inverse = layer_norm(inputs, gain, shift)
    joint = jnp.dot(normed_x, w_proj, preferred_element_type=jnp.float32)
    scaling = HEAD_WIDTH ** (-0.5)
    query = (joint[..., :width] * scaling).astype(jnp.bfloat16)
    keys = joint[..., width : 2 * width].astype(jnp.bfloat16)
    values = joint[..., 2 * width : 3 * width].astype(jnp.bfloat16)
    gate = jax.nn.sigmoid(joint[..., 3 * width :] + gate_bias)
    bias_rows = jnp.dot(normed_x, w_bias, preferred_element_type=jnp.float32).astype(jnp.bfloat16)
    bias_full = lax.all_gather(jnp.transpose(bias_rows, (2, 0, 1)), "dap", axis=1, tiled=True)
    return (normed_x, normed, inverse, query, keys, values, gate, bias_full)


def head_probs(query_head, keys_head, bias_head, key_term):
    scores = jnp.einsum("ijc,ikc->ijk", query_head, keys_head, preferred_element_type=jnp.float32)
    scores = scores + bias_head.astype(jnp.float32)[None, :, :] + key_term[None, None, :]
    row_top = jnp.max(scores, axis=-1, keepdims=True)
    expo = jnp.exp(scores - row_top)
    return expo / jnp.sum(expo, axis=-1, keepdims=True)


def attend(state, key_term):
    normed_x, normed, inverse, query, keys, values, gate, bias_full = state
    pieces = []
    for head_index in range(HEAD_COUNT):
        probab = head_probs(
            head_part(query, head_index),
            head_part(keys, head_index),
            bias_full[head_index],
            key_term,
        ).astype(jnp.bfloat16)
        pieces.append(
            jnp.einsum(
                "ijk,ikc->ijc",
                probab,
                head_part(values, head_index),
                preferred_element_type=jnp.float32,
            )
        )
    return jnp.concatenate(pieces, axis=-1)


def module_output(inputs, state, attended, w_out, out_bias):
    gate = state[6]
    mixed = (gate * attended).astype(jnp.bfloat16)
    projected = jnp.dot(mixed, w_out, preferred_element_type=jnp.float32)
    return (inputs.astype(jnp.float32) + projected + out_bias).astype(jnp.bfloat16)


def module_backward(state, attended, gain, w_proj, w_bias, w_out, key_term, upstream):
    normed_x, normed, inverse, query, keys, values, gate, bias_full = state
    scaling = HEAD_WIDTH ** (-0.5)
    local_rows = query.shape[0]
    upstream_f = upstream.astype(jnp.float32)
    mixed = (gate * attended).astype(jnp.bfloat16)
    grad_out_w = jnp.einsum("rnd,rnc->dc", mixed, upstream, preferred_element_type=jnp.float32)
    grad_out_bias = jnp.sum(upstream_f, axis=(0, 1))
    grad_mixed = jnp.dot(upstream, w_out.T, preferred_element_type=jnp.float32)
    grad_att = (grad_mixed * gate).astype(jnp.bfloat16)
    grad_logit = (grad_mixed * attended * gate * (1.0 - gate)).astype(jnp.bfloat16)
    query_grads = []
    keys_grads = []
    values_grads = []
    partials = []
    for head_index in range(HEAD_COUNT):
        query_head = head_part(query, head_index)
        keys_head = head_part(keys, head_index)
        values_head = head_part(values, head_index)
        grad_head = head_part(grad_att, head_index)
        probab = head_probs(query_head, keys_head, bias_full[head_index], key_term)
        probab_b = probab.astype(jnp.bfloat16)
        grad_probs = jnp.einsum(
            "ijc,ikc->ijk", grad_head, values_head, preferred_element_type=jnp.float32
        )
        values_grads.append(
            jnp.einsum(
                "ijk,ijc->ikc", probab_b, grad_head, preferred_element_type=jnp.float32
            ).astype(jnp.bfloat16)
        )
        inner_sum = jnp.sum(probab * grad_probs, axis=-1, keepdims=True)
        grad_scores = probab * (grad_probs - inner_sum)
        scores_b = grad_scores.astype(jnp.bfloat16)
        query_grads.append(
            (
                jnp.einsum("ijk,ikc->ijc", scores_b, keys_head, preferred_element_type=jnp.float32)
                * scaling
            ).astype(jnp.bfloat16)
        )
        keys_grads.append(
            jnp.einsum(
                "ijk,ijc->ikc", scores_b, query_head, preferred_element_type=jnp.float32
            ).astype(jnp.bfloat16)
        )
        partials.append(jnp.sum(grad_scores, axis=0))
    partial_sum = jnp.stack(partials, axis=0)
    whole_sum = lax.psum(partial_sum, "dap")
    own_rows = lax.dynamic_slice_in_dim(
        whole_sum, lax.axis_index("dap") * local_rows, local_rows, 1
    )
    grad_bias_b = own_rows.astype(jnp.bfloat16)
    grad_joint = jnp.concatenate(query_grads + keys_grads + values_grads + [grad_logit], axis=-1)
    grad_proj = jnp.einsum("rnc,rnd->cd", normed_x, grad_joint, preferred_element_type=jnp.float32)
    grad_gate = jnp.sum(grad_logit.astype(jnp.float32), axis=(0, 1))
    grad_bias_w = jnp.einsum(
        "rnc,hrn->ch", normed_x, grad_bias_b, preferred_element_type=jnp.float32
    )
    grad_normed = jnp.dot(grad_joint, w_proj.T, preferred_element_type=jnp.float32)
    grad_normed = grad_normed + jnp.einsum(
        "hrn,ch->rnc", grad_bias_b, w_bias, preferred_element_type=jnp.float32
    )
    grad_gain = jnp.sum(grad_normed * normed, axis=(0, 1))
    grad_shift = jnp.sum(grad_normed, axis=(0, 1))
    scaled = grad_normed * gain
    grad_ln = inverse * (
        scaled
        - jnp.mean(scaled, axis=-1, keepdims=True)
        - normed * jnp.mean(scaled * normed, axis=-1, keepdims=True)
    )
    grads = lax.psum(
        (grad_gain, grad_shift, grad_proj, grad_bias_w, grad_gate, grad_out_w, grad_out_bias), "dap"
    )
    return (upstream_f + grad_ln, grads)


def per_device(
    pair_rep, cotangent, residue_mask, ln_gain, ln_shift, w_proj, w_bias, gate_bias, w_out, out_bias
):
    key_term = jnp.where(residue_mask > 0, 0.0, -1000000000.0).astype(jnp.float32)
    state_start = prepare(pair_rep, ln_gain[0], ln_shift[0], w_proj[0], w_bias[0], gate_bias[0])
    attended_start = attend(state_start, key_term)
    first = module_output(pair_rep, state_start, attended_start, w_out[0], out_bias[0])
    first_cols, upstream_cols = (
        lax.all_to_all(first, "dap", split_axis=1, concat_axis=0, tiled=True),
        lax.all_to_all(cotangent, "dap", split_axis=1, concat_axis=0, tiled=True),
    )
    first_t = jnp.transpose(first_cols, (1, 0, 2))
    upstream_t = jnp.transpose(upstream_cols, (1, 0, 2))
    state_end = prepare(first_t, ln_gain[1], ln_shift[1], w_proj[1], w_bias[1], gate_bias[1])
    attended_end = attend(state_end, key_term)
    grad_t, grads_end = module_backward(
        state_end, attended_end, ln_gain[1], w_proj[1], w_bias[1], w_out[1], key_term, upstream_t
    )
    grad_cols = jnp.transpose(grad_t.astype(jnp.bfloat16), (1, 0, 2))
    grad_first = lax.all_to_all(grad_cols, "dap", split_axis=0, concat_axis=1, tiled=True)
    grad_in, grads_start = module_backward(
        state_start,
        attended_start,
        ln_gain[0],
        w_proj[0],
        w_bias[0],
        w_out[0],
        key_term,
        grad_first,
    )
    stacked = [jnp.stack([left, right]) / RESIDUES for left, right in zip(grads_start, grads_end)]
    return (
        grad_in.astype(jnp.bfloat16),
        stacked[0],
        stacked[1],
        stacked[2],
        stacked[3],
        stacked[4],
        stacked[5],
        stacked[6],
    )


def solution(mesh):
    in_specs = (
        P(("dp", "dap"), None, None),
        P(("dp", "dap"), None, None),
        P("dp"),
        P(),
        P(),
        P(),
        P(),
        P(),
        P(),
        P(),
    )
    out_specs = (
        P(("dp", "dap"), None, None),
        P("dp", None),
        P("dp", None),
        P("dp", None, None),
        P("dp", None, None),
        P("dp", None),
        P("dp", None, None),
        P("dp", None),
    )
    return jax.shard_map(
        per_device, mesh=mesh, in_specs=in_specs, out_specs=out_specs, check_vma=False
    )
```

profile of v0, /device:TPU:1, one launch (start us, length us, event | category | flops | bytes accessed | tf_op | source)
XLA Modules:
  0.0 388.2 jit_solution(9611647681118727339)
XLA Ops:
  12.6 3.0 fusion.227
  16.1 17.0 %all_gather.6 = bf16[4,96,96]{2,0,1:T(4,128)(2,1)S(1)} all-gather(bf16[4,12,96]{2,0,1:T(4,128)(2,1)S(1)} %fusion.42), channel_id=1, replica_groups=mesh['dap'=8,'dp'=32] {'dap'}, dimensions={1}, use_global_device_ids=true | all-gather | bytes 82944 | tf_op jit(solution)/shard_map/all_gather | solution.py:37
  44.7 3.0 multiply_convert_fusion.5
  48.8 4.4 %all-to-all-start.1 = ((bf16[12,96,128]{2,0,1:T(8,128)(2,1)}), bf16[12,96,128]{2,0,1:T(8,128)(2,1)S(1)}, u32[]{:S(2)}, u32[]{:S(2)}) async-start(bf16[12,96,128]{2,0,1:T(8,128)(2,1)} %copy.476), calls=%async_computation.1 | async-start | bytes 786432 | tf_op jit(solution)/shard_map/all_to_all | solution.py:160
  54.0 10.8 %all-to-all-done.1 = bf16[12,96,128]{2,0,1:T(8,128)(2,1)S(1)} async-done(((bf16[12,96,128]{2,0,1:T(8,128)(2,1)}), bf16[12,96,128]{2,0,1:T(8,128)(2,1)S(1)}, u32[]{:S(2)}, u32[]{:S(2)}) %all-to-all-start.1) | async-done | bytes 294944 | tf_op jit(solution)/shard_map/all_to_all | solution.py:160
  64.8 4.2 %all-to-all-start = ((bf16[12,96,128]{2,0,1:T(8,128)(2,1)}), bf16[12,96,128]{2,0,1:T(8,128)(2,1)S(1)}, u32[]{:S(2)}, u32[]{:S(2)}) async-start(bf16[12,96,128]{2,0,1:T(8,128)(2,1)} %copy.449), calls=%async_computation | async-start | bytes 786432 | tf_op jit(solution)/shard_map/all_to_all | solution.py:161
  72.9 1.8 fusion.232
  74.7 6.0 %all-to-all-done = bf16[12,96,128]{2,0,1:T(8,128)(2,1)S(1)} async-done(((bf16[12,96,128]{2,0,1:T(8,128)(2,1)}), bf16[12,96,128]{2,0,1:T(8,128)(2,1)S(1)}, u32[]{:S(2)}, u32[]{:S(2)}) %all-to-all-start) | async-done | bytes 294944 | tf_op jit(solution)/shard_map/all_to_all | solution.py:161
  82.6 15.0 %all_gather.7 = bf16[4,96,96]{2,0,1:T(4,128)(2,1)S(1)} all-gather(bf16[4,12,96]{2,0,1:T(4,128)(2,1)} %fusion.43), channel_id=1, replica_groups=mesh['dap'=8,'dp'=32] {'dap'}, dimensions={1}, use_global_device_ids=true | all-gather | bytes 82944 | tf_op jit(solution)/shard_map/all_gather | solution.py:37
  105.3 2.0 fusion.25
  107.3 2.8 fusion.233
  110.0 2.5 fusion.89
  117.7 2.5 fusion.99
  125.2 2.5 fusion.109
  127.8 2.5 fusion.119
  130.3 3.8 convert_reduce_fusion.3
  148.4 1.8 convolution_convert_fusion.10
  152.0 1.8 convolution_convert_fusion.8
  164.3 4.6 %concatenate.14 = bf16[12,96,512]{2,1,0:T(8,128)(2,1)S(1)} concatenate(bf16[12,96,32]{2,1,0:T(8,128)(2,1)S(1)} %copy.535, bf16[12,96,32]{2,1,0:T(8,128)(2,1)} %copy.536, bf16[12,96,32]{2,1,0:T(8,128)(2,1)} %copy.537, bf16[12,96,32]{2,1,0:T(8,128)(2,1)} %copy.538, bf16[12,96,32]{2,1,0:T(8,128)(2,1)} %copy.539, bf16[12,96,32]{2,1,0:T(8,128)(2,1)} %copy.540, ...), dimensions={2} | concatenate | bytes 2359296 | tf_op jit(solution)/shard_map/concatenate | solution.py:128
  169.0 2.2 fusion.189
  173.9 25.2 %all-reduce.7 = bf16[4,96,96]{2,0,1:T(4,128)(2,1)S(1)} all-reduce(f32[4,96,96]{2,0,1:T(4,128)S(1)} %pad_maximum_fusion.2), channel_id=1, replica_groups=mesh['dap'=8,'dp'=32] {'dap'}, use_global_device_ids=true, to_apply=%region_28.29 | all-reduce | flops 36864 | bytes 221184 | tf_op jit(solution)/shard_map/psum | solution.py:123
  199.9 2.7 multiply_reduce_fusion
  204.3 7.5 %all-to-all-start.2 = ((bf16[96,12,128]{2,1,0:T(8,128)(2,1)}), bf16[96,12,128]{2,1,0:T(8,128)(2,1)S(1)}, u32[]{:S(2)}, u32[]{:S(2)}) async-start(bf16[96,12,128]{2,1,0:T(8,128)(2,1)} %copy.551), calls=%async_computation.2 | async-start | bytes 786432 | tf_op jit(solution)/shard_map/all_to_all | solution.py:171
  211.8 2.2 convolution_bitcast_fusion.2
  215.1 8.4 %all-to-all-done.2 = bf16[96,12,128]{2,1,0:T(8,128)(2,1)S(1)} async-done(((bf16[96,12,128]{2,1,0:T(8,128)(2,1)}), bf16[96,12,128]{2,1,0:T(8,128)(2,1)S(1)}, u32[]{:S(2)}, u32[]{:S(2)}) %all-to-all-start.2) | async-done | bytes 294944 | tf_op jit(solution)/shard_map/all_to_all | solution.py:171
  223.6 2.8 convert_reduce_fusion.4
  239.7 1.8 convolution_convert_fusion
  249.9 4.9 %concatenate.15 = bf16[12,96,512]{2,1,0:T(8,128)(2,1)S(1)} concatenate(bf16[12,96,32]{2,1,0:T(8,128)(2,1)S(1)} %copy.586, bf16[12,96,32]{2,1,0:T(8,128)(2,1)S(1)} %copy.587, bf16[12,96,32]{2,1,0:T(8,128)(2,1)S(1)} %copy.588, bf16[12,96,32]{2,1,0:T(8,128)(2,1)} %copy.589, bf16[12,96,32]{2,1,0:T(8,128)(2,1)} %copy.590, bf16[12,96,32]{2,1,0:T(8,128)(2,1)} %copy.591, ...), dimensions={2} | concatenate | bytes 2359296 | tf_op jit(solution)/shard_map/concatenate | solution.py:128
  259.4 25.5 %all-reduce.8 = bf16[4,96,96]{2,0,1:T(4,128)(2,1)S(1)} all-reduce(f32[4,96,96]{2,0,1:T(4,128)S(1)} %pad_maximum_fusion.3), channel_id=1, replica_groups=mesh['dap'=8,'dp'=32] {'dap'}, use_global_device_ids=true, to_apply=%region_39.40 | all-reduce | flops 36864 | bytes 221184 | tf_op jit(solution)/shard_map/psum | solution.py:123
  287.1 17.3 %all-reduce = (f32[1,128]{1,0:T(1,128)S(1)}, f32[1,128]{1,0:T(1,128)S(1)}, f32[1,128]{1,0:T(1,128)S(1)}, f32[1,128]{1,0:T(1,128)S(1)}, f32[1,128,4]{1,2,0:T(4,12...) all-reduce(f32[1,128]{1,0:T(1,128)S(1)} %bitcast.233, ...), channel_id=1, replica_groups=mesh['dap'=8,'dp'=32] {'dap'}, use_global_device_ids=true, to_apply=%region_45.46 | all-reduce | flops 2048 | bytes 16384 | tf_op jit(solution)/shard_map/psum | solution.py:146
  308.8 69.2 %all-reduce.6.cloned.1.call-done = (f32[1,128,512]{2,1,0:T(8,128)}, f32[1,128,512]{2,1,0:T(8,128)}, f32[1,128,128]{2,1,0:T(8,128)}, f32[1,128,128]{2,1,0:T(8,128)}) async-done(((f32[1,128,512]{2,1,0:T(8,128)}, f32[1,128,512]{2,1,0:T(8,128)}, f32[1,128,128]{2,1,0:T(8,128)}, f32[1,128,128]{2,1,0:T(8,128)}), (f32[1,128,512]{2,1,0:T(8,128)}, f32[1,128,512]{2,1,0:T(8,128)}, f32[1,128,128]{2,1,0:T(8,128)}, ...) | async-done | bytes 655376 | tf_op jit(solution)/shard_map/psum | solution.py:146
  378.0 1.9 maximum_multiply_fusion
  (317 shorter events, 109.3 us)
Async XLA Ops:
  8.4 36.2 %copy-start.70 = (f32[128]{0:T(128)}, f32[128]{0:T(128)S(1)}, u32[]{:S(2)}) copy-start(f32[128]{0:T(128)S(1)} %get-tuple-element.68) | copy-start | bytes 1540
  9.2 6.4 %copy-start.65 = (f32[128]{0:T(128)}, f32[128]{0:T(128)S(1)}, u32[]{:S(2)}) copy-start(f32[128]{0:T(128)S(1)} %get-tuple-element.72) | copy-start | bytes 1540
  10.0 5.6 %copy-start.59 = (f32[128]{0:T(128)}, f32[128]{0:T(128)S(1)}, u32[]{:S(2)}) copy-start(f32[128]{0:T(128)S(1)} %get-tuple-element.70) | copy-start | bytes 1540
  10.0 61.6 %copy-start.63 = (f32[128]{0:T(128)}, f32[128]{0:T(128)S(1)}, u32[]{:S(2)}) copy-start(f32[128]{0:T(128)S(1)} %get-tuple-element.69) | copy-start | bytes 1540
  15.6 27.9 %copy-start.1 = (bf16[12,96,512]{2,1,0:T(8,128)(2,1)}, bf16[12,96,512]{2,1,0:T(8,128)(2,1)S(1)}, u32[]{:S(2)}) copy-start(bf16[12,96,512]{2,1,0:T(8,128)(2,1)S(1)} %get-tuple-element.73) | copy-start | bytes 3538948
  15.6 17.7 %copy-start.78 = (s32[96]{0:T(128)S(1)}, s32[96]{0:T(128)}, u32[]{:S(2)}) copy-start(s32[96]{0:T(128)} %param.12) | copy-start | bytes 1156
  33.3 8.8 %copy-start.54 = (f32[96]{0:T(128)}, f32[96]{0:T(128)S(1)}, u32[]{:S(2)}) copy-start(f32[96]{0:T(128)S(1)} %compare_select_fusion) | copy-start | bytes 1156
  47.7 5.5 %copy-start.27 = (bf16[12,96,128]{2,1,0:T(8,128)(2,1)S(1)}, bf16[12,96,128]{2,1,0:T(8,128)(2,1)}, u32[]{:S(2)}) copy-start(bf16[12,96,128]{2,1,0:T(8,128)(2,1)} %param.11) | copy-start | bytes 884740
  48.8 16.0 %all-to-all-start.1 = ((bf16[12,96,128]{2,0,1:T(8,128)(2,1)}), bf16[12,96,128]{2,0,1:T(8,128)(2,1)S(1)}, u32[]{:S(2)}, u32[]{:S(2)}) async-start(bf16[12,96,128]{2,0,1:T(8,128)(2,1)} %copy.476), calls=%async_computation.1 | async-start | bytes 786432 | tf_op jit(solution)/shard_map/all_to_all | solution.py:160
  64.8 15.9 %all-to-all-start = ((bf16[12,96,128]{2,0,1:T(8,128)(2,1)}), bf16[12,96,128]{2,0,1:T(8,128)(2,1)S(1)}, u32[]{:S(2)}, u32[]{:S(2)}) async-start(bf16[12,96,128]{2,0,1:T(8,128)(2,1)} %copy.449), calls=%async_computation | async-start | bytes 786432 | tf_op jit(solution)/shard_map/all_to_all | solution.py:161
  69.6 3.3 copy-start.18
  71.6 3.1 copy-start.38
  130.3 3.8 copy-start.9
  130.3 3.8 copy-start.49
  134.1 9.7 %copy-start.79 = (bf16[12,96,128]{2,1,0:T(8,128)(2,1)}, bf16[12,96,128]{2,1,0:T(8,128)(2,1)S(1)}, u32[]{:S(2)}) copy-start(bf16[12,96,128]{2,1,0:T(8,128)(2,1)S(1)} %get-tuple-element.38) | copy-start | bytes 884740
  152.0 3.6 copy-start.25
  153.8 3.6 copy-start.20
  153.8 4.4 %copy-start.22 = (bf16[12,96,32]{1,2,0:T(8,128)(2,1)S(1)}, bf16[12,96,32]{1,2,0:T(8,128)(2,1)}, u32[]{:S(2)}) copy-start(bf16[12,96,32]{1,2,0:T(8,128)(2,1)} %convolution_convert_fusion.14) | copy-start | bytes 221188
  154.6 4.6 %copy-start.24 = (bf16[12,96,32]{1,2,0:T(8,128)(2,1)S(1)}, bf16[12,96,32]{1,2,0:T(8,128)(2,1)}, u32[]{:S(2)}) copy-start(bf16[12,96,32]{1,2,0:T(8,128)(2,1)} %convolution_convert_fusion.13) | copy-start | bytes 221188
  169.0 3.2 copy-start.29
  199.1 3.5 copy-start.55
  199.1 3.5 copy-start.56
  199.1 3.5 copy-start.64
  203.4 8.4 %copy-start.76 = (f32[128]{0:T(128)S(1)}, f32[128]{0:T(128)}, u32[]{:S(2)}) copy-start(f32[128]{0:T(128)} %get-tuple-element.67) | copy-start | bytes 1540
  204.3 19.2 %all-to-all-start.2 = ((bf16[96,12,128]{2,1,0:T(8,128)(2,1)}), bf16[96,12,128]{2,1,0:T(8,128)(2,1)S(1)}, u32[]{:S(2)}, u32[]{:S(2)}) async-start(bf16[96,12,128]{2,1,0:T(8,128)(2,1)} %copy.551), calls=%async_computation.2 | async-start | bytes 786432 | tf_op jit(solution)/shard_map/all_to_all | solution.py:171
  211.8 166.2 %all-reduce.6.cloned.1.call-start = ((), (), s32[]{:S(2)}) async-start(), calls=%async_computation.3 | async-start | bytes 1310720 | tf_op jit(solution)/shard_map/psum | solution.py:146
  214.0 9.6 %copy-start.19 = (f32[12,96,128]{2,1,0:T(8,128)S(1)}, f32[12,96,128]{2,1,0:T(8,128)}, u32[]{:S(2)}) copy-start(f32[12,96,128]{2,1,0:T(8,128)} %get-tuple-element.36) | copy-start | bytes 1769476
  214.0 9.6 %copy-start.71 = (f32[128]{0:T(128)S(1)}, f32[128]{0:T(128)}, u32[]{:S(2)}) copy-start(f32[128]{0:T(128)} %copy-done.70) | copy-start | bytes 1540
  215.1 8.5 %copy-start.58 = (bf16[2,128,128]{2,1,0:T(8,128)(2,1)S(1)}, bf16[2,128,128]{2,1,0:T(8,128)(2,1)}, u32[]{:S(2)}) copy-start(bf16[2,128,128]{2,1,0:T(8,128)(2,1)} %param.18) | copy-start | bytes 196612
  226.4 5.9 %copy-start.81 = (bf16[12,96,128]{2,1,0:T(8,128)(2,1)}, bf16[12,96,128]{2,1,0:T(8,128)(2,1)S(1)}, u32[]{:S(2)}) copy-start(bf16[12,96,128]{2,1,0:T(8,128)(2,1)S(1)} %get-tuple-element.37) | copy-start | bytes 884740
  257.8 27.5 %copy-start.61 = (f32[128]{0:T(128)S(1)}, f32[128]{0:T(128)}, u32[]{:S(2)}) copy-start(f32[128]{0:T(128)} %copy-done.59) | copy-start | bytes 1540
  257.8 27.5 %copy-start.68 = (bf16[2,128,4]{1,2,0:T(4,128)(2,1)S(1)}, bf16[2,128,4]{1,2,0:T(4,128)(2,1)}, u32[]{:S(2)}) copy-start(bf16[2,128,4]{1,2,0:T(4,128)(2,1)} %param.16) | copy-start | bytes 6148
  (55 other events, 110.9 us)
Sparse Core Ops, SparseCore 0:
  307.4 70.5 all-reduce.5
where the time goes:
time: 392 us; the launch traced here: 388 us
  blocking collectives  100 us (26%)
  waiting for transfers between devices  94.5 us (24%)
  matrix products  77 us (20%)
  local copies, waits for them, and re-layouts  46 us (12%)
  other arithmetic  39.5 us (10%)
  starting transfers between devices  16 us (4%)
  between operations  15.2 us (4%)
    psum x1, waiting for transfers between devices, module_backward(): lax.psum((grad_gain, grad_shift, grad_proj, grad_bias_w, grad_gate, grad_...  69.2 us
    psum x2, blocking collectives, module_backward(): whole_sum = lax.psum(partial_sum, 'dap')  50.7 us
    all_gather x2, blocking collectives, prepare(): lax.all_gather(jnp.transpose(bias_rows, (2, 0, 1)), 'dap', axis=1, tiled=...  32 us
    psum x1, blocking collectives, module_backward(): lax.psum((grad_gain, grad_shift, grad_proj, grad_bias_w, grad_gate, grad_...  17.3 us
    dot_general x8, matrix products, module_backward(): jnp.einsum('ijk,ijc->ikc', probab_b, grad_head, preferred_element_type=jn...  14.1 us
    dot_general x8, matrix products, attend(): jnp.einsum('ijk,ikc->ijc', probab, head_part(values, head_index), preferr...  14 us
    sub x8, other arithmetic, head_probs(): expo = jnp.exp(scores - row_top)  11.6 us
    all_to_all x1, waiting for transfers between devices, per_device(): lax.all_to_all(first, 'dap', split_axis=1, concat_axis=0, tiled=True)  10.8 us
  transfers between devices with their start and end apart: 4, of which 4 were waited for; matrix products, arithmetic and copies ran while one was open for 3% of the time, Pallas kernels for 0%

commit v1 on v0

v1 whole, which is shorter than its diff:
```python
import jax
import jax.numpy as jnp
from jax import lax
from jax.experimental import pallas as pl
from jax.experimental.pallas import tpu as pltpu
from jax.sharding import PartitionSpec as P

HEADS = 4
WIDTH = 32
CH = 128
N = 96
GROUP = 8
ROWS = N // GROUP
CELLS = ROWS * N
BLOCK = ROWS * ROWS
BROWS = HEADS * ROWS
PACK = BLOCK + BROWS
SLICE = CH // GROUP
WROWS = 5 * SLICE
EPSILON = 1e-05
SCALING = WIDTH ** (-0.5)
F32 = jnp.float32
BF16 = jnp.bfloat16


def dot_nn(a, b):
    return lax.dot_general(a, b, (((1,), (0,)), ((), ())), preferred_element_type=F32)


def dot_nt(a, b):
    return lax.dot_general(a, b, (((1,), (1,)), ((), ())), preferred_element_type=F32)


def dot_tn(a, b):
    return lax.dot_general(a, b, (((0,), (0,)), ((), ())), preferred_element_type=F32)


def normalise(x):
    center = jnp.mean(x, axis=-1, keepdims=True)
    moved = x - center
    spread = jnp.mean(jnp.square(moved), axis=-1, keepdims=True)
    inverse = lax.rsqrt(spread + EPSILON)
    return moved * inverse, inverse


def norm_back(grad_normed, gain, normed, inverse):
    scaled = grad_normed * gain
    return inverse * (
        scaled
        - jnp.mean(scaled, axis=-1, keepdims=True)
        - normed * jnp.mean(scaled * normed, axis=-1, keepdims=True)
    )


def fold8(x):
    return jnp.sum(x.reshape(x.shape[0] // 8, 8, x.shape[1]), axis=0)


def head_stack(x):
    lane = lax.broadcasted_iota(jnp.int32, x.shape, 1) // WIDTH
    zero = jnp.zeros_like(x)
    return jnp.concatenate([jnp.where(lane == h, x, zero) for h in range(HEADS)], axis=0)


def head_pick(x):
    lane = lax.broadcasted_iota(jnp.int32, (N, CH), 1) // WIDTH
    out = x[0:N]
    for h in range(1, HEADS):
        out = jnp.where(lane == h, x[h * N : (h + 1) * N], out)
    return out


def project(nx, w_proj, gate_bias):
    joint = dot_nn(nx, w_proj)
    q = (joint[:, 0:CH] * SCALING).astype(BF16)
    k = joint[:, CH : 2 * CH].astype(BF16)
    v = joint[:, 2 * CH : 3 * CH].astype(BF16)
    gate = jax.nn.sigmoid(joint[:, 3 * CH :] + gate_bias)
    return q, k, v, gate


def probabilities(q, k, bias_ref):
    scores = dot_nt(head_stack(k), q)
    out = []
    for h in range(HEADS):
        s = scores[h * N : (h + 1) * N] + bias_ref[h]
        e = jnp.exp(s - jnp.max(s, axis=0, keepdims=True))
        out.append(e * (1.0 / jnp.sum(e, axis=0, keepdims=True)))
    return out


def weighted(x, mats):
    x_t = x.T
    parts = [dot_nn(x_t[h * WIDTH : (h + 1) * WIDTH], mats[h]) for h in range(HEADS)]
    return jnp.concatenate(parts, axis=0).T


def key_column(mask_ref):
    row = jnp.where(mask_ref[...] > 0, 0.0, -1000000000.0).astype(F32)
    wide = jnp.broadcast_to(row, (N, N))
    diag = lax.broadcasted_iota(jnp.int32, (N, N), 0) == lax.broadcasted_iota(jnp.int32, (N, N), 1)
    return jnp.sum(jnp.where(diag, wide, 0.0), axis=1, keepdims=True)


def attention_back(probs, q, k, v, grad_att, sum_ref):
    grad_probs = dot_nt(head_stack(v), grad_att)
    probs_b = []
    scores_b = []
    for h in range(HEADS):
        p = probs[h]
        gp = grad_probs[h * N : (h + 1) * N]
        inner = jnp.sum(p * gp, axis=0, keepdims=True)
        ds = p * (gp - inner)
        sum_ref[h] += ds
        probs_b.append(p.astype(BF16))
        scores_b.append(ds.astype(BF16))
    grad_v = head_pick(dot_nn(jnp.concatenate(probs_b, axis=0), grad_att)).astype(BF16)
    grad_k = head_pick(dot_nn(jnp.concatenate(scores_b, axis=0), q)).astype(BF16)
    grad_q = (weighted(k, scores_b) * SCALING).astype(BF16)
    return grad_q, grad_k, grad_v


def bias_rows(nx, w_bias_t):
    return dot_nt(w_bias_t, nx)


def w_bias_rows(w_bias_ref, m):
    wide = jnp.concatenate([w_bias_ref[m].astype(F32), jnp.zeros((CH, CH - HEADS), F32)], axis=1)
    return wide.T[0:8].astype(BF16)


def k1_body(x_ref, cot_ref, gain_ref, shift_ref, wb_ref, nx_ref, msg_ref, bias_s, cot_s):
    gain, shift = gain_ref[0:1], shift_ref[0:1]
    wb = w_bias_rows(wb_ref, 0)

    def row(i, _):
        normed, _inv = normalise(x_ref[i].astype(F32))
        nx = (normed * gain + shift).astype(BF16)
        nx_ref[i] = nx
        bias_s[i, :, 0:N] = bias_rows(nx, wb)[0:HEADS]
        cot_s[pl.ds(i, N, stride=ROWS), :] = cot_ref[i].astype(F32)
        return 0

    bias_s[...] = jnp.zeros_like(bias_s)
    lax.fori_loop(0, ROWS, row, 0)
    bias = bias_s[...].reshape(BROWS, CH).astype(BF16)
    for e in range(GROUP):
        msg_ref[e, 0:BLOCK] = cot_s[e * BLOCK : (e + 1) * BLOCK].astype(BF16)
        msg_ref[e, BLOCK:PACK] = bias


def k1b_body(nx_ref, wp_ref, gb_ref, q_ref, k_ref, v_ref, gate_ref):
    def row(i, _):
        q, k, v, gate = project(nx_ref[i], wp_ref[0], gb_ref[0:1])
        q_ref[i] = q
        k_ref[i] = k
        v_ref[i] = v
        gate_ref[i] = gate
        return 0

    lax.fori_loop(0, ROWS, row, 0)


def gather_rows(recv_ref, flat_s, row_s):
    for d in range(GROUP):
        flat_s[d * BLOCK : (d + 1) * BLOCK] = recv_ref[d, 0:BLOCK].astype(F32)
    for i in range(ROWS):
        for d in range(GROUP):
            at = d * BLOCK + i * ROWS
            row_s[i, d * ROWS : (d + 1) * ROWS] = flat_s[at : at + ROWS]


def k2_body(
    x_ref, q_ref, k_ref, v_ref, gate_ref, recv_ref, mask_ref, wo_ref, ob_ref, gain_ref, shift_ref, wb_ref,
    att_ref, first_ref, bias_ref, msg_ref, raw_s, bias_s, first_s,
):
    key = key_column(mask_ref)
    for d in range(GROUP):
        raw_s[d * BROWS : (d + 1) * BROWS] = recv_ref[d, BLOCK:PACK].astype(F32)
    for h in range(HEADS):
        bias_ref[h] = raw_s[pl.ds(h, N, stride=HEADS), :].T[0:N] + key
    wb = w_bias_rows(wb_ref, 1)
    w_out = wo_ref[0]
    out_bias = ob_ref[0:1]
    gain, shift = gain_ref[1:2], shift_ref[1:2]
    bias_s[...] = jnp.zeros_like(bias_s)

    def row(i, _):
        probs = probabilities(q_ref[i], k_ref[i], bias_ref)
        att = weighted(v_ref[i], [p.astype(BF16) for p in probs])
        att_ref[i] = att
        mixed = (gate_ref[i] * att).astype(BF16)
        first = (x_ref[i].astype(F32) + dot_nn(mixed, w_out) + out_bias).astype(BF16)
        first_ref[i] = first
        first_f = first.astype(F32)
        first_s[pl.ds(i, N, stride=ROWS), :] = first_f
        normed, _inv = normalise(first_f)
        nx = (normed * gain + shift).astype(BF16)
        bias_s[i, :, 0:N] = bias_rows(nx, wb)[0:HEADS]
        return 0

    lax.fori_loop(0, ROWS, row, 0)
    bias = bias_s[...].reshape(BROWS, CH).astype(BF16)
    for e in range(GROUP):
        msg_ref[e, 0:BLOCK] = first_s[e * BLOCK : (e + 1) * BLOCK].astype(BF16)
        msg_ref[e, BLOCK:PACK] = bias


def weight_grads(nx_s, joint_s, mixed_s, up_s, out_ref):
    nx = nx_s[...]
    for block in range(4):
        part = dot_tn(nx, joint_s[:, block * CH : (block + 1) * CH]).astype(BF16)
        for e in range(GROUP):
            out_ref[e, block * SLICE : (block + 1) * SLICE] = part[e * SLICE : (e + 1) * SLICE]
    part = dot_tn(mixed_s[...], up_s[...]).astype(BF16)
    for e in range(GROUP):
        out_ref[e, 4 * SLICE : 5 * SLICE] = part[e * SLICE : (e + 1) * SLICE]


def k3_body(
    recv0_ref, recv1_ref, mask_ref, gain_ref, shift_ref, wp_ref, wb_ref, gb_ref, wo_ref,
    msg_ref, wg_ref, small_ref,
    flat_s, x_s, up_s, raw_s, bias_s, sum_s, nx_s, joint_s, mixed_s, upb_s,
):
    key = key_column(mask_ref)
    for d in range(GROUP):
        raw_s[d * BROWS : (d + 1) * BROWS] = recv1_ref[d, BLOCK:PACK].astype(F32)
    for h in range(HEADS):
        bias_s[h] = raw_s[pl.ds(h, N, stride=HEADS), :][:, 0:N] + key
    gather_rows(recv0_ref, flat_s, up_s)
    gather_rows(recv1_ref, flat_s, x_s)
    sum_s[...] = jnp.zeros_like(sum_s)
    small_ref[...] = jnp.zeros_like(small_ref)
    gain, shift = gain_ref[1:2], shift_ref[1:2]
    gate_bias = gb_ref[1:2]

    def row(i, _):
        normed, inverse = normalise(x_s[i])
        nx = (normed * gain + shift).astype(BF16)
        nx_s[pl.ds(i * N, N), :] = nx
        q, k, v, gate = project(nx, wp_ref[1], gate_bias)
        probs = probabilities(q, k, bias_s)
        att = weighted(v, [p.astype(BF16) for p in probs])
        mixed_s[pl.ds(i * N, N), :] = (gate * att).astype(BF16)
        up_f = up_s[i]
        up = up_f.astype(BF16)
        upb_s[pl.ds(i * N, N), :] = up
        grad_mixed = dot_nt(up, wo_ref[1])
        grad_att = (grad_mixed * gate).astype(BF16)
        grad_logit = (grad_mixed * att * gate * (1.0 - gate)).astype(BF16)
        grad_q, grad_k, grad_v = attention_back(probs, q, k, v, grad_att, sum_s)
        joint = jnp.concatenate([grad_q, grad_k, grad_v, grad_logit], axis=1)
        joint_s[pl.ds(i * N, N), :] = joint
        grad_normed = dot_nt(joint, wp_ref[1])
        flat_s[pl.ds(i, N, stride=ROWS), :] = norm_back(grad_normed, gain, normed, inverse)
        small_ref[0:8] += fold8(grad_normed * normed)
        small_ref[8:16] += fold8(grad_normed)
        small_ref[16:24] += fold8(grad_logit.astype(F32))
        small_ref[24:32] += fold8(up_f)
        return 0

    lax.fori_loop(0, ROWS, row, 0)
    for e in range(GROUP):
        msg_ref[e, 0:BLOCK] = flat_s[e * BLOCK : (e + 1) * BLOCK].astype(BF16)
        rows = [sum_s[h, e * ROWS : (e + 1) * ROWS] for h in range(HEADS)]
        msg_ref[e, BLOCK:PACK, 0:N] = jnp.concatenate(rows, axis=0).astype(BF16)
        msg_ref[e, BLOCK:PACK, N:CH] = jnp.zeros((BROWS, CH - N), BF16)
    weight_grads(nx_s, joint_s, mixed_s, upb_s, wg_ref)


def bias_sum(recv_ref, start, gb_s):
    total = recv_ref[0, start : start + BROWS].astype(F32)
    for d in range(1, GROUP):
        total += recv_ref[d, start : start + BROWS].astype(F32)
    gb_s[...] = jnp.zeros_like(gb_s)
    total = total.astype(BF16).astype(F32)
    for r in range(ROWS):
        for h in range(HEADS):
            gb_s[r * 8 + h : r * 8 + h + 1] = total[h * ROWS + r : h * ROWS + r + 1]
    return gb_s[...].T[0:N].astype(BF16)


def bias_part(i, gb_s, gb_t, wb_tiled, nx):
    rows = lax.broadcasted_iota(jnp.int32, (ROWS * 8, CH), 0) // 8
    picked = jnp.where(rows == i, wb_tiled, jnp.zeros_like(wb_tiled))
    grad_w = dot_nn(gb_s[pl.ds(pl.multiple_of(i * 8, 8), 8), 0:N].astype(BF16), nx)
    return dot_nn(gb_t, picked), grad_w


def k4_body(
    recv_ref, first_ref, cot_ref, x_ref, q_ref, k_ref, v_ref, gate_ref, att_ref, nx_ref, bias_ref,
    gain_ref, shift_ref, wp_ref, wb_ref, wo_ref, small1_ref, wg1_ref,
    up_ref, gn_ref, msg_ref, small_ref,
    flat_s, la_s, gb_s, sum_s, nx_s, joint_s, mixed_s, upb_s,
):
    gather_rows(recv_ref, flat_s, la_s)
    gb_t = bias_sum(recv_ref, BLOCK, gb_s)
    wb = w_bias_rows(wb_ref, 1)
    wb_tiled = jnp.concatenate([wb.astype(F32)] * ROWS, axis=0).astype(BF16)
    sum_s[...] = jnp.zeros_like(sum_s)
    small_ref[...] = jnp.zeros_like(small_ref)
    small_ref[0:32] = small1_ref[...]
    gain1, shift1 = gain_ref[1:2], shift_ref[1:2]

    def row(i, _):
        normed, inverse = normalise(first_ref[i].astype(F32))
        nx1 = (normed * gain1 + shift1).astype(BF16)
        from_bias, grad_w = bias_part(i, gb_s, gb_t, wb_tiled, nx1)
        small_ref[0:8] += fold8(from_bias * normed)
        small_ref[8:16] += fold8(from_bias)
        small_ref[32:40] += grad_w
        up_f = cot_ref[i].astype(F32) + la_s[i] + norm_back(from_bias, gain1, normed, inverse)
        up = up_f.astype(BF16)
        up_f = up.astype(F32)
        up_ref[i] = up
        upb_s[pl.ds(i * N, N), :] = up
        nx_s[pl.ds(i * N, N), :] = nx_ref[i]

        q, k, v, gate, att = q_ref[i], k_ref[i], v_ref[i], gate_ref[i], att_ref[i]
        probs = probabilities(q, k, bias_ref)
        mixed_s[pl.ds(i * N, N), :] = (gate * att).astype(BF16)
        grad_mixed = dot_nt(up, wo_ref[0])
        grad_att = (grad_mixed * gate).astype(BF16)
        grad_logit = (grad_mixed * att * gate * (1.0 - gate)).astype(BF16)
        grad_q, grad_k, grad_v = attention_back(probs, q, k, v, grad_att, sum_s)
        joint = jnp.concatenate([grad_q, grad_k, grad_v, grad_logit], axis=1)
        joint_s[pl.ds(i * N, N), :] = joint
        gn_ref[i] = dot_nt(joint, wp_ref[0])
        small_ref[40:48] += fold8(grad_logit.astype(F32))
        small_ref[48:56] += fold8(up_f)
        return 0

    lax.fori_loop(0, ROWS, row, 0)
    for h in range(HEADS):
        flat_s[h * N : (h + 1) * N, 0:N] = sum_s[h].T
    for e in range(GROUP):
        rows = [flat_s[h * N + e * ROWS : h * N + (e + 1) * ROWS, 0:N] for h in range(HEADS)]
        msg_ref[e, 2 * WROWS : 2 * WROWS + BROWS, 0:N] = jnp.concatenate(rows, axis=0).astype(BF16)
        msg_ref[e, 2 * WROWS : 2 * WROWS + BROWS, N:CH] = jnp.zeros((BROWS, CH - N), BF16)
        msg_ref[e, WROWS : 2 * WROWS] = wg1_ref[e]
    weight_grads(nx_s, joint_s, mixed_s, upb_s, msg_ref)


def split2(x):
    top = x.astype(BF16)
    return top, (x - top.astype(F32)).astype(BF16)


def k5_body(
    recv_ref, x_ref, up_ref, gn_ref, nx_ref, small_in_ref, gain_ref, wb_ref,
    out_ref, msg_ref, gb_s, small_s,
):
    gb_t = bias_sum(recv_ref, 2 * WROWS, gb_s)
    wb = w_bias_rows(wb_ref, 0)
    wb_tiled = jnp.concatenate([wb.astype(F32)] * ROWS, axis=0).astype(BF16)
    gain = gain_ref[0:1]
    small_s[...] = jnp.zeros_like(small_s)

    def row(i, _):
        normed, inverse = normalise(x_ref[i].astype(F32))
        from_bias, grad_w = bias_part(i, gb_s, gb_t, wb_tiled, nx_ref[i])
        grad_normed = gn_ref[i] + from_bias
        small_s[0:8] += fold8(grad_normed * normed)
        small_s[8:16] += fold8(grad_normed)
        small_s[16:24] += grad_w
        back = norm_back(grad_normed, gain, normed, inverse)
        out_ref[i] = (up_ref[i].astype(F32) + back).astype(BF16)
        return 0

    lax.fori_loop(0, ROWS, row, 0)
    total = recv_ref[0, 0 : 2 * WROWS].astype(F32)
    for d in range(1, GROUP):
        total += recv_ref[d, 0 : 2 * WROWS].astype(F32)
    total *= 1.0 / N
    total = total.astype(BF16)

    def one(x):
        return jnp.sum(x, axis=0, keepdims=True)

    rows = [
        one(small_s[0:8]), one(small_s[8:16]), one(small_in_ref[40:48]), one(small_in_ref[48:56]),
        small_s[16:20],
        one(small_in_ref[0:8]), one(small_in_ref[8:16]), one(small_in_ref[16:24]), one(small_in_ref[24:32]),
        small_in_ref[32:36],
    ]
    top, low = split2(jnp.concatenate(rows, axis=0))
    for e in range(GROUP):
        msg_ref[e, 0 : 2 * WROWS] = total
        msg_ref[e, 2 * WROWS : 2 * WROWS + 16] = top
        msg_ref[e, 2 * WROWS + 16 : 2 * WROWS + 32] = low


def k6_body(recv_ref, gain_ref, shift_ref, proj_ref, wb_ref, gate_ref, ow_ref, ob_ref):
    small = jnp.zeros((16, CH), F32)
    for d in range(GROUP):
        for m in range(2):
            for block in range(4):
                at = m * WROWS + block * SLICE
                proj_ref[m, d * SLICE : (d + 1) * SLICE, block * CH : (block + 1) * CH] = recv_ref[
                    d, at : at + SLICE
                ].astype(F32)
            at = m * WROWS + 4 * SLICE
            ow_ref[m, d * SLICE : (d + 1) * SLICE] = recv_ref[d, at : at + SLICE].astype(F32)
        at = 2 * WROWS
        small += recv_ref[d, at : at + 16].astype(F32) + recv_ref[d, at + 16 : at + 32].astype(F32)
    small = small * (1.0 / N)
    for m in range(2):
        at = m * 8
        gain_ref[m : m + 1] = small[at : at + 1]
        shift_ref[m : m + 1] = small[at + 1 : at + 2]
        gate_ref[m : m + 1] = small[at + 2 : at + 3]
        ob_ref[m : m + 1] = small[at + 3 : at + 4]
        wide = jnp.concatenate([small[at + 4 : at + 8], jnp.zeros((CH - HEADS, CH), F32)], axis=0)
        wb_ref[m] = wide.T[:, 0:HEADS]


def call(body, outs, scratch, name, flops=100000000):
    return pl.pallas_call(
        body,
        out_shape=[jax.ShapeDtypeStruct(shape, dtype) for shape, dtype in outs],
        scratch_shapes=[pltpu.VMEM(shape, dtype) for shape, dtype in scratch],
        compiler_params=pltpu.CompilerParams(vmem_limit_bytes=40 * 1024 * 1024),
        cost_estimate=pl.CostEstimate(flops=flops, bytes_accessed=2000000, transcendentals=500000),
        name=name,
    )


def swap(x):
    return lax.all_to_all(x, "dap", 0, 0, tiled=True)


def per_device(
    pair_rep, cotangent, residue_mask, ln_gain, ln_shift, w_proj, w_bias, gate_bias, w_out, out_bias
):
    mask = residue_mask.reshape(1, N)
    rows_b = ((ROWS, N, CH), BF16)
    rows_f = ((ROWS, N, CH), F32)
    flat_f = ((CELLS, CH), F32)
    flat_b = ((CELLS, CH), BF16)
    pack = ((GROUP, PACK, CH), BF16)
    mats = ((HEADS, N, N), F32)
    raw = ((GROUP * BROWS, CH), F32)
    own_bias = ((ROWS, HEADS, CH), F32)
    weights = [flat_b, ((CELLS, 4 * CH), BF16), flat_b, flat_b]

    nx, msg0 = call(k1_body, [rows_b, pack], [own_bias, flat_f], "norm_first")(
        pair_rep, cotangent, ln_gain, ln_shift, w_bias
    )
    recv0 = swap(msg0)
    q, k, v, gate = call(k1b_body, [rows_b, rows_b, rows_b, rows_f], [], "project_first")(
        nx, w_proj, gate_bias
    )
    att, first, bias0, msg1 = call(
        k2_body, [rows_f, rows_b, mats, pack], [raw, own_bias, flat_f], "attend_first"
    )(pair_rep, q, k, v, gate, recv0, mask, w_out, out_bias, ln_gain, ln_shift, w_bias)
    recv1 = swap(msg1)
    msg2, wg1, small1 = call(
        k3_body,
        [pack, ((GROUP, WROWS, CH), BF16), ((32, CH), F32)],
        [flat_f, rows_f, rows_f, raw, mats, mats] + weights,
        "second_module",
    )(recv0, recv1, mask, ln_gain, ln_shift, w_proj, w_bias, gate_bias, w_out)
    recv2 = swap(msg2)
    up, gn, msg3, small = call(
        k4_body,
        [rows_b, rows_f, ((GROUP, 2 * WROWS + BROWS, CH), BF16), ((56, CH), F32)],
        [flat_f, rows_f, ((ROWS * 8, CH), F32), mats] + weights,
        "back_first",
    )(
        recv2, first, cotangent, pair_rep, q, k, v, gate, att, nx, bias0,
        ln_gain, ln_shift, w_proj, w_bias, w_out, small1, wg1,
    )
    recv3 = swap(msg3)
    grad_pair, msg4 = call(
        k5_body,
        [rows_b, ((GROUP, 2 * WROWS + 32, CH), BF16)],
        [((ROWS * 8, CH), F32), ((24, CH), F32)],
        "grad_pair",
    )(recv3, pair_rep, up, gn, nx, small, ln_gain, w_bias)
    recv4 = swap(msg4)
    grad_gain, grad_shift, grad_proj, grad_bias_w, grad_gate, grad_out_w, grad_out_bias = call(
        k6_body,
        [
            ((2, CH), F32), ((2, CH), F32), ((2, CH, 4 * CH), F32), ((2, CH, HEADS), F32),
            ((2, CH), F32), ((2, CH, CH), F32), ((2, CH), F32),
        ],
        [],
        "weight_sums",
    )(recv4)
    return (
        grad_pair, grad_gain, grad_shift, grad_proj, grad_bias_w, grad_gate, grad_out_w, grad_out_bias
    )


def solution(mesh):
    in_specs = (
        P(("dp", "dap"), None, None),
        P(("dp", "dap"), None, None),
        P("dp"),
        P(),
        P(),
        P(),
        P(),
        P(),
        P(),
        P(),
    )
    out_specs = (
        P(("dp", "dap"), None, None),
        P("dp", None),
        P("dp", None),
        P("dp", None, None),
        P("dp", None, None),
        P("dp", None),
        P("dp", None, None),
        P("dp", None),
    )
    return jax.shard_map(
        per_device, mesh=mesh, in_specs=in_specs, out_specs=out_specs, check_vma=False
    )
```

time: 392 us -> 134 us (0.34)
  waiting for transfers between devices: 94.5 us -> 8.92 us
  matrix products: 77 us -> 0 us
  Pallas kernels: 0 us -> 51.1 us
  local copies, waits for them, and re-layouts: 46 us -> 4.81 us
  other arithmetic: 39.5 us -> 0 us
  blocking collectives: 100 us -> 60.6 us
  between operations: 15.2 us -> 0.72 us
  starting transfers between devices: 16 us -> 7.53 us
    dot_general x65 -> x0, matrix products: 77 us -> none  [the longest x8 14.1 us: module_backward(): jnp.einsum('ijk,ijc->ikc', probab_b, grad_head, preferred_element_type=jn...]
    psum x1 -> x0, waiting for transfers between devices: 69.2 us -> none  [module_backward(): lax.psum((grad_gain, grad_shift, grad_proj, grad_bias_w, grad_gate, grad_...]
    psum x3 -> x0, blocking collectives: 68 us -> none  [the longest x2 50.7 us: module_backward(): whole_sum = lax.psum(partial_sum, 'dap')]
    all_to_all x0 -> x4, blocking collectives: none -> 60.6 us  [swap(): return lax.all_to_all(x, 'dap', 0, 0, tiled=True)]
    pallas_call x0 -> x7, Pallas kernels: none -> 51.1 us  [the longest x1 15.3 us: per_device(): call(k3_body, [pack, ((GROUP, WROWS, CH), BF16), ((32, CH), F32)], [flat_...]
    all_gather x2 -> x0, blocking collectives: 32 us -> none  [prepare(): lax.all_gather(jnp.transpose(bias_rows, (2, 0, 1)), 'dap', axis=1, tiled=...]
    convert_element_type x29 -> x0, local copies, waits for them, and re-layouts: 20.3 us -> none  [the longest x8 6.94 us: module_backward(): values_grads.append(jnp.einsum('ijk,ijc->ikc', probab_b, grad_head, prefe...]
    all_to_all x3 -> x1, waiting for transfers between devices: 25.3 us -> 8.92 us  [swap(): return lax.all_to_all(x, 'dap', 0, 0, tiled=True)]
  transfers between devices with their start and end apart: 4 -> 1, of which waited for: 4 -> 1; matrix products, arithmetic and copies ran while one was open for 3% -> 0% of each run, Pallas kernels for 0% -> 2%
where the time goes in v1:
time: 134 us
  blocking collectives  60.6 us (45%)
  Pallas kernels  51.1 us (38%)
  waiting for transfers between devices  8.92 us (7%)
  starting transfers between devices  7.53 us (6%)
  local copies, waits for them, and re-layouts  4.81 us (4%)
    all_to_all x4, blocking collectives, swap(): return lax.all_to_all(x, 'dap', 0, 0, tiled=True)  60.6 us
    pallas_call x1, Pallas kernels, per_device(): call(k3_body, [pack, ((GROUP, WROWS, CH), BF16), ((32, CH), F32)], [flat_...  15.3 us
    pallas_call x1, Pallas kernels, per_device(): call(k4_body, [rows_b, rows_f, ((GROUP, 2 * WROWS + BROWS, CH), BF16), ((...  13.9 us
    pallas_call x1, Pallas kernels, per_device(): call(k2_body, [rows_f, rows_b, mats, pack], [raw, own_bias, flat_f], 'att...  10.4 us
    all_to_all x1, waiting for transfers between devices, swap(): return lax.all_to_all(x, 'dap', 0, 0, tiled=True)  8.92 us
    all_to_all x1, starting transfers between devices, swap(): return lax.all_to_all(x, 'dap', 0, 0, tiled=True)  7.53 us
    unnamed x24, local copies, waits for them, and re-layouts  4.81 us
    pallas_call x1, Pallas kernels, per_device(): call(k1_body, [rows_b, pack], [own_bias, flat_f], 'norm_first')  4.54 us
  transfers between devices with their start and end apart: 1, of which 1 were waited for; matrix products, arithmetic and copies ran while one was open for 0% of the time, Pallas kernels for 2%

profile of v1, /device:TPU:1, one launch (start us, length us, event | category | flops | bytes accessed | tf_op | source)
XLA Modules:
  0.0 133.7 jit_solution(17886116139472752649)
XLA Ops:
  0.6 0.0 copy-start.6
  0.6 0.0 copy-start.7
  0.7 0.8 copy.18.wb_ref
  1.5 0.0 copy-done.6
  1.5 0.0 copy-done.7
  1.5 0.0 copy-start
  1.5 1.0 copy-done
  2.5 0.0 copy-start.4
  2.5 1.0 copy-done.4
  3.4 4.5 %norm_first.1 = (bf16[12,96,128]{2,1,0:T(8,128)(2,1)S(1)}, bf16[8,192,128]{2,1,0:T(8,128)(2,1)}) custom-call(bf16[12,96,128]{2,1,0:T(8,128)(2,1)S(1)} %copy-done, bf16[12,96,128]{2,1,0:T(8,128)(2,1)S(1)} %copy-done.4, f32[2,128]{1,0:T(2,128)S(1)} %copy-done.6, f32[2,128]{1,0:T(2,128)S(1)} %copy-done.7, bf16[2,128,4]{2,1,0:T(8,128)(2,1)S(1)} %copy.18.wb_ref), custom_call_target="tpu_custom_call" | custom-call | flops 100000000 | bytes 2000000 | tf_op jit(solution)/shard_map/norm_first/pallas_call | solution.py:446
  8.0 0.0 copy-start.2
  8.0 7.5 %all-to-all-start = ((bf16[8,192,128]{2,1,0:T(8,128)(2,1)}), bf16[8,192,128]{2,1,0:T(8,128)(2,1)S(1)}, u32[]{:S(2)}, u32[]{:S(2)}) async-start(bf16[8,192,128]{2,1,0:T(8,128)(2,1)} %get-tuple-element.34), calls=%async_computation | async-start | bytes 786432 | tf_op jit(solution)/shard_map/all_to_all | solution.py:429
  15.5 0.0 copy-done.2
  15.5 0.7 copy-done.10
  16.2 2.1 %project_first.1 = (bf16[12,96,128]{2,1,0:T(8,128)(2,1)S(1)}, bf16[12,96,128]{2,1,0:T(8,128)(2,1)S(1)}, bf16[12,96,128]{2,1,0:T(8,128)(2,1)S(1)}, f32[12,96,128]{2,1,0:T(8,128)S(1)}) custom-call(bf16[12,96,128]{2,1,0:T(8,128)(2,1)S(1)} %get-tuple-element.35.nx_ref, bf16[2,128,512]{2,1,0:T(8,128)(2,1)S(1)} %copy-done.2, f32[2,128]{1,0:T(2,128)S(1)} %copy-done.10), custom_call_target="tpu_custom_call" | custom-call | flops 100000000 | bytes 2000000 | tf_op jit(solution)/shard_map/project_first/pallas_call | solution.py:450
  18.3 8.9 %all-to-all-done.recv_ref.recv0_ref = bf16[8,192,128]{2,1,0:T(8,128)(2,1)S(1)} async-done(((bf16[8,192,128]{2,1,0:T(8,128)(2,1)}), bf16[8,192,128]{2,1,0:T(8,128)(2,1)S(1)}, u32[]{:S(2)}, u32[]{:S(2)}) %all-to-all-start) | async-done | bytes 393248 | tf_op jit(solution)/shard_map/all_to_all | solution.py:429
  27.2 0.0 copy-done.1
  27.2 0.0 copy-done.3
  27.2 0.6 copy-done.8
  27.8 0.0 copy-done.9
  27.9 10.4 %attend_first.1 = (f32[12,96,128]{2,1,0:T(8,128)S(1)}, bf16[12,96,128]{2,1,0:T(8,128)(2,1)S(1)}, f32[4,96,96]{2,1,0:T(8,128)S(1)}, bf16[8,192,128]{2,1,0:T(8,128)(2,1)S(1)}) custom-call(bf16[12,96,128]{2,1,0:T(8,128)(2,1)S(1)} %copy-done.1, bf16[12,96,128]{2,1,0:T(8,128)(2,1)S(1)} %get-tuple-element.36.q_ref, ...), custom_call_target="tpu_custom_call" | custom-call | flops 100000000 | bytes 2000000 | tf_op jit(solution)/shard_map/attend_first/pallas_call | solution.py:453
  38.3 14.9 %all_to_all.25.recv1_ref = bf16[8,192,128]{2,1,0:T(8,128)(2,1)S(1)} all-to-all(bf16[8,192,128]{2,1,0:T(8,128)(2,1)S(1)} %get-tuple-element.40), channel_id=1, replica_groups=mesh['dap'=8,'dp'=32] {'dap'}, dimensions={0} | all-to-all | bytes 786432 | tf_op jit(solution)/shard_map/all_to_all | solution.py:429
  53.3 15.3 %second_module.1 = (bf16[8,192,128]{2,1,0:T(8,128)(2,1)S(1)}, bf16[8,80,128]{2,1,0:T(8,128)(2,1)S(1)}, f32[32,128]{1,0:T(8,128)S(1)}) custom-call(bf16[8,192,128]{2,1,0:T(8,128)(2,1)S(1)} %all-to-all-done.recv_ref.recv0_ref, bf16[8,192,128]{2,1,0:T(8,128)(2,1)S(1)} %all_to_all.25.recv1_ref, s32[1,96]{1,0:T(1,128)S(1)} %bitcast.2, f32[2,128]{1,0:T(2,128)S(1)} %copy-done.6, ...), custom_call_target="tpu_custom_call" | custom-call | flops 100000000 | bytes 2000000 | tf_op jit(solution)/shard_map/second_module/pallas_call | solution.py:457
  68.6 0.0 copy-start.5
  68.6 15.1 %all_to_all.26.recv_ref = bf16[8,192,128]{2,1,0:T(8,128)(2,1)S(1)} all-to-all(bf16[8,192,128]{2,1,0:T(8,128)(2,1)S(1)} %get-tuple-element.41), channel_id=1, replica_groups=mesh['dap'=8,'dp'=32] {'dap'}, dimensions={0} | all-to-all | bytes 786432 | tf_op jit(solution)/shard_map/all_to_all | solution.py:429
  83.7 0.0 copy-done.5
  83.7 13.9 %back_first.1 = (bf16[12,96,128]{2,1,0:T(8,128)(2,1)S(1)}, f32[12,96,128]{2,1,0:T(8,128)S(1)}, bf16[8,208,128]{2,1,0:T(8,128)(2,1)S(1)}, f32[56,128]{1,0:T(8,128)S(1)}) custom-call(bf16[8,192,128]{2,1,0:T(8,128)(2,1)S(1)} %all_to_all.26.recv_ref, bf16[12,96,128]{2,1,0:T(8,128)(2,1)S(1)} %get-tuple-element.42.first_ref, bf16[12,96,128]{2,1,0:T(8,128)(2,1)S(1)} %copy-done.5, ...), custom_call_target="tpu_custom_call" | custom-call | flops 100000000 | bytes 2000000 | tf_op jit(solution)/shard_map/back_first/pallas_call | solution.py:464
  97.5 15.6 %all_to_all.27.recv_ref = bf16[8,208,128]{2,1,0:T(8,128)(2,1)S(1)} all-to-all(bf16[8,208,128]{2,1,0:T(8,128)(2,1)S(1)} %get-tuple-element.47), channel_id=1, replica_groups=mesh['dap'=8,'dp'=32] {'dap'}, dimensions={0} | all-to-all | bytes 851968 | tf_op jit(solution)/shard_map/all_to_all | solution.py:429
  113.1 4.0 %grad_pair.1 = (bf16[12,96,128]{2,1,0:T(8,128)(2,1)}, bf16[8,192,128]{2,1,0:T(8,128)(2,1)S(1)}) custom-call(bf16[8,208,128]{2,1,0:T(8,128)(2,1)S(1)} %all_to_all.27.recv_ref, bf16[12,96,128]{2,1,0:T(8,128)(2,1)S(1)} %copy-done.1, bf16[12,96,128]{2,1,0:T(8,128)(2,1)S(1)} %get-tuple-element.48.up_ref, f32[12,96,128]{2,1,0:T(8,128)S(1)} %get-tuple-element.49.gn_ref, ...), custom_call_target="tpu_custom_call" | custom-call | flops 100000000 | bytes 2000000 | tf_op jit(solution)/shard_map/grad_pair/pallas_call | solution.py:474
  117.1 15.0 %all_to_all.28.recv_ref = bf16[8,192,128]{2,1,0:T(8,128)(2,1)S(1)} all-to-all(bf16[8,192,128]{2,1,0:T(8,128)(2,1)S(1)} %get-tuple-element.52), channel_id=1, replica_groups=mesh['dap'=8,'dp'=32] {'dap'}, dimensions={0} | all-to-all | bytes 786432 | tf_op jit(solution)/shard_map/all_to_all | solution.py:429
  132.1 0.9 weight_sums.1
  133.0 0.7 copy.23
  (5 shorter events, 0.0 us)
Async XLA Ops:
  0.6 0.9 copy-start.6
  0.6 0.8 copy-start.7
  1.5 1.0 copy-start
  2.5 1.0 copy-start.4
  8.0 7.5 %copy-start.2 = (bf16[2,128,512]{2,1,0:T(8,128)(2,1)S(1)}, bf16[2,128,512]{2,1,0:T(8,128)(2,1)}, u32[]{:S(2)}) copy-start(bf16[2,128,512]{2,1,0:T(8,128)(2,1)} %wp_ref.5) | copy-start | bytes 786436
  8.0 19.2 %all-to-all-start = ((bf16[8,192,128]{2,1,0:T(8,128)(2,1)}), bf16[8,192,128]{2,1,0:T(8,128)(2,1)S(1)}, u32[]{:S(2)}, u32[]{:S(2)}) async-start(bf16[8,192,128]{2,1,0:T(8,128)(2,1)} %get-tuple-element.34), calls=%async_computation | async-start | bytes 786432 | tf_op jit(solution)/shard_map/all_to_all | solution.py:429
  15.5 0.7 copy-start.10
  16.2 11.0 %copy-start.1 = (bf16[12,96,128]{2,1,0:T(8,128)(2,1)S(1)}, bf16[12,96,128]{2,1,0:T(8,128)(2,1)}, u32[]{:S(2)}) copy-start(bf16[12,96,128]{2,1,0:T(8,128)(2,1)} %x_ref.7) | copy-start | bytes 884740
  16.2 11.0 %copy-start.3 = (bf16[2,128,128]{2,1,0:T(8,128)(2,1)S(1)}, bf16[2,128,128]{2,1,0:T(8,128)(2,1)}, u32[]{:S(2)}) copy-start(bf16[2,128,128]{2,1,0:T(8,128)(2,1)} %wo_ref.5) | copy-start | bytes 196612
  27.2 0.7 copy-start.8
  27.2 0.7 copy-start.9
  68.6 15.1 %copy-start.5 = (bf16[12,96,128]{2,1,0:T(8,128)(2,1)S(1)}, bf16[12,96,128]{2,1,0:T(8,128)(2,1)}, u32[]{:S(2)}) copy-start(bf16[12,96,128]{2,1,0:T(8,128)(2,1)} %cot_ref.3) | copy-start | bytes 884740

commit v2 on v1

v2 whole, which is shorter than its diff:
```python
import jax
import jax.numpy as jnp
from jax import lax
from jax.experimental import pallas as pl
from jax.experimental.pallas import tpu as pltpu
from jax.sharding import PartitionSpec as P

HEADS = 4
WIDTH = 32
CH = 128
N = 96
GROUP = 8
ROWS = N // GROUP
CELLS = ROWS * N
BLOCK = ROWS * ROWS
BROWS = HEADS * ROWS
PACK = BLOCK + BROWS
SLICE = CH // GROUP
WROWS = 5 * SLICE
LOW2, LOW3 = 1, 0
EPSILON = 1e-05
SCALING = WIDTH ** (-0.5)
F32 = jnp.float32
BF16 = jnp.bfloat16


def dot_nn(a, b):
    return lax.dot_general(a, b, (((1,), (0,)), ((), ())), preferred_element_type=F32)


def dot_nt(a, b):
    return lax.dot_general(a, b, (((1,), (1,)), ((), ())), preferred_element_type=F32)


def dot_tn(a, b):
    return lax.dot_general(a, b, (((0,), (0,)), ((), ())), preferred_element_type=F32)


def normalise(x):
    center = jnp.mean(x, axis=-1, keepdims=True)
    moved = x - center
    spread = jnp.mean(jnp.square(moved), axis=-1, keepdims=True)
    inverse = lax.rsqrt(spread + EPSILON)
    return moved * inverse, inverse


def norm_back(grad_normed, gain, normed, inverse):
    scaled = grad_normed * gain
    return inverse * (
        scaled
        - jnp.mean(scaled, axis=-1, keepdims=True)
        - normed * jnp.mean(scaled * normed, axis=-1, keepdims=True)
    )


def fold8(x):
    return jnp.sum(x.reshape(x.shape[0] // 8, 8, x.shape[1]), axis=0)


def head_stack(x):
    lane = lax.broadcasted_iota(jnp.int32, x.shape, 1) // WIDTH
    zero = jnp.zeros_like(x)
    return jnp.concatenate([jnp.where(lane == h, x, zero) for h in range(HEADS)], axis=0)


def head_pick(x):
    lane = lax.broadcasted_iota(jnp.int32, (N, CH), 1) // WIDTH
    out = x[0:N]
    for h in range(1, HEADS):
        out = jnp.where(lane == h, x[h * N : (h + 1) * N], out)
    return out


def project(nx, w_proj, gate_bias):
    joint = dot_nn(nx, w_proj)
    q = (joint[:, 0:CH] * SCALING).astype(BF16)
    k = joint[:, CH : 2 * CH].astype(BF16)
    v = joint[:, 2 * CH : 3 * CH].astype(BF16)
    gate = jax.nn.sigmoid(joint[:, 3 * CH :] + gate_bias)
    return q, k, v, gate


def probabilities(q, k, bias_ref):
    scores = dot_nt(head_stack(k), q)
    out = []
    for h in range(HEADS):
        s = scores[h * N : (h + 1) * N] + bias_ref[h]
        e = jnp.exp(s - jnp.max(s, axis=0, keepdims=True))
        out.append(e * (1.0 / jnp.sum(e, axis=0, keepdims=True)))
    return out


def weighted(x, mats):
    x_t = x.T
    parts = [dot_nn(x_t[h * WIDTH : (h + 1) * WIDTH], mats[h]) for h in range(HEADS)]
    return jnp.concatenate(parts, axis=0).T


def key_column(mask_ref):
    row = jnp.where(mask_ref[...] > 0, 0.0, -1000000000.0).astype(F32)
    wide = jnp.broadcast_to(row, (N, N))
    diag = lax.broadcasted_iota(jnp.int32, (N, N), 0) == lax.broadcasted_iota(jnp.int32, (N, N), 1)
    return jnp.sum(jnp.where(diag, wide, 0.0), axis=1, keepdims=True)


def attention_back(probs, q, k, v, grad_att, sum_ref):
    grad_probs = dot_nt(head_stack(v), grad_att)
    probs_b = []
    scores_b = []
    for h in range(HEADS):
        p = probs[h]
        gp = grad_probs[h * N : (h + 1) * N]
        inner = jnp.sum(p * gp, axis=0, keepdims=True)
        ds = p * (gp - inner)
        sum_ref[h] += ds
        probs_b.append(p.astype(BF16))
        scores_b.append(ds.astype(BF16))
    grad_v = head_pick(dot_nn(jnp.concatenate(probs_b, axis=0), grad_att)).astype(BF16)
    grad_k = head_pick(dot_nn(jnp.concatenate(scores_b, axis=0), q)).astype(BF16)
    grad_q = (weighted(k, scores_b) * SCALING).astype(BF16)
    return jnp.concatenate([grad_q, grad_k, grad_v], axis=1)


def gate_back(grad_mixed, gate, part):
    return (grad_mixed * gate).astype(BF16), (grad_mixed * part).astype(BF16)


def bias_rows(nx, w_bias_t):
    return dot_nt(w_bias_t, nx)


def w_bias_rows(w_bias_ref, m):
    rows = w_bias_ref[m].astype(F32)
    return jnp.concatenate([rows, jnp.zeros((8 - HEADS, CH), F32)], axis=0).astype(BF16)


def fetch(pairs, sems):
    copies = [pltpu.make_async_copy(src, dst, sems.at[n]) for n, (src, dst) in enumerate(pairs)]
    for copy in copies:
        copy.start()
    return copies


def k1_body(
    x_hbm, cot_hbm, gain_hbm, shift_hbm, wb_hbm, nx_ref, msg_ref,
    x_ref, cot_ref, gain_ref, shift_ref, wb_ref, bias_s, cot_s, sems,
):
    copies = fetch(
        [(gain_hbm, gain_ref), (shift_hbm, shift_ref), (wb_hbm, wb_ref), (x_hbm, x_ref), (cot_hbm, cot_ref)],
        sems,
    )
    bias_s[...] = jnp.zeros_like(bias_s)
    for copy in copies[0:4]:
        copy.wait()
    gain, shift = gain_ref[0:1], shift_ref[0:1]
    wb = w_bias_rows(wb_ref, 0)
    for i in range(ROWS):
        normed, _inv = normalise(x_ref[i].astype(F32))
        nx = (normed * gain + shift).astype(BF16)
        nx_ref[i * N : (i + 1) * N] = nx
        bias_s[i, :, 0:N] = bias_rows(nx, wb)[0:HEADS]
    copies[4].wait()
    for i in range(ROWS):
        cot_s[pl.ds(i, N, stride=ROWS), :] = cot_ref[i].astype(F32)
    bias = bias_s[...].reshape(BROWS, CH).astype(BF16)
    for e in range(GROUP):
        msg_ref[e, 0:BLOCK] = cot_s[e * BLOCK : (e + 1) * BLOCK].astype(BF16)
        msg_ref[e, BLOCK:PACK] = bias


def k1b_body(nx_ref, wp_ref, gb_ref, q_ref, k_ref, v_ref, gate_ref):
    for i in range(ROWS):
        q, k, v, gate = project(nx_ref[i * N : (i + 1) * N], wp_ref[0], gb_ref[0:1])
        q_ref[i] = q
        k_ref[i] = k
        v_ref[i] = v
        gate_ref[i] = gate


def gather_rows(recv_ref, flat_s, row_s):
    for d in range(GROUP):
        flat_s[d * BLOCK : (d + 1) * BLOCK] = recv_ref[d, 0:BLOCK].astype(F32)
    for i in range(ROWS):
        for d in range(GROUP):
            at = d * BLOCK + i * ROWS
            row_s[i, d * ROWS : (d + 1) * ROWS] = flat_s[at : at + ROWS]


def k2_body(
    x_ref, q_ref, k_ref, v_ref, gate_ref, recv_ref, mask_ref, wo_ref, ob_ref, gain_ref, shift_ref, wb_ref,
    part_ref, mixed_ref, probs_ref, nx_ref, norm_ref, inv_ref, msg_ref,
    raw_s, own_s, first_s, row_ref, bias_ref,
):
    key = key_column(mask_ref)
    for d in range(GROUP):
        raw_s[d * BROWS : (d + 1) * BROWS] = recv_ref[d, BLOCK:PACK].astype(F32)
    for h in range(HEADS):
        bias_ref[h] = raw_s[pl.ds(h, N, stride=HEADS), :].T[0:N] + key
    wb = w_bias_rows(wb_ref, 1)
    w_out = wo_ref[0]
    out_bias = ob_ref[0:1]
    gain, shift = gain_ref[1:2], shift_ref[1:2]
    own_s[...] = jnp.zeros_like(own_s)
    for i in range(ROWS):
        probs = probabilities(q_ref[i], k_ref[i], bias_ref)
        for h in range(HEADS):
            probs_ref[i, h] = probs[h]
        att = weighted(v_ref[i], [p.astype(BF16) for p in probs])
        gate = gate_ref[i]
        gated = gate * att
        part_ref[i] = gated * (1.0 - gate)
        mixed = gated.astype(BF16)
        mixed_ref[i * N : (i + 1) * N] = mixed
        first = x_ref[i].astype(F32) + dot_nn(mixed, w_out) + out_bias
        first = first.astype(BF16)
        row_ref[i] = first
        first_s[pl.ds(i, N, stride=ROWS), :] = first.astype(F32)
    for i in range(ROWS):
        normed, inverse = normalise(row_ref[i].astype(F32))
        nx = (normed * gain + shift).astype(BF16)
        nx_ref[i] = nx
        norm_ref[i] = normed
        inv_ref[i] = jnp.broadcast_to(inverse, (N, CH))
        own_s[i, :, 0:N] = bias_rows(nx, wb)[0:HEADS]
    bias = own_s[...].reshape(BROWS, CH).astype(BF16)
    for e in range(GROUP):
        msg_ref[e, 0:BLOCK] = first_s[e * BLOCK : (e + 1) * BLOCK].astype(BF16)
        msg_ref[e, BLOCK:PACK] = bias


def k2b_body(recv_ref, wo_ref, up_ref, gm_ref, total_ref, flat_s, row_s):
    gather_rows(recv_ref, flat_s, row_s)
    total = jnp.zeros((8, CH), F32)
    for i in range(ROWS):
        up_f = row_s[i]
        total += fold8(up_f)
        up = up_f.astype(BF16)
        up_ref[i * N : (i + 1) * N] = up
        gm_ref[i] = dot_nt(up, wo_ref[1])
    total_ref[...] = total


def weight_grads(nx_ref, joint_ref, mixed_ref, up_ref, put):
    nx = nx_ref[...]
    for block in range(4):
        put(block, dot_tn(nx, joint_ref[:, block * CH : (block + 1) * CH]))
    put(4, dot_tn(mixed_ref[...], up_ref[...]))


def split2(x):
    top = x.astype(BF16)
    return top, (x - top.astype(F32)).astype(BF16)


def put_sums(msg_ref, e, start, rows, low):
    parts = split2(rows) if low else [rows.astype(BF16)]
    for n, part in enumerate(parts):
        at = start + n * BROWS
        msg_ref[e, at : at + BROWS, 0:N] = part
        msg_ref[e, at : at + BROWS, N:CH] = jnp.zeros((BROWS, CH - N), BF16)


def k3_body(
    recv_ref, mask_ref, gm_ref, gain_ref, shift_ref, wp_ref, gb_ref,
    msg_ref, small_ref, nx_ref, joint_ref, mixed_ref,
    flat_s, x_s, raw_s, bias_s, sum_s, norm_s, inv_s, q_s, k_s, v_s, gate_s, att_s, probs_s, grad_s,
):
    key = key_column(mask_ref)
    for d in range(GROUP):
        raw_s[d * BROWS : (d + 1) * BROWS] = recv_ref[d, BLOCK:PACK].astype(F32)
    for h in range(HEADS):
        bias_s[h] = raw_s[pl.ds(h, N, stride=HEADS), :][:, 0:N] + key
    gather_rows(recv_ref, flat_s, x_s)
    sum_s[...] = jnp.zeros_like(sum_s)
    gain, shift = gain_ref[1:2], shift_ref[1:2]
    gate_bias = gb_ref[1:2]
    for i in range(ROWS):
        normed, inverse = normalise(x_s[i])
        nx_ref[i * N : (i + 1) * N] = (normed * gain + shift).astype(BF16)
        norm_s[i] = normed
        inv_s[i] = jnp.broadcast_to(inverse, (N, CH))
    for i in range(ROWS):
        q_s[i], k_s[i], v_s[i], gate_s[i] = project(nx_ref[i * N : (i + 1) * N], wp_ref[1], gate_bias)
    for i in range(ROWS):
        probs = probabilities(q_s[i], k_s[i], bias_s)
        for h in range(HEADS):
            probs_s[i, h] = probs[h]
        att_s[i] = weighted(v_s[i], [p.astype(BF16) for p in probs])
    logit_sum = jnp.zeros((8, CH), F32)
    for i in range(ROWS):
        gate, att = gate_s[i], att_s[i]
        mixed_ref[i * N : (i + 1) * N] = (gate * att).astype(BF16)
        grad_s[i], grad_logit = gate_back(gm_ref[i], gate, att * gate * (1.0 - gate))
        joint_ref[i * N : (i + 1) * N, 3 * CH :] = grad_logit
        logit_sum += fold8(grad_logit.astype(F32))
    for i in range(ROWS):
        probs = [probs_s[i, h] for h in range(HEADS)]
        joint_ref[i * N : (i + 1) * N, 0 : 3 * CH] = attention_back(
            probs, q_s[i], k_s[i], v_s[i], grad_s[i], sum_s
        )
    gain_sum = jnp.zeros((8, CH), F32)
    shift_sum = jnp.zeros((8, CH), F32)
    for i in range(ROWS):
        grad_normed = dot_nt(joint_ref[i * N : (i + 1) * N], wp_ref[1])
        normed = norm_s[i]
        flat_s[pl.ds(i, N, stride=ROWS), :] = norm_back(grad_normed, gain, normed, inv_s[i])
        gain_sum += fold8(grad_normed * normed)
        shift_sum += fold8(grad_normed)
    small_ref[0:8] = gain_sum
    small_ref[8:16] = shift_sum
    small_ref[16:24] = logit_sum
    for e in range(GROUP):
        msg_ref[e, 0:BLOCK] = flat_s[e * BLOCK : (e + 1) * BLOCK].astype(BF16)
        rows = [sum_s[h, e * ROWS : (e + 1) * ROWS] for h in range(HEADS)]
        put_sums(msg_ref, e, BLOCK, jnp.concatenate(rows, axis=0), LOW2)


def k3w_body(nx_ref, joint_ref, mixed_ref, up_ref, out_ref):
    def put(block, part):
        part = part.astype(BF16)
        for e in range(GROUP):
            out_ref[e, block * SLICE : (block + 1) * SLICE] = part[e * SLICE : (e + 1) * SLICE]

    weight_grads(nx_ref, joint_ref, mixed_ref, up_ref, put)


def bias_sum(recv_ref, start, gb_s, low):
    total = recv_ref[0, start : start + BROWS].astype(F32)
    for d in range(1, GROUP):
        total += recv_ref[d, start : start + BROWS].astype(F32)
    if low:
        for d in range(GROUP):
            total += recv_ref[d, start + BROWS : start + 2 * BROWS].astype(F32)
    gb_s[...] = jnp.zeros_like(gb_s)
    total = total.astype(BF16).astype(F32)
    for r in range(ROWS):
        for h in range(HEADS):
            gb_s[r * 8 + h : r * 8 + h + 1] = total[h * ROWS + r : h * ROWS + r + 1]
    return gb_s[...].T[0:N].astype(BF16)


def bias_part(i, gb_s, gb_t, wb_tiled, nx):
    rows = lax.broadcasted_iota(jnp.int32, (ROWS * 8, CH), 0) // 8
    picked = jnp.where(rows == i, wb_tiled, jnp.zeros_like(wb_tiled))
    grad_w = dot_nn(gb_s[i * 8 : (i + 1) * 8, 0:N].astype(BF16), nx)
    return dot_nn(gb_t, picked), grad_w


def k4_body(
    recv_ref, cot_ref, q_ref, k_ref, v_ref, gate_ref, part_ref, probs_ref, mixed_ref, nx_ref,
    nx1_ref, norm1_ref, inv1_ref, gain_ref, wp_ref, wb_ref, wo_ref, wg1_ref,
    up_ref, gn_ref, msg_ref, small_ref,
    flat_s, la_s, gb_s, sum_s, joint_s, grad_s, upb_s,
):
    gather_rows(recv_ref, flat_s, la_s)
    gb_t = bias_sum(recv_ref, BLOCK, gb_s, LOW2)
    wb = w_bias_rows(wb_ref, 1)
    wb_tiled = jnp.concatenate([wb.astype(F32)] * ROWS, axis=0).astype(BF16)
    sum_s[...] = jnp.zeros_like(sum_s)
    gain1 = gain_ref[1:2]
    zero = jnp.zeros((8, CH), F32)
    gain_sum, shift_sum, bias_w, logit_sum, up_sum = zero, zero, zero, zero, zero
    for i in range(ROWS):
        from_bias, grad_w = bias_part(i, gb_s, gb_t, wb_tiled, nx1_ref[i])
        normed = norm1_ref[i]
        gain_sum += fold8(from_bias * normed)
        shift_sum += fold8(from_bias)
        bias_w += grad_w
        up_f = cot_ref[i].astype(F32) + la_s[i] + norm_back(from_bias, gain1, normed, inv1_ref[i])
        up = up_f.astype(BF16)
        up_ref[i] = up
        upb_s[i * N : (i + 1) * N] = up
        up_sum += fold8(up.astype(F32))
    for i in range(ROWS):
        grad_mixed = dot_nt(up_ref[i], wo_ref[0])
        grad_s[i], grad_logit = gate_back(grad_mixed, gate_ref[i], part_ref[i])
        joint_s[i * N : (i + 1) * N, 3 * CH :] = grad_logit
        logit_sum += fold8(grad_logit.astype(F32))
    for i in range(ROWS):
        probs = [probs_ref[i, h] for h in range(HEADS)]
        joint_s[i * N : (i + 1) * N, 0 : 3 * CH] = attention_back(
            probs, q_ref[i], k_ref[i], v_ref[i], grad_s[i], sum_s
        )
    for i in range(ROWS):
        gn_ref[i] = dot_nt(joint_s[i * N : (i + 1) * N], wp_ref[0])
    small_ref[0:8] = gain_sum
    small_ref[8:16] = shift_sum
    small_ref[16:24] = bias_w
    small_ref[24:32] = logit_sum
    small_ref[32:40] = up_sum
    for h in range(HEADS):
        flat_s[h * N : (h + 1) * N, 0:N] = sum_s[h].T
    for e in range(GROUP):
        rows = [flat_s[h * N + e * ROWS : h * N + (e + 1) * ROWS, 0:N] for h in range(HEADS)]
        put_sums(msg_ref, e, 2 * WROWS, jnp.concatenate(rows, axis=0), LOW3)
        msg_ref[e, WROWS : 2 * WROWS] = wg1_ref[e]

    def put(block, part):
        part = part.astype(BF16)
        for e in range(GROUP):
            msg_ref[e, block * SLICE : (block + 1) * SLICE] = part[e * SLICE : (e + 1) * SLICE]

    weight_grads(nx_ref, joint_s, mixed_ref, upb_s, put)


def k4x_body(x_ref, norm_ref, inv_ref):
    for i in range(ROWS):
        normed, inverse = normalise(x_ref[i].astype(F32))
        norm_ref[i] = normed
        inv_ref[i] = jnp.broadcast_to(inverse, (N, CH))


def k5_body(
    recv_ref, norm_ref, gn_ref, nx_ref, small1_ref, total1_ref, small_ref, wb_ref,
    full_ref, msg_ref, gb_s,
):
    gb_t = bias_sum(recv_ref, 2 * WROWS, gb_s, LOW3)
    wb = w_bias_rows(wb_ref, 0)
    wb_tiled = jnp.concatenate([wb.astype(F32)] * ROWS, axis=0).astype(BF16)
    zero = jnp.zeros((8, CH), F32)
    gain_sum, shift_sum, bias_w = zero, zero, zero
    for i in range(ROWS):
        from_bias, grad_w = bias_part(i, gb_s, gb_t, wb_tiled, nx_ref[i * N : (i + 1) * N])
        grad_normed = gn_ref[i] + from_bias
        full_ref[i] = grad_normed
        gain_sum += fold8(grad_normed * norm_ref[i])
        shift_sum += fold8(grad_normed)
        bias_w += grad_w
    total = recv_ref[0, 0 : 2 * WROWS].astype(F32)
    for d in range(1, GROUP):
        total += recv_ref[d, 0 : 2 * WROWS].astype(F32)
    total *= 1.0 / N
    total = total.astype(BF16)

    def one(x):
        return jnp.sum(x, axis=0, keepdims=True)

    rows = [
        one(gain_sum), one(shift_sum), one(small_ref[24:32]), one(small_ref[32:40]), bias_w[0:HEADS],
        one(small1_ref[0:8] + small_ref[0:8]), one(small1_ref[8:16] + small_ref[8:16]),
        one(small1_ref[16:24]), one(total1_ref[...]), small_ref[16 : 16 + HEADS],
    ]
    top, low = split2(jnp.concatenate(rows, axis=0))
    for e in range(GROUP):
        msg_ref[e, 0 : 2 * WROWS] = total
        msg_ref[e, 2 * WROWS : 2 * WROWS + 16] = top
        msg_ref[e, 2 * WROWS + 16 : 2 * WROWS + 32] = low


def k5b_body(full_ref, norm_ref, inv_ref, up_ref, gain_ref, out_ref):
    gain = gain_ref[0:1]
    for i in range(ROWS):
        back = norm_back(full_ref[i], gain, norm_ref[i], inv_ref[i])
        out_ref[i] = (up_ref[i].astype(F32) + back).astype(BF16)


def k6_body(recv_ref, gain_ref, shift_ref, proj_ref, wb_ref, gate_ref, ow_ref, ob_ref):
    small = jnp.zeros((16, CH), F32)
    for d in range(GROUP):
        for m in range(2):
            for block in range(4):
                at = m * WROWS + block * SLICE
                proj_ref[m, d * SLICE : (d + 1) * SLICE, block * CH : (block + 1) * CH] = recv_ref[
                    d, at : at + SLICE
                ].astype(F32)
            at = m * WROWS + 4 * SLICE
            ow_ref[m, d * SLICE : (d + 1) * SLICE] = recv_ref[d, at : at + SLICE].astype(F32)
        at = 2 * WROWS
        small += recv_ref[d, at : at + 16].astype(F32) + recv_ref[d, at + 16 : at + 32].astype(F32)
    small = small * (1.0 / N)
    for m in range(2):
        at = m * 8
        gain_ref[m : m + 1] = small[at : at + 1]
        shift_ref[m : m + 1] = small[at + 1 : at + 2]
        gate_ref[m : m + 1] = small[at + 2 : at + 3]
        ob_ref[m : m + 1] = small[at + 3 : at + 4]
        wb_ref[m] = small[at + 4 : at + 8]


def call(body, outs, scratch, name, far=(), far_out=(), copies=0, flops=100000000, big=False):
    near_spec = pl.BlockSpec(memory_space=pltpu.VMEM)
    far_spec = pl.BlockSpec(memory_space=pltpu.HBM)
    scratch = [pltpu.VMEM(shape, dtype) for shape, dtype in scratch]
    if copies:
        scratch.append(pltpu.SemaphoreType.DMA((copies,)) if copies > 1 else pltpu.SemaphoreType.DMA)

    def run(*args):
        return pl.pallas_call(
            body,
            in_specs=[far_spec if n in far else near_spec for n in range(len(args))],
            out_specs=[far_spec if n in far_out else near_spec for n in range(len(outs))],
            out_shape=[jax.ShapeDtypeStruct(shape, dtype) for shape, dtype in outs],
            scratch_shapes=scratch,
            compiler_params=pltpu.CompilerParams(vmem_limit_bytes=(62 if big else 24) * 1024 * 1024),
            cost_estimate=pl.CostEstimate(flops=flops, bytes_accessed=2000000, transcendentals=500000),
            name=name,
        )(*args)

    return run


def after(x, y):
    return lax.optimization_barrier((x, y))[0]


def swap(x):
    return lax.all_to_all(x, "dap", 0, 0, tiled=True)


def per_device(
    pair_rep, cotangent, residue_mask, ln_gain, ln_shift, w_proj, w_bias, gate_bias, w_out, out_bias
):
    mask = residue_mask.reshape(1, N)
    w_bias = jnp.swapaxes(w_bias, 1, 2)
    rows_b = ((ROWS, N, CH), BF16)
    rows_f = ((ROWS, N, CH), F32)
    flat_f = ((CELLS, CH), F32)
    flat_b = ((CELLS, CH), BF16)
    joint_b = ((CELLS, 4 * CH), BF16)
    pack = ((GROUP, PACK, CH), BF16)
    mats = ((HEADS, N, N), F32)
    probs = ((ROWS, HEADS, N, N), F32)
    raw = ((GROUP * BROWS, CH), F32)
    own_bias = ((ROWS, HEADS, CH), F32)
    bias_8 = ((ROWS * 8, CH), F32)

    vec_f = ((2, CH), F32)

    nx0, msg0 = call(
        k1_body,
        [flat_b, pack],
        [rows_b, rows_b, vec_f, vec_f, ((2, HEADS, CH), BF16), own_bias, flat_f],
        "norm_first",
        far=range(5),
        copies=5,
        big=True,
    )(pair_rep, cotangent, ln_gain, ln_shift, w_bias)
    recv0 = swap(msg0)
    q, k, v, gate = call(k1b_body, [rows_b, rows_b, rows_b, rows_f], [], "project_first")(
        nx0, w_proj, gate_bias
    )
    part0, mixed0, probs0, nx1, norm1, inv1, msg1 = call(
        k2_body,
        [rows_f, flat_b, probs, rows_b, rows_f, rows_f, pack],
        [raw, own_bias, flat_f, rows_b, mats],
        "attend_first",
    )(pair_rep, q, k, v, gate, recv0, mask, w_out, out_bias, ln_gain, ln_shift, w_bias)
    recv1 = swap(msg1)
    up1, gm1, total1 = call(
        k2b_body, [flat_b, rows_f, ((8, CH), F32)], [flat_f, rows_f], "cotangent_rows"
    )(after(recv0, recv1), w_out)
    msg2, small1, nxw, joint1, mixed1 = call(
        k3_body,
        [((GROUP, BLOCK + (1 + LOW2) * BROWS, CH), BF16), ((24, CH), F32), flat_b, joint_b, flat_b],
        [flat_f, rows_f, raw, mats, mats, rows_f, rows_f]
        + [rows_b, rows_b, rows_b, rows_f, rows_f, probs, rows_b],
        "second_module",
    )(recv1, mask, gm1, ln_gain, ln_shift, w_proj, gate_bias)
    recv2 = swap(msg2)
    (wg1,) = call(k3w_body, [((GROUP, WROWS, CH), BF16)], [], "second_weights")(
        after(nxw, recv2), joint1, mixed1, up1
    )
    up, gn, msg3, small = call(
        k4_body,
        [rows_b, rows_f, ((GROUP, 2 * WROWS + (1 + LOW3) * BROWS, CH), BF16), ((40, CH), F32)],
        [flat_f, rows_f, bias_8, mats, joint_b, rows_b, flat_b],
        "back_first",
    )(
        recv2, cotangent, q, k, v, gate, part0, probs0, mixed0, nx0, nx1, norm1, inv1,
        ln_gain, w_proj, w_bias, w_out, wg1,
    )
    recv3 = swap(msg3)
    norm0, inv0 = call(k4x_body, [rows_f, rows_f], [], "norm_again")(after(pair_rep, recv3))
    full, msg4 = call(
        k5_body, [rows_f, ((GROUP, 2 * WROWS + 32, CH), BF16)], [bias_8], "grad_sums"
    )(recv3, norm0, gn, nx0, small1, total1, small, w_bias)
    recv4 = swap(msg4)
    (grad_pair,) = call(k5b_body, [rows_b], [], "grad_pair")(after(full, recv4), norm0, inv0, up, ln_gain)
    grad_gain, grad_shift, grad_proj, grad_bias_w, grad_gate, grad_out_w, grad_out_bias = call(
        k6_body,
        [
            ((2, CH), F32), ((2, CH), F32), ((2, CH, 4 * CH), F32), ((2, HEADS, CH), F32),
            ((2, CH), F32), ((2, CH, CH), F32), ((2, CH), F32),
        ],
        [],
        "weight_sums",
    )(recv4)
    return (
        grad_pair, grad_gain, grad_shift, grad_proj, jnp.swapaxes(grad_bias_w, 1, 2), grad_gate,
        grad_out_w, grad_out_bias,
    )


def solution(mesh):
    in_specs = (
        P(("dp", "dap"), None, None),
        P(("dp", "dap"), None, None),
        P("dp"),
        P(),
        P(),
        P(),
        P(),
        P(),
        P(),
        P(),
    )
    out_specs = (
        P(("dp", "dap"), None, None),
        P("dp", None),
        P("dp", None),
        P("dp", None, None),
        P("dp", None, None),
        P("dp", None),
        P("dp", None, None),
        P("dp", None),
    )
    return jax.shard_map(
        per_device, mesh=mesh, in_specs=in_specs, out_specs=out_specs, check_vma=False
    )
```

time: 134 us -> 103 us (0.77)
  Pallas kernels: 51.1 us -> 20.6 us
  local copies, waits for them, and re-layouts: 4.81 us -> 2.64 us
  blocking collectives: 60.6 us -> 62.6 us
    pallas_call x7 -> x11, Pallas kernels: 51.1 us -> 20.6 us  [run(): pl.pallas_call(body, in_specs=[far_spec if n in far else near_spec for n...]
    unnamed x24 -> x28, local copies, waits for them, and re-layouts: 4.81 us -> 2.64 us
    all_to_all x4, blocking collectives: 60.6 us -> 62.6 us  [swap(): return lax.all_to_all(x, 'dap', 0, 0, tiled=True)]
  transfers between devices with their start and end apart: 1 -> 1, of which waited for: 1 -> 1; matrix products, arithmetic and copies ran while one was open for 0% -> 0% of each run, Pallas kernels for 2% -> 0%
where the time goes in v2:
time: 103 us
  blocking collectives  62.6 us (61%)
  Pallas kernels  20.6 us (20%)
  waiting for transfers between devices  8.61 us (8%)
  starting transfers between devices  7.41 us (7%)
  local copies, waits for them, and re-layouts  2.64 us (3%)
    all_to_all x4, blocking collectives, swap(): return lax.all_to_all(x, 'dap', 0, 0, tiled=True)  62.6 us
    pallas_call x11, Pallas kernels, run(): pl.pallas_call(body, in_specs=[far_spec if n in far else near_spec for n...  20.6 us
    all_to_all x1, waiting for transfers between devices, swap(): return lax.all_to_all(x, 'dap', 0, 0, tiled=True)  8.61 us
    all_to_all x1, starting transfers between devices, swap(): return lax.all_to_all(x, 'dap', 0, 0, tiled=True)  7.41 us
    unnamed x28, local copies, waits for them, and re-layouts  2.64 us
  transfers between devices with their start and end apart: 1, of which 1 were waited for; matrix products, arithmetic and copies ran while one was open for 0% of the time, Pallas kernels for 0%

profile of v2, /device:TPU:1, one launch (start us, length us, event | category | flops | bytes accessed | tf_op | source)
XLA Modules:
  0.0 102.7 jit_solution(10025985191481186609)
XLA Ops:
  0.6 0.0 copy-start.8
  0.6 0.0 copy-start.9
  0.7 0.0 copy-start.5
  0.7 0.0 copy-start.7
  0.7 0.0 copy-start.6
  0.7 0.0 copy-start.11
  0.7 2.5 %norm_first.1 = (bf16[1152,128]{1,0:T(8,128)(2,1)}, bf16[8,192,128]{2,1,0:T(8,128)(2,1)}) custom-call(bf16[12,96,128]{2,1,0:T(8,128)(2,1)} %x_ref.2, bf16[12,96,128]{2,1,0:T(8,128)(2,1)} %cot_ref.1, f32[2,128]{1,0:T(2,128)} %gain_ref.7, f32[2,128]{1,0:T(2,128)} %shift_ref.3, bf16[2,4,128]{2,1,0:T(4,128)(2,1)} %bitcast.3), custom_call_target="tpu_custom_call" | custom-call | flops 100000000 | bytes 2000000 | tf_op jit(solution)/shard_map/norm_first/pallas_call | solution.py:488
  3.2 7.4 %all-to-all-start = ((bf16[8,192,128]{2,1,0:T(8,128)(2,1)}), bf16[8,192,128]{2,1,0:T(8,128)(2,1)S(1)}, u32[]{:S(2)}, u32[]{:S(2)}) async-start(bf16[8,192,128]{2,1,0:T(8,128)(2,1)} %get-tuple-element.53), calls=%async_computation | async-start | bytes 786432 | tf_op jit(solution)/shard_map/all_to_all | solution.py:507
  10.6 1.0 copy-done
  11.6 0.9 copy-done.2
  12.5 0.7 copy-done.12
  13.2 0.5 project_first.1
  13.7 8.6 %all-to-all-done.recv_ref = bf16[8,192,128]{2,1,0:T(8,128)(2,1)S(1)} async-done(((bf16[8,192,128]{2,1,0:T(8,128)(2,1)}), bf16[8,192,128]{2,1,0:T(8,128)(2,1)S(1)}, u32[]{:S(2)}, u32[]{:S(2)}) %all-to-all-start) | async-done | bytes 393248 | tf_op jit(solution)/shard_map/all_to_all | solution.py:507
  22.3 0.0 copy-done.5
  22.3 0.0 copy-done.7
  22.3 0.0 copy-done.6
  22.3 0.0 copy-done.11
  22.4 0.0 copy-done.10
  22.4 3.7 %attend_first.1 = (f32[12,96,128]{2,1,0:T(8,128)S(1)}, bf16[1152,128]{1,0:T(8,128)(2,1)S(1)}, f32[12,4,96,96]{3,2,1,0:T(8,128)S(1)}, bf16[12,96,128]{2,1,0:T(8,1...) custom-call(bf16[12,96,128]{2,1,0:T(8,128)(2,1)S(1)} %copy-done.5, ...), custom_call_target="tpu_custom_call" | custom-call | flops 100000000 | bytes 2000000 | tf_op jit(solution)/shard_map/attend_first/pallas_call | solution.py:488
  26.0 14.9 %all_to_all.25.recv_ref = bf16[8,192,128]{2,1,0:T(8,128)(2,1)S(1)} all-to-all(bf16[8,192,128]{2,1,0:T(8,128)(2,1)S(1)} %get-tuple-element.54), channel_id=1, replica_groups=mesh['dap'=8,'dp'=32] {'dap'}, dimensions={0} | all-to-all | bytes 786432 | tf_op jit(solution)/shard_map/all_to_all | solution.py:507
  41.0 0.4 cotangent_rows.1
  41.4 0.0 copy-start.4
  41.4 5.4 %second_module.1 = (bf16[8,240,128]{2,1,0:T(8,128)(2,1)S(1)}, f32[24,128]{1,0:T(8,128)S(1)}, bf16[1152,128]{1,0:T(8,128)(2,1)S(1)}, bf16[1152,512]{1,0:T(8,128)(2,1)S(1)}, bf16[1152,128]{1,0:T(8,128)(2,1)S(1)}) custom-call(bf16[8,192,128]{2,1,0:T(8,128)(2,1)S(1)} %all_to_all.25.recv_ref, s32[1,96]{1,0:T(1,128)S(1)} %bitcast.8, ...), custom_call_target="tpu_custom_call" | custom-call | flops 100000000 | bytes 2000000 | tf_op jit(solution)/shard_map/second_module/pallas_call | solution.py:488
  46.8 16.9 %all_to_all.26.recv_ref = bf16[8,240,128]{2,1,0:T(8,128)(2,1)S(1)} all-to-all(bf16[8,240,128]{2,1,0:T(8,128)(2,1)S(1)} %get-tuple-element.57), channel_id=1, replica_groups=mesh['dap'=8,'dp'=32] {'dap'}, dimensions={0} | all-to-all | bytes 983040 | tf_op jit(solution)/shard_map/all_to_all | solution.py:507
  63.7 0.6 second_weights.1.wg1_ref
  64.3 4.4 %back_first.1 = (bf16[12,96,128]{2,1,0:T(8,128)(2,1)S(1)}, f32[12,96,128]{2,1,0:T(8,128)S(1)}, bf16[8,208,128]{2,1,0:T(8,128)(2,1)S(1)}, f32[40,128]{1,0:T(8,128)S(1)}) custom-call(bf16[8,240,128]{2,1,0:T(8,128)(2,1)S(1)} %all_to_all.26.recv_ref, bf16[12,96,128]{2,1,0:T(8,128)(2,1)S(1)} %copy-done.4, bf16[12,96,128]{2,1,0:T(8,128)(2,1)S(1)} %get-tuple-element.49.q_ref, ...), custom_call_target="tpu_custom_call" | custom-call | flops 100000000 | bytes 2000000 | tf_op jit(solution)/shard_map/back_first/pallas_call | solution.py:488
  68.7 15.7 %all_to_all.27.recv_ref = bf16[8,208,128]{2,1,0:T(8,128)(2,1)S(1)} all-to-all(bf16[8,208,128]{2,1,0:T(8,128)(2,1)S(1)} %get-tuple-element.69), channel_id=1, replica_groups=mesh['dap'=8,'dp'=32] {'dap'}, dimensions={0} | all-to-all | bytes 851968 | tf_op jit(solution)/shard_map/all_to_all | solution.py:507
  84.5 0.8 norm_again.1
  85.3 0.4 grad_sums.1
  85.7 15.0 %all_to_all.28.recv_ref = bf16[8,192,128]{2,1,0:T(8,128)(2,1)S(1)} all-to-all(bf16[8,192,128]{2,1,0:T(8,128)(2,1)S(1)} %get-tuple-element.77), channel_id=1, replica_groups=mesh['dap'=8,'dp'=32] {'dap'}, dimensions={0} | all-to-all | bytes 786432 | tf_op jit(solution)/shard_map/all_to_all | solution.py:507
  100.7 1.1 %grad_pair.1 = bf16[12,96,128]{2,1,0:T(8,128)(2,1)} custom-call(f32[12,96,128]{2,1,0:T(8,128)S(1)} %get-tuple-element.78.full_ref, f32[12,96,128]{2,1,0:T(8,128)S(1)} %get-tuple-element.71.norm_ref, f32[12,96,128]{2,1,0:T(8,128)S(1)} %get-tuple-element.79.inv_ref, bf16[12,96,128]{2,1,0:T(8,128)(2,1)S(1)} %get-tuple-element.80.up_ref, f32[2,128]{1,0:T(2,128)S(1)} %copy-done.8), custom_call_target="tpu_custom_call" | custom-call | flops 100000000 | bytes 2000000 | tf_op jit(solution)/shard_map/grad_pair/pallas_call | solution.py:488
  101.8 0.9 weight_sums.1
  (13 shorter events, 0.0 us)
Async XLA Ops:
  0.6 21.7 %copy-start.8 = (f32[2,128]{1,0:T(2,128)S(1)}, f32[2,128]{1,0:T(2,128)}, u32[]{:S(2)}) copy-start(f32[2,128]{1,0:T(2,128)} %gain_ref.7) | copy-start | bytes 3076
  0.6 21.7 %copy-start.9 = (f32[2,128]{1,0:T(2,128)S(1)}, f32[2,128]{1,0:T(2,128)}, u32[]{:S(2)}) copy-start(f32[2,128]{1,0:T(2,128)} %shift_ref.3) | copy-start | bytes 3076
  0.7 21.7 %copy-start.5 = (bf16[12,96,128]{2,1,0:T(8,128)(2,1)S(1)}, bf16[12,96,128]{2,1,0:T(8,128)(2,1)}, u32[]{:S(2)}) copy-start(bf16[12,96,128]{2,1,0:T(8,128)(2,1)} %x_ref.2) | copy-start | bytes 884740
  0.7 21.7 %copy-start.7 = (bf16[2,128,4]{1,2,0:T(4,128)(2,1)S(1)}, bf16[2,128,4]{1,2,0:T(4,128)(2,1)}, u32[]{:S(2)}) copy-start(bf16[2,128,4]{1,2,0:T(4,128)(2,1)} %param.16) | copy-start | bytes 6148
  0.7 21.7 %copy-start.6 = (bf16[2,128,128]{2,1,0:T(8,128)(2,1)S(1)}, bf16[2,128,128]{2,1,0:T(8,128)(2,1)}, u32[]{:S(2)}) copy-start(bf16[2,128,128]{2,1,0:T(8,128)(2,1)} %wo_ref.5) | copy-start | bytes 196612
  0.7 21.7 %copy-start.11 = (f32[2,128]{1,0:T(2,128)S(1)}, f32[2,128]{1,0:T(2,128)}, u32[]{:S(2)}) copy-start(f32[2,128]{1,0:T(2,128)} %ob_ref.1) | copy-start | bytes 3076
  0.7 21.7 %copy-start.10 = (s32[96]{0:T(128)S(1)}, s32[96]{0:T(128)}, u32[]{:S(2)}) copy-start(s32[96]{0:T(128)} %param.12) | copy-start | bytes 1156
  3.2 19.1 %all-to-all-start = ((bf16[8,192,128]{2,1,0:T(8,128)(2,1)}), bf16[8,192,128]{2,1,0:T(8,128)(2,1)S(1)}, u32[]{:S(2)}, u32[]{:S(2)}) async-start(bf16[8,192,128]{2,1,0:T(8,128)(2,1)} %get-tuple-element.53), calls=%async_computation | async-start | bytes 786432 | tf_op jit(solution)/shard_map/all_to_all | solution.py:507
  10.6 1.0 copy-start
  11.6 0.9 copy-start.2
  12.5 0.7 copy-start.12
  13.2 28.2 %copy-start.3 = (bf16[2,128,512]{2,1,0:T(8,128)(2,1)S(1)}, bf16[2,128,512]{2,1,0:T(8,128)(2,1)}, u32[]{:S(2)}) copy-start(bf16[2,128,512]{2,1,0:T(8,128)(2,1)} %wp_ref.5) | copy-start | bytes 786436
  13.2 28.2 %copy-start.13 = (f32[2,128]{1,0:T(2,128)S(1)}, f32[2,128]{1,0:T(2,128)}, u32[]{:S(2)}) copy-start(f32[2,128]{1,0:T(2,128)} %gb_ref.3) | copy-start | bytes 3076
  41.4 22.9 %copy-start.1 = (bf16[1152,128]{1,0:T(8,128)(2,1)S(1)}, bf16[1152,128]{1,0:T(8,128)(2,1)}, u32[]{:S(2)}) copy-start(bf16[1152,128]{1,0:T(8,128)(2,1)} %get-tuple-element.48.nx_ref) | copy-start | bytes 884740
  41.4 22.9 %copy-start.4 = (bf16[12,96,128]{2,1,0:T(8,128)(2,1)S(1)}, bf16[12,96,128]{2,1,0:T(8,128)(2,1)}, u32[]{:S(2)}) copy-start(bf16[12,96,128]{2,1,0:T(8,128)(2,1)} %cot_ref.1) | copy-start | bytes 884740

commit v3 on v2

--- a/solution.py
+++ b/solution.py
@@ -103,22 +103,29 @@
     return jnp.sum(jnp.where(diag, wide, 0.0), axis=1, keepdims=True)
 
 
-def attention_back(probs, q, k, v, grad_att, sum_ref):
-    grad_probs = dot_nt(head_stack(v), grad_att)
-    probs_b = []
-    scores_b = []
+def scores_back(i, probs_ref, v_ref, grad_ref, sum_ref, scores_ref):
+    grad_probs = dot_nt(head_stack(v_ref[i]), grad_ref[i])
     for h in range(HEADS):
-        p = probs[h]
+        p = probs_ref[i, h]
         gp = grad_probs[h * N : (h + 1) * N]
         inner = jnp.sum(p * gp, axis=0, keepdims=True)
         ds = p * (gp - inner)
         sum_ref[h] += ds
-        probs_b.append(p.astype(BF16))
-        scores_b.append(ds.astype(BF16))
-    grad_v = head_pick(dot_nn(jnp.concatenate(probs_b, axis=0), grad_att)).astype(BF16)
-    grad_k = head_pick(dot_nn(jnp.concatenate(scores_b, axis=0), q)).astype(BF16)
-    grad_q = (weighted(k, scores_b) * SCALING).astype(BF16)
-    return jnp.concatenate([grad_q, grad_k, grad_v], axis=1)
+        scores_ref[i, h] = ds.astype(BF16)
+
+
+def joint_back(probs_ref, scores_ref, q_ref, k_ref, grad_ref, joint_ref):
+    for i in range(ROWS):
+        stack = jnp.concatenate([probs_ref[i, h].astype(BF16) for h in range(HEADS)], axis=0)
+        grad_v = head_pick(dot_nn(stack, grad_ref[i]))
+        joint_ref[i * N : (i + 1) * N, 2 * CH : 3 * CH] = grad_v.astype(BF16)
+    for i in range(ROWS):
+        stack = jnp.concatenate([scores_ref[i, h] for h in range(HEADS)], axis=0)
+        grad_k = head_pick(dot_nn(stack, q_ref[i]))
+        joint_ref[i * N : (i + 1) * N, CH : 2 * CH] = grad_k.astype(BF16)
+    for i in range(ROWS):
+        grad_q = weighted(k_ref[i], [scores_ref[i, h] for h in range(HEADS)]) * SCALING
+        joint_ref[i * N : (i + 1) * N, 0:CH] = grad_q.astype(BF16)
 
 
 def gate_back(grad_mixed, gate, part):
@@ -142,7 +149,7 @@
 
 
 def k1_body(
-    x_hbm, cot_hbm, gain_hbm, shift_hbm, wb_hbm, nx_ref, msg_ref,
+    x_hbm, cot_hbm, gain_hbm, shift_hbm, wb_hbm, msg_ref,
     x_ref, cot_ref, gain_ref, shift_ref, wb_ref, bias_s, cot_s, sems,
 ):
     copies = fetch(
@@ -157,7 +164,6 @@
     for i in range(ROWS):
         normed, _inv = normalise(x_ref[i].astype(F32))
         nx = (normed * gain + shift).astype(BF16)
-        nx_ref[i * N : (i + 1) * N] = nx
         bias_s[i, :, 0:N] = bias_rows(nx, wb)[0:HEADS]
     copies[4].wait()
     for i in range(ROWS):
@@ -168,7 +174,15 @@
         msg_ref[e, BLOCK:PACK] = bias
 
 
-def k1b_body(nx_ref, wp_ref, gb_ref, q_ref, k_ref, v_ref, gate_ref):
+def k1b_body(
+    x_ref, gain_ref, shift_ref, wp_ref, gb_ref, q_ref, k_ref, v_ref, gate_ref, nx_ref, norm_ref, inv_ref
+):
+    gain, shift = gain_ref[0:1], shift_ref[0:1]
+    for i in range(ROWS):
+        normed, inverse = normalise(x_ref[i].astype(F32))
+        nx_ref[i * N : (i + 1) * N] = (normed * gain + shift).astype(BF16)
+        norm_ref[i] = normed
+        inv_ref[i] = jnp.broadcast_to(inverse, (N, CH))
     for i in range(ROWS):
         q, k, v, gate = project(nx_ref[i * N : (i + 1) * N], wp_ref[0], gb_ref[0:1])
         q_ref[i] = q
@@ -189,7 +203,7 @@
 def k2_body(
     x_ref, q_ref, k_ref, v_ref, gate_ref, recv_ref, mask_ref, wo_ref, ob_ref, gain_ref, shift_ref, wb_ref,
     part_ref, mixed_ref, probs_ref, nx_ref, norm_ref, inv_ref, msg_ref,
-    raw_s, own_s, first_s, row_ref, bias_ref,
+    raw_s, own_s, first_s, row_ref, bias_ref, att_s,
 ):
     key = key_column(mask_ref)
     for d in range(GROUP):
@@ -205,12 +219,15 @@
         probs = probabilities(q_ref[i], k_ref[i], bias_ref)
         for h in range(HEADS):
             probs_ref[i, h] = probs[h]
-        att = weighted(v_ref[i], [p.astype(BF16) for p in probs])
+        att_s[i] = weighted(v_ref[i], [p.astype(BF16) for p in probs])
+    for i in range(ROWS):
         gate = gate_ref[i]
-        gated = gate * att
+        gated = gate * att_s[i]
         part_ref[i] = gated * (1.0 - gate)
         mixed = gated.astype(BF16)
         mixed_ref[i * N : (i + 1) * N] = mixed
+    for i in range(ROWS):
+        mixed = mixed_ref[i * N : (i + 1) * N]
         first = x_ref[i].astype(F32) + dot_nn(mixed, w_out) + out_bias
         first = first.astype(BF16)
         row_ref[i] = first
@@ -263,7 +280,7 @@
 def k3_body(
     recv_ref, mask_ref, gm_ref, gain_ref, shift_ref, wp_ref, gb_ref,
     msg_ref, small_ref, nx_ref, joint_ref, mixed_ref,
-    flat_s, x_s, raw_s, bias_s, sum_s, norm_s, inv_s, q_s, k_s, v_s, gate_s, att_s, probs_s, grad_s,
+    flat_s, x_s, raw_s, bias_s, sum_s, norm_s, inv_s, q_s, k_s, v_s, gate_s, att_s, probs_s, grad_s, scores_s,
 ):
     key = key_column(mask_ref)
     for d in range(GROUP):
@@ -294,10 +311,8 @@
         joint_ref[i * N : (i + 1) * N, 3 * CH :] = grad_logit
         logit_sum += fold8(grad_logit.astype(F32))
     for i in range(ROWS):
-        probs = [probs_s[i, h] for h in range(HEADS)]
-        joint_ref[i * N : (i + 1) * N, 0 : 3 * CH] = attention_back(
-            probs, q_s[i], k_s[i], v_s[i], grad_s[i], sum_s
-        )
+        scores_back(i, probs_s, v_s, grad_s, sum_s, scores_s)
+    joint_back(probs_s, scores_s, q_s, k_s, grad_s, joint_ref)
     gain_sum = jnp.zeros((8, CH), F32)
     shift_sum = jnp.zeros((8, CH), F32)
     for i in range(ROWS):
@@ -350,7 +365,7 @@
     recv_ref, cot_ref, q_ref, k_ref, v_ref, gate_ref, part_ref, probs_ref, mixed_ref, nx_ref,
     nx1_ref, norm1_ref, inv1_ref, gain_ref, wp_ref, wb_ref, wo_ref, wg1_ref,
     up_ref, gn_ref, msg_ref, small_ref,
-    flat_s, la_s, gb_s, sum_s, joint_s, grad_s, upb_s,
+    flat_s, la_s, gb_s, sum_s, joint_s, grad_s, upb_s, scores_s,
 ):
     gather_rows(recv_ref, flat_s, la_s)
     gb_t = bias_sum(recv_ref, BLOCK, gb_s, LOW2)
@@ -377,10 +392,8 @@
         joint_s[i * N : (i + 1) * N, 3 * CH :] = grad_logit
         logit_sum += fold8(grad_logit.astype(F32))
     for i in range(ROWS):
-        probs = [probs_ref[i, h] for h in range(HEADS)]
-        joint_s[i * N : (i + 1) * N, 0 : 3 * CH] = attention_back(
-            probs, q_ref[i], k_ref[i], v_ref[i], grad_s[i], sum_s
-        )
+        scores_back(i, probs_ref, v_ref, grad_s, sum_s, scores_s)
+    joint_back(probs_ref, scores_s, q_ref, k_ref, grad_s, joint_s)
     for i in range(ROWS):
         gn_ref[i] = dot_nt(joint_s[i * N : (i + 1) * N], wp_ref[0])
     small_ref[0:8] = gain_sum
@@ -401,13 +414,6 @@
             msg_ref[e, block * SLICE : (block + 1) * SLICE] = part[e * SLICE : (e + 1) * SLICE]
 
     weight_grads(nx_ref, joint_s, mixed_ref, upb_s, put)
-
-
-def k4x_body(x_ref, norm_ref, inv_ref):
-    for i in range(ROWS):
-        normed, inverse = normalise(x_ref[i].astype(F32))
-        norm_ref[i] = normed
-        inv_ref[i] = jnp.broadcast_to(inverse, (N, CH))
 
 
 def k5_body(
@@ -526,9 +532,9 @@
 
     vec_f = ((2, CH), F32)
 
-    nx0, msg0 = call(
+    (msg0,) = call(
         k1_body,
-        [flat_b, pack],
+        [pack],
         [rows_b, rows_b, vec_f, vec_f, ((2, HEADS, CH), BF16), own_bias, flat_f],
         "norm_first",
         far=range(5),
@@ -536,13 +542,13 @@
         big=True,
     )(pair_rep, cotangent, ln_gain, ln_shift, w_bias)
     recv0 = swap(msg0)
-    q, k, v, gate = call(k1b_body, [rows_b, rows_b, rows_b, rows_f], [], "project_first")(
-        nx0, w_proj, gate_bias
-    )
+    q, k, v, gate, nx0, norm0, inv0 = call(
+        k1b_body, [rows_b, rows_b, rows_b, rows_f, flat_b, rows_f, rows_f], [], "project_first"
+    )(pair_rep, ln_gain, ln_shift, w_proj, gate_bias)
     part0, mixed0, probs0, nx1, norm1, inv1, msg1 = call(
         k2_body,
         [rows_f, flat_b, probs, rows_b, rows_f, rows_f, pack],
-        [raw, own_bias, flat_f, rows_b, mats],
+        [raw, own_bias, flat_f, rows_b, mats, rows_f],
         "attend_first",
     )(pair_rep, q, k, v, gate, recv0, mask, w_out, out_bias, ln_gain, ln_shift, w_bias)
     recv1 = swap(msg1)
@@ -553,7 +559,7 @@
         k3_body,
         [((GROUP, BLOCK + (1 + LOW2) * BROWS, CH), BF16), ((24, CH), F32), flat_b, joint_b, flat_b],
         [flat_f, rows_f, raw, mats, mats, rows_f, rows_f]
-        + [rows_b, rows_b, rows_b, rows_f, rows_f, probs, rows_b],
+        + [rows_b, rows_b, rows_b, rows_f, rows_f, probs, rows_b, ((ROWS, HEADS, N, N), BF16)],
         "second_module",
     )(recv1, mask, gm1, ln_gain, ln_shift, w_proj, gate_bias)
     recv2 = swap(msg2)
@@ -563,14 +569,13 @@
     up, gn, msg3, small = call(
         k4_body,
         [rows_b, rows_f, ((GROUP, 2 * WROWS + (1 + LOW3) * BROWS, CH), BF16), ((40, CH), F32)],
-        [flat_f, rows_f, bias_8, mats, joint_b, rows_b, flat_b],
+        [flat_f, rows_f, bias_8, mats, joint_b, rows_b, flat_b, ((ROWS, HEADS, N, N), BF16)],
         "back_first",
     )(
         recv2, cotangent, q, k, v, gate, part0, probs0, mixed0, nx0, nx1, norm1, inv1,
         ln_gain, w_proj, w_bias, w_out, wg1,
     )
     recv3 = swap(msg3)
-    norm0, inv0 = call(k4x_body, [rows_f, rows_f], [], "norm_again")(after(pair_rep, recv3))
     full, msg4 = call(
         k5_body, [rows_f, ((GROUP, 2 * WROWS + 32, CH), BF16)], [bias_8], "grad_sums"
     )(recv3, norm0, gn, nx0, small1, total1, small, w_bias)

time: 103 us -> 99.1 us (0.962)
  Pallas kernels: 20.6 us -> 17 us
  waiting for transfers between devices: 8.61 us -> 5.85 us
  local copies, waits for them, and re-layouts: 2.64 us -> 4.83 us
    pallas_call x11 -> x10, Pallas kernels: 20.6 us -> 17 us  [run(): pl.pallas_call(body, in_specs=[far_spec if n in far else near_spec for n...]
    all_to_all x1, waiting for transfers between devices: 8.61 us -> 5.85 us  [swap(): return lax.all_to_all(x, 'dap', 0, 0, tiled=True)]
    unnamed x28 -> x34, local copies, waits for them, and re-layouts: 2.64 us -> 4.83 us
  transfers between devices with their start and end apart: 1 -> 1, of which waited for: 1 -> 1; matrix products, arithmetic and copies ran while one was open for 0% -> 0% of each run, Pallas kernels for 0% -> 1%
where the time goes in v3:
time: 99.1 us; the launch traced here: 98.6 us
  blocking collectives  62.7 us (63%)
  Pallas kernels  17 us (17%)
  starting transfers between devices  7.41 us (7%)
  waiting for transfers between devices  5.85 us (6%)
  local copies, waits for them, and re-layouts  4.83 us (5%)
    all_to_all x4, blocking collectives, swap(): return lax.all_to_all(x, 'dap', 0, 0, tiled=True)  62.7 us
    pallas_call x10, Pallas kernels, run(): pl.pallas_call(body, in_specs=[far_spec if n in far else near_spec for n...  17 us
    all_to_all x1, starting transfers between devices, swap(): return lax.all_to_all(x, 'dap', 0, 0, tiled=True)  7.41 us
    all_to_all x1, waiting for transfers between devices, swap(): return lax.all_to_all(x, 'dap', 0, 0, tiled=True)  5.85 us
    unnamed x34, local copies, waits for them, and re-layouts  4.83 us
  transfers between devices with their start and end apart: 1, of which 1 were waited for; matrix products, arithmetic and copies ran while one was open for 0% of the time, Pallas kernels for 1%

profile of v3, /device:TPU:1, one launch (start us, length us, event | category | flops | bytes accessed | tf_op | source)
XLA Modules:
  0.0 98.6 jit_solution(4938732418911569044)
XLA Ops:
  0.6 0.0 copy-start.10
  0.6 0.0 copy-start.12
  0.7 0.0 copy-start.1
  0.7 0.0 copy-start.8
  0.7 0.0 copy-start.7
  0.7 0.0 copy-start.14
  0.7 0.0 copy-start.13
  0.7 2.5 %norm_first.1 = bf16[8,192,128]{2,1,0:T(8,128)(2,1)} custom-call(bf16[12,96,128]{2,1,0:T(8,128)(2,1)} %x_ref.3, bf16[12,96,128]{2,1,0:T(8,128)(2,1)} %cot_ref.1, f32[2,128]{1,0:T(2,128)} %gain_ref.9, f32[2,128]{1,0:T(2,128)} %shift_ref.5, bf16[2,4,128]{2,1,0:T(4,128)(2,1)} %bitcast.3), custom_call_target="tpu_custom_call" | custom-call | flops 100000000 | bytes 2000000 | tf_op jit(solution)/shard_map/norm_first/pallas_call | solution.py:494
  3.2 7.4 %all-to-all-start = ((bf16[8,192,128]{2,1,0:T(8,128)(2,1)}), bf16[8,192,128]{2,1,0:T(8,128)(2,1)S(1)}, u32[]{:S(2)}, u32[]{:S(2)}) async-start(bf16[8,192,128]{2,1,0:T(8,128)(2,1)} %norm_first.1), calls=%async_computation | async-start | bytes 786432 | tf_op jit(solution)/shard_map/all_to_all | solution.py:513
  10.6 1.0 copy-done
  11.6 0.9 copy-done.3
  12.5 0.7 copy-done.9
  13.2 0.7 copy-done.11
  13.9 0.7 copy-done.15
  14.6 1.0 %project_first.1 = (bf16[12,96,128]{2,1,0:T(8,128)(2,1)S(1)}, bf16[12,96,128]{2,1,0:T(8,128)(2,1)S(1)}, bf16[12,96,128]{2,1,0:T(8,128)(2,1)S(1)}, f32[12,96,128]...) custom-call(bf16[12,96,128]{2,1,0:T(8,128)(2,1)S(1)} %copy-done, ...), custom_call_target="tpu_custom_call" | custom-call | flops 100000000 | bytes 2000000 | tf_op jit(solution)/shard_map/project_first/pallas_call | solution.py:494
  15.6 0.0 copy-start.5
  15.6 0.8 copy-done.5
  16.5 5.8 %all-to-all-done.recv_ref = bf16[8,192,128]{2,1,0:T(8,128)(2,1)S(1)} async-done(((bf16[8,192,128]{2,1,0:T(8,128)(2,1)}), bf16[8,192,128]{2,1,0:T(8,128)(2,1)S(1)}, u32[]{:S(2)}, u32[]{:S(2)}) %all-to-all-start) | async-done | bytes 393248 | tf_op jit(solution)/shard_map/all_to_all | solution.py:513
  22.3 0.0 copy-done.12
  22.4 2.0 %attend_first.1 = (f32[12,96,128]{2,1,0:T(8,128)S(1)}, bf16[1152,128]{1,0:T(8,128)(2,1)S(1)}, f32[12,4,96,96]{3,2,1,0:T(8,128)S(1)}, bf16[12,96,128]{2,1,0:T(8,1...) custom-call(bf16[12,96,128]{2,1,0:T(8,128)(2,1)S(1)} %copy-done.1, ...), custom_call_target="tpu_custom_call" | custom-call | flops 100000000 | bytes 2000000 | tf_op jit(solution)/shard_map/attend_first/pallas_call | solution.py:494
  24.4 14.9 %all_to_all.25.recv_ref = bf16[8,192,128]{2,1,0:T(8,128)(2,1)S(1)} all-to-all(bf16[8,192,128]{2,1,0:T(8,128)(2,1)S(1)} %get-tuple-element.50), channel_id=1, replica_groups=mesh['dap'=8,'dp'=32] {'dap'}, dimensions={0} | all-to-all | bytes 786432 | tf_op jit(solution)/shard_map/all_to_all | solution.py:513
  39.3 0.4 cotangent_rows.1
  39.8 4.5 %second_module.1 = (bf16[8,240,128]{2,1,0:T(8,128)(2,1)S(1)}, f32[24,128]{1,0:T(8,128)S(1)}, bf16[1152,128]{1,0:T(8,128)(2,1)S(1)}, bf16[1152,512]{1,0:T(8,128)(2,1)S(1)}, bf16[1152,128]{1,0:T(8,128)(2,1)S(1)}) custom-call(bf16[8,192,128]{2,1,0:T(8,128)(2,1)S(1)} %all_to_all.25.recv_ref, s32[1,96]{1,0:T(1,128)S(1)} %bitcast.8, ...), custom_call_target="tpu_custom_call" | custom-call | flops 100000000 | bytes 2000000 | tf_op jit(solution)/shard_map/second_module/pallas_call | solution.py:494
  44.3 16.9 %all_to_all.26.recv_ref = bf16[8,240,128]{2,1,0:T(8,128)(2,1)S(1)} all-to-all(bf16[8,240,128]{2,1,0:T(8,128)(2,1)S(1)} %get-tuple-element.53), channel_id=1, replica_groups=mesh['dap'=8,'dp'=32] {'dap'}, dimensions={0} | all-to-all | bytes 983040 | tf_op jit(solution)/shard_map/all_to_all | solution.py:513
  61.2 0.6 second_weights.1.wg1_ref
  61.8 0.0 copy-done.2
  61.8 3.5 %back_first.1 = (bf16[12,96,128]{2,1,0:T(8,128)(2,1)S(1)}, f32[12,96,128]{2,1,0:T(8,128)S(1)}, bf16[8,208,128]{2,1,0:T(8,128)(2,1)S(1)}, f32[40,128]{1,0:T(8,128)S(1)}) custom-call(bf16[8,240,128]{2,1,0:T(8,128)(2,1)S(1)} %all_to_all.26.recv_ref, bf16[12,96,128]{2,1,0:T(8,128)(2,1)S(1)} %copy-done.2, bf16[12,96,128]{2,1,0:T(8,128)(2,1)S(1)} %get-tuple-element.46.q_ref, ...), custom_call_target="tpu_custom_call" | custom-call | flops 100000000 | bytes 2000000 | tf_op jit(solution)/shard_map/back_first/pallas_call | solution.py:494
  65.4 15.9 %all_to_all.27.recv_ref = bf16[8,208,128]{2,1,0:T(8,128)(2,1)S(1)} all-to-all(bf16[8,208,128]{2,1,0:T(8,128)(2,1)S(1)} %get-tuple-element.66), channel_id=1, replica_groups=mesh['dap'=8,'dp'=32] {'dap'}, dimensions={0} | all-to-all | bytes 851968 | tf_op jit(solution)/shard_map/all_to_all | solution.py:513
  81.2 0.4 grad_sums.1
  81.7 15.0 %all_to_all.28.recv_ref = bf16[8,192,128]{2,1,0:T(8,128)(2,1)S(1)} all-to-all(bf16[8,192,128]{2,1,0:T(8,128)(2,1)S(1)} %get-tuple-element.73), channel_id=1, replica_groups=mesh['dap'=8,'dp'=32] {'dap'}, dimensions={0} | all-to-all | bytes 786432 | tf_op jit(solution)/shard_map/all_to_all | solution.py:513
  96.6 1.1 %grad_pair.1 = bf16[12,96,128]{2,1,0:T(8,128)(2,1)} custom-call(f32[12,96,128]{2,1,0:T(8,128)S(1)} %get-tuple-element.74.full_ref, f32[12,96,128]{2,1,0:T(8,128)S(1)} %get-tuple-element.67.norm_ref, f32[12,96,128]{2,1,0:T(8,128)S(1)} %copy-done.6, bf16[12,96,128]{2,1,0:T(8,128)(2,1)S(1)} %get-tuple-element.76.up_ref, f32[2,128]{1,0:T(2,128)S(1)} %copy-done.10), custom_call_target="tpu_custom_call" | custom-call | flops 100000000 | bytes 2000000 | tf_op jit(solution)/shard_map/grad_pair/pallas_call | solution.py:494
  97.8 0.9 weight_sums.1
  (18 shorter events, 0.0 us)
Async XLA Ops:
  0.6 21.7 %copy-start.10 = (f32[2,128]{1,0:T(2,128)S(1)}, f32[2,128]{1,0:T(2,128)}, u32[]{:S(2)}) copy-start(f32[2,128]{1,0:T(2,128)} %gain_ref.9) | copy-start | bytes 3076
  0.6 21.7 %copy-start.12 = (f32[2,128]{1,0:T(2,128)S(1)}, f32[2,128]{1,0:T(2,128)}, u32[]{:S(2)}) copy-start(f32[2,128]{1,0:T(2,128)} %shift_ref.5) | copy-start | bytes 3076
  0.7 21.7 %copy-start.1 = (bf16[12,96,128]{2,1,0:T(8,128)(2,1)S(1)}, bf16[12,96,128]{2,1,0:T(8,128)(2,1)}, u32[]{:S(2)}) copy-start(bf16[12,96,128]{2,1,0:T(8,128)(2,1)} %x_ref.3) | copy-start | bytes 884740
  0.7 21.6 %copy-start.8 = (bf16[2,128,4]{1,2,0:T(4,128)(2,1)S(1)}, bf16[2,128,4]{1,2,0:T(4,128)(2,1)}, u32[]{:S(2)}) copy-start(bf16[2,128,4]{1,2,0:T(4,128)(2,1)} %param.16) | copy-start | bytes 6148
  0.7 21.6 %copy-start.7 = (bf16[2,128,128]{2,1,0:T(8,128)(2,1)S(1)}, bf16[2,128,128]{2,1,0:T(8,128)(2,1)}, u32[]{:S(2)}) copy-start(bf16[2,128,128]{2,1,0:T(8,128)(2,1)} %wo_ref.5) | copy-start | bytes 196612
  0.7 21.6 %copy-start.14 = (f32[2,128]{1,0:T(2,128)S(1)}, f32[2,128]{1,0:T(2,128)}, u32[]{:S(2)}) copy-start(f32[2,128]{1,0:T(2,128)} %ob_ref.1) | copy-start | bytes 3076
  0.7 21.6 %copy-start.13 = (s32[96]{0:T(128)S(1)}, s32[96]{0:T(128)}, u32[]{:S(2)}) copy-start(s32[96]{0:T(128)} %param.12) | copy-start | bytes 1156
  3.2 19.1 %all-to-all-start = ((bf16[8,192,128]{2,1,0:T(8,128)(2,1)}), bf16[8,192,128]{2,1,0:T(8,128)(2,1)S(1)}, u32[]{:S(2)}, u32[]{:S(2)}) async-start(bf16[8,192,128]{2,1,0:T(8,128)(2,1)} %norm_first.1), calls=%async_computation | async-start | bytes 786432 | tf_op jit(solution)/shard_map/all_to_all | solution.py:513
  10.6 1.0 copy-start
  11.6 0.9 copy-start.3
  12.5 0.7 copy-start.9
  13.2 0.7 copy-start.11
  13.9 0.7 copy-start.15
  14.6 25.2 %copy-start.4 = (bf16[2,128,512]{2,1,0:T(8,128)(2,1)S(1)}, bf16[2,128,512]{2,1,0:T(8,128)(2,1)}, u32[]{:S(2)}) copy-start(bf16[2,128,512]{2,1,0:T(8,128)(2,1)} %wp_ref.5) | copy-start | bytes 786436
  14.6 25.2 %copy-start.16 = (f32[2,128]{1,0:T(2,128)S(1)}, f32[2,128]{1,0:T(2,128)}, u32[]{:S(2)}) copy-start(f32[2,128]{1,0:T(2,128)} %gb_ref.3) | copy-start | bytes 3076
  15.6 0.8 copy-start.5
  39.7 22.1 %copy-start.2 = (bf16[12,96,128]{2,1,0:T(8,128)(2,1)S(1)}, bf16[12,96,128]{2,1,0:T(8,128)(2,1)}, u32[]{:S(2)}) copy-start(bf16[12,96,128]{2,1,0:T(8,128)(2,1)} %cot_ref.1) | copy-start | bytes 884740
  65.4 31.3 %copy-start.6 = (f32[12,96,128]{2,1,0:T(8,128)S(1)}, f32[12,96,128]{2,1,0:T(8,128)}, u32[]{:S(2)}) copy-start(f32[12,96,128]{2,1,0:T(8,128)} %copy-done.5) | copy-start | bytes 1769476

commit v4 on v3

--- a/solution.py
+++ b/solution.py
@@ -17,7 +17,6 @@
 PACK = BLOCK + BROWS
 SLICE = CH // GROUP
 WROWS = 5 * SLICE
-LOW2, LOW3 = 1, 0
 EPSILON = 1e-05
 SCALING = WIDTH ** (-0.5)
 F32 = jnp.float32
@@ -269,12 +268,9 @@
     return top, (x - top.astype(F32)).astype(BF16)
 
 
-def put_sums(msg_ref, e, start, rows, low):
-    parts = split2(rows) if low else [rows.astype(BF16)]
-    for n, part in enumerate(parts):
-        at = start + n * BROWS
-        msg_ref[e, at : at + BROWS, 0:N] = part
-        msg_ref[e, at : at + BROWS, N:CH] = jnp.zeros((BROWS, CH - N), BF16)
+def put_sums(msg_ref, e, start, rows):
+    msg_ref[e, start : start + BROWS, 0:N] = rows.astype(BF16)
+    msg_ref[e, start : start + BROWS, N:CH] = jnp.zeros((BROWS, CH - N), BF16)
 
 
 def k3_body(
@@ -327,7 +323,7 @@
     for e in range(GROUP):
         msg_ref[e, 0:BLOCK] = flat_s[e * BLOCK : (e + 1) * BLOCK].astype(BF16)
         rows = [sum_s[h, e * ROWS : (e + 1) * ROWS] for h in range(HEADS)]
-        put_sums(msg_ref, e, BLOCK, jnp.concatenate(rows, axis=0), LOW2)
+        put_sums(msg_ref, e, BLOCK, jnp.concatenate(rows, axis=0))
 
 
 def k3w_body(nx_ref, joint_ref, mixed_ref, up_ref, out_ref):
@@ -339,26 +335,22 @@
     weight_grads(nx_ref, joint_ref, mixed_ref, up_ref, put)
 
 
-def bias_sum(recv_ref, start, gb_s, low):
+def bias_sum(recv_ref, start, gb_s):
     total = recv_ref[0, start : start + BROWS].astype(F32)
     for d in range(1, GROUP):
         total += recv_ref[d, start : start + BROWS].astype(F32)
-    if low:
-        for d in range(GROUP):
-            total += recv_ref[d, start + BROWS : start + 2 * BROWS].astype(F32)
     gb_s[...] = jnp.zeros_like(gb_s)
-    total = total.astype(BF16).astype(F32)
     for r in range(ROWS):
         for h in range(HEADS):
             gb_s[r * 8 + h : r * 8 + h + 1] = total[h * ROWS + r : h * ROWS + r + 1]
-    return gb_s[...].T[0:N].astype(BF16)
+    return jnp.concatenate(split2(gb_s[...].T[0:N]), axis=1)
 
 
 def bias_part(i, gb_s, gb_t, wb_tiled, nx):
     rows = lax.broadcasted_iota(jnp.int32, (ROWS * 8, CH), 0) // 8
     picked = jnp.where(rows == i, wb_tiled, jnp.zeros_like(wb_tiled))
-    grad_w = dot_nn(gb_s[i * 8 : (i + 1) * 8, 0:N].astype(BF16), nx)
-    return dot_nn(gb_t, picked), grad_w
+    top, low = split2(gb_s[i * 8 : (i + 1) * 8, 0:N])
+    return dot_nn(gb_t, jnp.concatenate([picked, picked], axis=0)), dot_nn(top, nx) + dot_nn(low, nx)
 
 
 def k4_body(
@@ -368,7 +360,7 @@
     flat_s, la_s, gb_s, sum_s, joint_s, grad_s, upb_s, scores_s,
 ):
     gather_rows(recv_ref, flat_s, la_s)
-    gb_t = bias_sum(recv_ref, BLOCK, gb_s, LOW2)
+    gb_t = bias_sum(recv_ref, BLOCK, gb_s)
     wb = w_bias_rows(wb_ref, 1)
     wb_tiled = jnp.concatenate([wb.astype(F32)] * ROWS, axis=0).astype(BF16)
     sum_s[...] = jnp.zeros_like(sum_s)
@@ -405,7 +397,7 @@
         flat_s[h * N : (h + 1) * N, 0:N] = sum_s[h].T
     for e in range(GROUP):
         rows = [flat_s[h * N + e * ROWS : h * N + (e + 1) * ROWS, 0:N] for h in range(HEADS)]
-        put_sums(msg_ref, e, 2 * WROWS, jnp.concatenate(rows, axis=0), LOW3)
+        put_sums(msg_ref, e, 2 * WROWS, jnp.concatenate(rows, axis=0))
         msg_ref[e, WROWS : 2 * WROWS] = wg1_ref[e]
 
     def put(block, part):
@@ -420,7 +412,7 @@
     recv_ref, norm_ref, gn_ref, nx_ref, small1_ref, total1_ref, small_ref, wb_ref,
     full_ref, msg_ref, gb_s,
 ):
-    gb_t = bias_sum(recv_ref, 2 * WROWS, gb_s, LOW3)
+    gb_t = bias_sum(recv_ref, 2 * WROWS, gb_s)
     wb = w_bias_rows(wb_ref, 0)
     wb_tiled = jnp.concatenate([wb.astype(F32)] * ROWS, axis=0).astype(BF16)
     zero = jnp.zeros((8, CH), F32)
@@ -557,7 +549,7 @@
     )(after(recv0, recv1), w_out)
     msg2, small1, nxw, joint1, mixed1 = call(
         k3_body,
-        [((GROUP, BLOCK + (1 + LOW2) * BROWS, CH), BF16), ((24, CH), F32), flat_b, joint_b, flat_b],
+        [pack, ((24, CH), F32), flat_b, joint_b, flat_b],
         [flat_f, rows_f, raw, mats, mats, rows_f, rows_f]
         + [rows_b, rows_b, rows_b, rows_f, rows_f, probs, rows_b, ((ROWS, HEADS, N, N), BF16)],
         "second_module",
@@ -568,7 +560,7 @@
     )
     up, gn, msg3, small = call(
         k4_body,
-        [rows_b, rows_f, ((GROUP, 2 * WROWS + (1 + LOW3) * BROWS, CH), BF16), ((40, CH), F32)],
+        [rows_b, rows_f, ((GROUP, 2 * WROWS + BROWS, CH), BF16), ((40, CH), F32)],
         [flat_f, rows_f, bias_8, mats, joint_b, rows_b, flat_b, ((ROWS, HEADS, N, N), BF16)],
         "back_first",
     )(

time: 99.1 us -> 97.3 us (0.982)
  blocking collectives: 62.7 us -> 60.6 us
    all_to_all x4, blocking collectives: 62.7 us -> 60.6 us  [swap(): return lax.all_to_all(x, 'dap', 0, 0, tiled=True)]
where the time goes in v4:
time: 97.3 us; the launch traced here: 96.9 us
  blocking collectives  60.6 us (62%)
  Pallas kernels  17.3 us (18%)
  starting transfers between devices  7.41 us (8%)
  waiting for transfers between devices  5.85 us (6%)
  local copies, waits for them, and re-layouts  4.83 us (5%)
    all_to_all x4, blocking collectives, swap(): return lax.all_to_all(x, 'dap', 0, 0, tiled=True)  60.6 us
    pallas_call x10, Pallas kernels, run(): pl.pallas_call(body, in_specs=[far_spec if n in far else near_spec for n...  17.3 us
    all_to_all x1, starting transfers between devices, swap(): return lax.all_to_all(x, 'dap', 0, 0, tiled=True)  7.41 us
    all_to_all x1, waiting for transfers between devices, swap(): return lax.all_to_all(x, 'dap', 0, 0, tiled=True)  5.85 us
    unnamed x34, local copies, waits for them, and re-layouts  4.83 us
  transfers between devices with their start and end apart: 1, of which 1 were waited for; matrix products, arithmetic and copies ran while one was open for 0% of the time, Pallas kernels for 1%

profile of v4, /device:TPU:1, one launch (start us, length us, event | category | flops | bytes accessed | tf_op | source)
XLA Modules:
  0.0 96.9 jit_solution(5732825855172261849)
XLA Ops:
  0.6 0.0 copy-start.10
  0.6 0.0 copy-start.12
  0.7 0.0 copy-start.1
  0.7 0.0 copy-start.8
  0.7 0.0 copy-start.7
  0.7 0.0 copy-start.14
  0.7 0.0 copy-start.13
  0.7 2.5 %norm_first.1 = bf16[8,192,128]{2,1,0:T(8,128)(2,1)} custom-call(bf16[12,96,128]{2,1,0:T(8,128)(2,1)} %x_ref.3, bf16[12,96,128]{2,1,0:T(8,128)(2,1)} %cot_ref.1, f32[2,128]{1,0:T(2,128)} %gain_ref.9, f32[2,128]{1,0:T(2,128)} %shift_ref.5, bf16[2,4,128]{2,1,0:T(4,128)(2,1)} %bitcast.3), custom_call_target="tpu_custom_call" | custom-call | flops 100000000 | bytes 2000000 | tf_op jit(solution)/shard_map/norm_first/pallas_call | solution.py:486
  3.2 7.4 %all-to-all-start = ((bf16[8,192,128]{2,1,0:T(8,128)(2,1)}), bf16[8,192,128]{2,1,0:T(8,128)(2,1)S(1)}, u32[]{:S(2)}, u32[]{:S(2)}) async-start(bf16[8,192,128]{2,1,0:T(8,128)(2,1)} %norm_first.1), calls=%async_computation | async-start | bytes 786432 | tf_op jit(solution)/shard_map/all_to_all | solution.py:505
  10.6 1.0 copy-done
  11.6 0.9 copy-done.3
  12.5 0.7 copy-done.9
  13.2 0.7 copy-done.11
  13.9 0.7 copy-done.15
  14.6 1.0 %project_first.1 = (bf16[12,96,128]{2,1,0:T(8,128)(2,1)S(1)}, bf16[12,96,128]{2,1,0:T(8,128)(2,1)S(1)}, bf16[12,96,128]{2,1,0:T(8,128)(2,1)S(1)}, f32[12,96,128]...) custom-call(bf16[12,96,128]{2,1,0:T(8,128)(2,1)S(1)} %copy-done, ...), custom_call_target="tpu_custom_call" | custom-call | flops 100000000 | bytes 2000000 | tf_op jit(solution)/shard_map/project_first/pallas_call | solution.py:486
  15.6 0.0 copy-start.5
  15.6 0.8 copy-done.5
  16.5 5.8 %all-to-all-done.recv_ref = bf16[8,192,128]{2,1,0:T(8,128)(2,1)S(1)} async-done(((bf16[8,192,128]{2,1,0:T(8,128)(2,1)}), bf16[8,192,128]{2,1,0:T(8,128)(2,1)S(1)}, u32[]{:S(2)}, u32[]{:S(2)}) %all-to-all-start) | async-done | bytes 393248 | tf_op jit(solution)/shard_map/all_to_all | solution.py:505
  22.3 0.0 copy-done.10
  22.3 0.0 copy-done.12
  22.4 2.0 %attend_first.1 = (f32[12,96,128]{2,1,0:T(8,128)S(1)}, bf16[1152,128]{1,0:T(8,128)(2,1)S(1)}, f32[12,4,96,96]{3,2,1,0:T(8,128)S(1)}, bf16[12,96,128]{2,1,0:T(8,1...) custom-call(bf16[12,96,128]{2,1,0:T(8,128)(2,1)S(1)} %copy-done.1, ...), custom_call_target="tpu_custom_call" | custom-call | flops 100000000 | bytes 2000000 | tf_op jit(solution)/shard_map/attend_first/pallas_call | solution.py:486
  24.4 14.9 %all_to_all.25.recv_ref = bf16[8,192,128]{2,1,0:T(8,128)(2,1)S(1)} all-to-all(bf16[8,192,128]{2,1,0:T(8,128)(2,1)S(1)} %get-tuple-element.50), channel_id=1, replica_groups=mesh['dap'=8,'dp'=32] {'dap'}, dimensions={0} | all-to-all | bytes 786432 | tf_op jit(solution)/shard_map/all_to_all | solution.py:505
  39.3 0.4 cotangent_rows.1
  39.8 4.5 %second_module.1 = (bf16[8,192,128]{2,1,0:T(8,128)(2,1)S(1)}, f32[24,128]{1,0:T(8,128)S(1)}, bf16[1152,128]{1,0:T(8,128)(2,1)S(1)}, bf16[1152,512]{1,0:T(8,128)(2,1)S(1)}, bf16[1152,128]{1,0:T(8,128)(2,1)S(1)}) custom-call(bf16[8,192,128]{2,1,0:T(8,128)(2,1)S(1)} %all_to_all.25.recv_ref, s32[1,96]{1,0:T(1,128)S(1)} %bitcast.8, ...), custom_call_target="tpu_custom_call" | custom-call | flops 100000000 | bytes 2000000 | tf_op jit(solution)/shard_map/second_module/pallas_call | solution.py:486
  44.3 14.9 %all_to_all.26.recv_ref = bf16[8,192,128]{2,1,0:T(8,128)(2,1)S(1)} all-to-all(bf16[8,192,128]{2,1,0:T(8,128)(2,1)S(1)} %get-tuple-element.53), channel_id=1, replica_groups=mesh['dap'=8,'dp'=32] {'dap'}, dimensions={0} | all-to-all | bytes 786432 | tf_op jit(solution)/shard_map/all_to_all | solution.py:505
  59.2 0.6 second_weights.1.wg1_ref
  59.8 3.7 %back_first.1 = (bf16[12,96,128]{2,1,0:T(8,128)(2,1)S(1)}, f32[12,96,128]{2,1,0:T(8,128)S(1)}, bf16[8,208,128]{2,1,0:T(8,128)(2,1)S(1)}, f32[40,128]{1,0:T(8,128)S(1)}) custom-call(bf16[8,192,128]{2,1,0:T(8,128)(2,1)S(1)} %all_to_all.26.recv_ref, bf16[12,96,128]{2,1,0:T(8,128)(2,1)S(1)} %copy-done.2, bf16[12,96,128]{2,1,0:T(8,128)(2,1)S(1)} %get-tuple-element.46.q_ref, ...), custom_call_target="tpu_custom_call" | custom-call | flops 100000000 | bytes 2000000 | tf_op jit(solution)/shard_map/back_first/pallas_call | solution.py:486
  63.5 15.7 %all_to_all.27.recv_ref = bf16[8,208,128]{2,1,0:T(8,128)(2,1)S(1)} all-to-all(bf16[8,208,128]{2,1,0:T(8,128)(2,1)S(1)} %get-tuple-element.66), channel_id=1, replica_groups=mesh['dap'=8,'dp'=32] {'dap'}, dimensions={0} | all-to-all | bytes 851968 | tf_op jit(solution)/shard_map/all_to_all | solution.py:505
  79.3 0.6 grad_sums.1
  79.9 15.0 %all_to_all.28.recv_ref = bf16[8,192,128]{2,1,0:T(8,128)(2,1)S(1)} all-to-all(bf16[8,192,128]{2,1,0:T(8,128)(2,1)S(1)} %get-tuple-element.73), channel_id=1, replica_groups=mesh['dap'=8,'dp'=32] {'dap'}, dimensions={0} | all-to-all | bytes 786432 | tf_op jit(solution)/shard_map/all_to_all | solution.py:505
  94.9 1.1 %grad_pair.1 = bf16[12,96,128]{2,1,0:T(8,128)(2,1)} custom-call(f32[12,96,128]{2,1,0:T(8,128)S(1)} %get-tuple-element.74.full_ref, f32[12,96,128]{2,1,0:T(8,128)S(1)} %get-tuple-element.67.norm_ref, f32[12,96,128]{2,1,0:T(8,128)S(1)} %copy-done.6, bf16[12,96,128]{2,1,0:T(8,128)(2,1)S(1)} %get-tuple-element.76.up_ref, f32[2,128]{1,0:T(2,128)S(1)} %copy-done.10), custom_call_target="tpu_custom_call" | custom-call | flops 100000000 | bytes 2000000 | tf_op jit(solution)/shard_map/grad_pair/pallas_call | solution.py:486
  96.0 0.9 weight_sums.1
  (18 shorter events, 0.0 us)
Async XLA Ops:
  0.6 21.7 %copy-start.10 = (f32[2,128]{1,0:T(2,128)S(1)}, f32[2,128]{1,0:T(2,128)}, u32[]{:S(2)}) copy-start(f32[2,128]{1,0:T(2,128)} %gain_ref.9) | copy-start | bytes 3076
  0.6 21.7 %copy-start.12 = (f32[2,128]{1,0:T(2,128)S(1)}, f32[2,128]{1,0:T(2,128)}, u32[]{:S(2)}) copy-start(f32[2,128]{1,0:T(2,128)} %shift_ref.5) | copy-start | bytes 3076
  0.7 21.7 %copy-start.1 = (bf16[12,96,128]{2,1,0:T(8,128)(2,1)S(1)}, bf16[12,96,128]{2,1,0:T(8,128)(2,1)}, u32[]{:S(2)}) copy-start(bf16[12,96,128]{2,1,0:T(8,128)(2,1)} %x_ref.3) | copy-start | bytes 884740
  0.7 21.6 %copy-start.8 = (bf16[2,128,4]{1,2,0:T(4,128)(2,1)S(1)}, bf16[2,128,4]{1,2,0:T(4,128)(2,1)}, u32[]{:S(2)}) copy-start(bf16[2,128,4]{1,2,0:T(4,128)(2,1)} %param.16) | copy-start | bytes 6148
  0.7 21.6 %copy-start.7 = (bf16[2,128,128]{2,1,0:T(8,128)(2,1)S(1)}, bf16[2,128,128]{2,1,0:T(8,128)(2,1)}, u32[]{:S(2)}) copy-start(bf16[2,128,128]{2,1,0:T(8,128)(2,1)} %wo_ref.5) | copy-start | bytes 196612
  0.7 21.6 %copy-start.14 = (f32[2,128]{1,0:T(2,128)S(1)}, f32[2,128]{1,0:T(2,128)}, u32[]{:S(2)}) copy-start(f32[2,128]{1,0:T(2,128)} %ob_ref.1) | copy-start | bytes 3076
  0.7 21.6 %copy-start.13 = (s32[96]{0:T(128)S(1)}, s32[96]{0:T(128)}, u32[]{:S(2)}) copy-start(s32[96]{0:T(128)} %param.12) | copy-start | bytes 1156
  3.2 19.1 %all-to-all-start = ((bf16[8,192,128]{2,1,0:T(8,128)(2,1)}), bf16[8,192,128]{2,1,0:T(8,128)(2,1)S(1)}, u32[]{:S(2)}, u32[]{:S(2)}) async-start(bf16[8,192,128]{2,1,0:T(8,128)(2,1)} %norm_first.1), calls=%async_computation | async-start | bytes 786432 | tf_op jit(solution)/shard_map/all_to_all | solution.py:505
  10.6 1.0 copy-start
  11.6 0.9 copy-start.3
  12.5 0.7 copy-start.9
  13.2 0.7 copy-start.11
  13.9 0.7 copy-start.15
  14.6 25.2 %copy-start.4 = (bf16[2,128,512]{2,1,0:T(8,128)(2,1)S(1)}, bf16[2,128,512]{2,1,0:T(8,128)(2,1)}, u32[]{:S(2)}) copy-start(bf16[2,128,512]{2,1,0:T(8,128)(2,1)} %wp_ref.5) | copy-start | bytes 786436
  14.6 25.2 %copy-start.16 = (f32[2,128]{1,0:T(2,128)S(1)}, f32[2,128]{1,0:T(2,128)}, u32[]{:S(2)}) copy-start(f32[2,128]{1,0:T(2,128)} %gb_ref.3) | copy-start | bytes 3076
  15.6 0.8 copy-start.5
  39.7 20.1 %copy-start.2 = (bf16[12,96,128]{2,1,0:T(8,128)(2,1)S(1)}, bf16[12,96,128]{2,1,0:T(8,128)(2,1)}, u32[]{:S(2)}) copy-start(bf16[12,96,128]{2,1,0:T(8,128)(2,1)} %cot_ref.1) | copy-start | bytes 884740
  63.5 31.3 %copy-start.6 = (f32[12,96,128]{2,1,0:T(8,128)S(1)}, f32[12,96,128]{2,1,0:T(8,128)}, u32[]{:S(2)}) copy-start(f32[12,96,128]{2,1,0:T(8,128)} %copy-done.5) | copy-start | bytes 1769476

commit v5 on v4

--- a/solution.py
+++ b/solution.py
@@ -1,3 +1,5 @@
+import functools
+
 import jax
 import jax.numpy as jnp
 from jax import lax
@@ -257,9 +259,9 @@
 
 
 def weight_grads(nx_ref, joint_ref, mixed_ref, up_ref, put):
-    nx = nx_ref[...]
+    part = dot_tn(nx_ref[...], joint_ref[...])
     for block in range(4):
-        put(block, dot_tn(nx, joint_ref[:, block * CH : (block + 1) * CH]))
+        put(block, part[:, block * CH : (block + 1) * CH])
     put(4, dot_tn(mixed_ref[...], up_ref[...]))
 
 
@@ -268,9 +270,22 @@
     return top, (x - top.astype(F32)).astype(BF16)
 
 
-def put_sums(msg_ref, e, start, rows):
+def put_sums(msg_ref, e, start, rows, rest):
     msg_ref[e, start : start + BROWS, 0:N] = rows.astype(BF16)
-    msg_ref[e, start : start + BROWS, N:CH] = jnp.zeros((BROWS, CH - N), BF16)
+    msg_ref[e, start : start + BROWS, N:CH] = rest
+
+
+def one(x):
+    return jnp.sum(x, axis=0, keepdims=True)
+
+
+def fold_lanes(x):
+    return jnp.concatenate([x[:, g * WIDTH : (g + 1) * WIDTH] for g in range(4)], axis=0)
+
+
+def unfold_lanes(x):
+    r = x.shape[0] // 4
+    return jnp.concatenate([x[g * r : (g + 1) * r] for g in range(4)], axis=1)
 
 
 def k3_body(
@@ -320,19 +335,11 @@
     small_ref[0:8] = gain_sum
     small_ref[8:16] = shift_sum
     small_ref[16:24] = logit_sum
+    rest = jnp.zeros((BROWS, CH - N), BF16)
     for e in range(GROUP):
         msg_ref[e, 0:BLOCK] = flat_s[e * BLOCK : (e + 1) * BLOCK].astype(BF16)
         rows = [sum_s[h, e * ROWS : (e + 1) * ROWS] for h in range(HEADS)]
-        put_sums(msg_ref, e, BLOCK, jnp.concatenate(rows, axis=0))
-
-
-def k3w_body(nx_ref, joint_ref, mixed_ref, up_ref, out_ref):
-    def put(block, part):
-        part = part.astype(BF16)
-        for e in range(GROUP):
-            out_ref[e, block * SLICE : (block + 1) * SLICE] = part[e * SLICE : (e + 1) * SLICE]
-
-    weight_grads(nx_ref, joint_ref, mixed_ref, up_ref, put)
+        put_sums(msg_ref, e, BLOCK, jnp.concatenate(rows, axis=0), rest)
 
 
 def bias_sum(recv_ref, start, gb_s):
@@ -343,7 +350,7 @@
     for r in range(ROWS):
         for h in range(HEADS):
             gb_s[r * 8 + h : r * 8 + h + 1] = total[h * ROWS + r : h * ROWS + r + 1]
-    return jnp.concatenate(split2(gb_s[...].T[0:N]), axis=1)
+    return jnp.concatenate(split2(gb_s[...].T[0:N]), axis=1), total[:, N:CH]
 
 
 def bias_part(i, gb_s, gb_t, wb_tiled, nx):
@@ -355,12 +362,13 @@
 
 def k4_body(
     recv_ref, cot_ref, q_ref, k_ref, v_ref, gate_ref, part_ref, probs_ref, mixed_ref, nx_ref,
-    nx1_ref, norm1_ref, inv1_ref, gain_ref, wp_ref, wb_ref, wo_ref, wg1_ref,
+    nx1_ref, norm1_ref, inv1_ref, gain_ref, wp_ref, wb_ref, wo_ref,
+    nxw_ref, joint1_ref, mixed1_ref, upw_ref, small1_ref, total1_ref,
     up_ref, gn_ref, msg_ref, small_ref,
     flat_s, la_s, gb_s, sum_s, joint_s, grad_s, upb_s, scores_s,
 ):
     gather_rows(recv_ref, flat_s, la_s)
-    gb_t = bias_sum(recv_ref, BLOCK, gb_s)
+    gb_t, _rest = bias_sum(recv_ref, BLOCK, gb_s)
     wb = w_bias_rows(wb_ref, 1)
     wb_tiled = jnp.concatenate([wb.astype(F32)] * ROWS, axis=0).astype(BF16)
     sum_s[...] = jnp.zeros_like(sum_s)
@@ -388,31 +396,36 @@
     joint_back(probs_ref, scores_s, q_ref, k_ref, grad_s, joint_s)
     for i in range(ROWS):
         gn_ref[i] = dot_nt(joint_s[i * N : (i + 1) * N], wp_ref[0])
-    small_ref[0:8] = gain_sum
-    small_ref[8:16] = shift_sum
-    small_ref[16:24] = bias_w
-    small_ref[24:32] = logit_sum
-    small_ref[32:40] = up_sum
+    small_ref[0:8] = logit_sum
+    small_ref[8:16] = up_sum
+    rows = [
+        one(small1_ref[0:8] + gain_sum), one(small1_ref[8:16] + shift_sum), one(small1_ref[16:24]),
+        one(total1_ref[...]), bias_w[0:HEADS],
+    ]
+    top, low = split2(jnp.concatenate(rows, axis=0))
+    rest = [fold_lanes(top.astype(F32)), fold_lanes(low.astype(F32)[HEADS:8])]
+    rest = jnp.concatenate(rest, axis=0).astype(BF16)
     for h in range(HEADS):
         flat_s[h * N : (h + 1) * N, 0:N] = sum_s[h].T
     for e in range(GROUP):
         rows = [flat_s[h * N + e * ROWS : h * N + (e + 1) * ROWS, 0:N] for h in range(HEADS)]
-        put_sums(msg_ref, e, 2 * WROWS, jnp.concatenate(rows, axis=0))
-        msg_ref[e, WROWS : 2 * WROWS] = wg1_ref[e]
-
-    def put(block, part):
+        put_sums(msg_ref, e, 2 * WROWS, jnp.concatenate(rows, axis=0), rest)
+
+    def put(start, block, part):
         part = part.astype(BF16)
         for e in range(GROUP):
-            msg_ref[e, block * SLICE : (block + 1) * SLICE] = part[e * SLICE : (e + 1) * SLICE]
-
-    weight_grads(nx_ref, joint_s, mixed_ref, upb_s, put)
+            at = start + block * SLICE
+            msg_ref[e, at : at + SLICE] = part[e * SLICE : (e + 1) * SLICE]
+
+    weight_grads(nx_ref, joint_s, mixed_ref, upb_s, functools.partial(put, 0))
+    weight_grads(nxw_ref, joint1_ref, mixed1_ref, upw_ref, functools.partial(put, WROWS))
 
 
 def k5_body(
-    recv_ref, norm_ref, gn_ref, nx_ref, small1_ref, total1_ref, small_ref, wb_ref,
-    full_ref, msg_ref, gb_s,
+    recv_ref, norm_ref, gn_ref, nx_ref, small_ref, wb_ref,
+    full_ref, msg_ref, sums1_ref, gb_s,
 ):
-    gb_t = bias_sum(recv_ref, 2 * WROWS, gb_s)
+    gb_t, rest = bias_sum(recv_ref, 2 * WROWS, gb_s)
     wb = w_bias_rows(wb_ref, 0)
     wb_tiled = jnp.concatenate([wb.astype(F32)] * ROWS, axis=0).astype(BF16)
     zero = jnp.zeros((8, CH), F32)
@@ -429,20 +442,14 @@
         total += recv_ref[d, 0 : 2 * WROWS].astype(F32)
     total *= 1.0 / N
     total = total.astype(BF16)
-
-    def one(x):
-        return jnp.sum(x, axis=0, keepdims=True)
-
-    rows = [
-        one(gain_sum), one(shift_sum), one(small_ref[24:32]), one(small_ref[32:40]), bias_w[0:HEADS],
-        one(small1_ref[0:8] + small_ref[0:8]), one(small1_ref[8:16] + small_ref[8:16]),
-        one(small1_ref[16:24]), one(total1_ref[...]), small_ref[16 : 16 + HEADS],
-    ]
-    top, low = split2(jnp.concatenate(rows, axis=0))
+    sums1_ref[...] = unfold_lanes(rest[0:32])
+    sums1_ref[HEADS:8] += unfold_lanes(rest[32:48])
+    rows = [one(gain_sum), one(shift_sum), one(small_ref[0:8]), one(small_ref[8:16]), bias_w[0:HEADS]]
+    sums = jnp.concatenate([part.astype(F32) for part in split2(jnp.concatenate(rows, axis=0))], axis=0)
+    sums = sums.astype(BF16)
     for e in range(GROUP):
         msg_ref[e, 0 : 2 * WROWS] = total
-        msg_ref[e, 2 * WROWS : 2 * WROWS + 16] = top
-        msg_ref[e, 2 * WROWS + 16 : 2 * WROWS + 32] = low
+        msg_ref[e, 2 * WROWS : 2 * WROWS + 16] = sums
 
 
 def k5b_body(full_ref, norm_ref, inv_ref, up_ref, gain_ref, out_ref):
@@ -452,8 +459,8 @@
         out_ref[i] = (up_ref[i].astype(F32) + back).astype(BF16)
 
 
-def k6_body(recv_ref, gain_ref, shift_ref, proj_ref, wb_ref, gate_ref, ow_ref, ob_ref):
-    small = jnp.zeros((16, CH), F32)
+def k6_body(recv_ref, sums1_ref, gain_ref, shift_ref, proj_ref, wb_ref, gate_ref, ow_ref, ob_ref):
+    small = jnp.zeros((8, CH), F32)
     for d in range(GROUP):
         for m in range(2):
             for block in range(4):
@@ -464,8 +471,9 @@
             at = m * WROWS + 4 * SLICE
             ow_ref[m, d * SLICE : (d + 1) * SLICE] = recv_ref[d, at : at + SLICE].astype(F32)
         at = 2 * WROWS
-        small += recv_ref[d, at : at + 16].astype(F32) + recv_ref[d, at + 16 : at + 32].astype(F32)
-    small = small * (1.0 / N)
+        both = recv_ref[d, at : at + 16].astype(F32)
+        small += both[0:8] + both[8:16]
+    small = jnp.concatenate([small, sums1_ref[...]], axis=0) * (1.0 / N)
     for m in range(2):
         at = m * 8
         gain_ref[m : m + 1] = small[at : at + 1]
@@ -555,22 +563,22 @@
         "second_module",
     )(recv1, mask, gm1, ln_gain, ln_shift, w_proj, gate_bias)
     recv2 = swap(msg2)
-    (wg1,) = call(k3w_body, [((GROUP, WROWS, CH), BF16)], [], "second_weights")(
-        after(nxw, recv2), joint1, mixed1, up1
-    )
     up, gn, msg3, small = call(
         k4_body,
-        [rows_b, rows_f, ((GROUP, 2 * WROWS + BROWS, CH), BF16), ((40, CH), F32)],
+        [rows_b, rows_f, ((GROUP, 2 * WROWS + BROWS, CH), BF16), ((16, CH), F32)],
         [flat_f, rows_f, bias_8, mats, joint_b, rows_b, flat_b, ((ROWS, HEADS, N, N), BF16)],
         "back_first",
     )(
         recv2, cotangent, q, k, v, gate, part0, probs0, mixed0, nx0, nx1, norm1, inv1,
-        ln_gain, w_proj, w_bias, w_out, wg1,
+        ln_gain, w_proj, w_bias, w_out, nxw, joint1, mixed1, up1, small1, total1,
     )
     recv3 = swap(msg3)
-    full, msg4 = call(
-        k5_body, [rows_f, ((GROUP, 2 * WROWS + 32, CH), BF16)], [bias_8], "grad_sums"
-    )(recv3, norm0, gn, nx0, small1, total1, small, w_bias)
+    full, msg4, sums1 = call(
+        k5_body,
+        [rows_f, ((GROUP, 2 * WROWS + 16, CH), BF16), ((8, CH), F32)],
+        [bias_8],
+        "grad_sums",
+    )(recv3, norm0, gn, nx0, small, w_bias)
     recv4 = swap(msg4)
     (grad_pair,) = call(k5b_body, [rows_b], [], "grad_pair")(after(full, recv4), norm0, inv0, up, ln_gain)
     grad_gain, grad_shift, grad_proj, grad_bias_w, grad_gate, grad_out_w, grad_out_bias = call(
@@ -581,7 +589,7 @@
         ],
         [],
         "weight_sums",
-    )(recv4)
+    )(recv4, sums1)
     return (
         grad_pair, grad_gain, grad_shift, grad_proj, jnp.swapaxes(grad_bias_w, 1, 2), grad_gate,
         grad_out_w, grad_out_bias,

time: 97.3 us -> 96.3 us (0.990)
    pallas_call x10 -> x9, Pallas kernels: 17.3 us -> 16.9 us  [run(): pl.pallas_call(body, in_specs=[far_spec if n in far else near_spec for n...]
where the time goes in v5:
time: 96.3 us; the launch traced here: 95.9 us
  blocking collectives  60.1 us (62%)
  Pallas kernels  16.9 us (18%)
  starting transfers between devices  7.41 us (8%)
  waiting for transfers between devices  5.85 us (6%)
  local copies, waits for them, and re-layouts  4.83 us (5%)
    all_to_all x4, blocking collectives, swap(): return lax.all_to_all(x, 'dap', 0, 0, tiled=True)  60.1 us
    pallas_call x9, Pallas kernels, run(): pl.pallas_call(body, in_specs=[far_spec if n in far else near_spec for n...  16.9 us
    all_to_all x1, starting transfers between devices, swap(): return lax.all_to_all(x, 'dap', 0, 0, tiled=True)  7.41 us
    all_to_all x1, waiting for transfers between devices, swap(): return lax.all_to_all(x, 'dap', 0, 0, tiled=True)  5.85 us
    unnamed x34, local copies, waits for them, and re-layouts  4.83 us
  transfers between devices with their start and end apart: 1, of which 1 were waited for; matrix products, arithmetic and copies ran while one was open for 0% of the time, Pallas kernels for 1%

profile of v5, /device:TPU:1, one launch (start us, length us, event | category | flops | bytes accessed | tf_op | source)
XLA Modules:
  0.0 95.9 jit_solution(6493023184277720016)
XLA Ops:
  0.6 0.0 copy-start.10
  0.6 0.0 copy-start.12
  0.7 0.0 copy-start.1
  0.7 0.0 copy-start.8
  0.7 0.0 copy-start.7
  0.7 0.0 copy-start.14
  0.7 0.0 copy-start.13
  0.7 2.5 %norm_first.1 = bf16[8,192,128]{2,1,0:T(8,128)(2,1)} custom-call(bf16[12,96,128]{2,1,0:T(8,128)(2,1)} %x_ref.3, bf16[12,96,128]{2,1,0:T(8,128)(2,1)} %cot_ref.1, f32[2,128]{1,0:T(2,128)} %gain_ref.9, f32[2,128]{1,0:T(2,128)} %shift_ref.5, bf16[2,4,128]{2,1,0:T(4,128)(2,1)} %bitcast.3), custom_call_target="tpu_custom_call" | custom-call | flops 100000000 | bytes 2000000 | tf_op jit(solution)/shard_map/norm_first/pallas_call | solution.py:494
  3.2 7.4 %all-to-all-start = ((bf16[8,192,128]{2,1,0:T(8,128)(2,1)}), bf16[8,192,128]{2,1,0:T(8,128)(2,1)S(1)}, u32[]{:S(2)}, u32[]{:S(2)}) async-start(bf16[8,192,128]{2,1,0:T(8,128)(2,1)} %norm_first.1), calls=%async_computation | async-start | bytes 786432 | tf_op jit(solution)/shard_map/all_to_all | solution.py:513
  10.6 1.0 %copy-done = bf16[12,96,128]{2,1,0:T(8,128)(2,1)S(1)} copy-done((bf16[12,96,128]{2,1,0:T(8,128)(2,1)S(1)}, bf16[12,96,128]{2,1,0:T(8,128)(2,1)}, u32[]{:S(2)}) %copy-start) | copy-done | bytes 294936
  11.6 0.9 copy-done.3
  12.5 0.7 copy-done.9
  13.2 0.7 copy-done.11
  13.9 0.7 copy-done.15
  14.6 1.0 %project_first.1 = (bf16[12,96,128]{2,1,0:T(8,128)(2,1)S(1)}, bf16[12,96,128]{2,1,0:T(8,128)(2,1)S(1)}, bf16[12,96,128]{2,1,0:T(8,128)(2,1)S(1)}, f32[12,96,128]...) custom-call(bf16[12,96,128]{2,1,0:T(8,128)(2,1)S(1)} %copy-done, ...), custom_call_target="tpu_custom_call" | custom-call | flops 100000000 | bytes 2000000 | tf_op jit(solution)/shard_map/project_first/pallas_call | solution.py:494
  15.6 0.0 copy-start.5
  15.6 0.8 copy-done.5
  16.5 5.8 %all-to-all-done.recv_ref = bf16[8,192,128]{2,1,0:T(8,128)(2,1)S(1)} async-done(((bf16[8,192,128]{2,1,0:T(8,128)(2,1)}), bf16[8,192,128]{2,1,0:T(8,128)(2,1)S(1)}, u32[]{:S(2)}, u32[]{:S(2)}) %all-to-all-start) | async-done | bytes 393248 | tf_op jit(solution)/shard_map/all_to_all | solution.py:513
  22.3 0.0 copy-done.10
  22.3 0.0 copy-done.1
  22.4 2.0 %attend_first.1 = (f32[12,96,128]{2,1,0:T(8,128)S(1)}, bf16[1152,128]{1,0:T(8,128)(2,1)S(1)}, f32[12,4,96,96]{3,2,1,0:T(8,128)S(1)}, bf16[12,96,128]{2,1,0:T(8,1...) custom-call(bf16[12,96,128]{2,1,0:T(8,128)(2,1)S(1)} %copy-done.1, ...), custom_call_target="tpu_custom_call" | custom-call | flops 100000000 | bytes 2000000 | tf_op jit(solution)/shard_map/attend_first/pallas_call | solution.py:494
  24.4 15.1 %all_to_all.25.recv_ref = bf16[8,192,128]{2,1,0:T(8,128)(2,1)S(1)} all-to-all(bf16[8,192,128]{2,1,0:T(8,128)(2,1)S(1)} %get-tuple-element.50), channel_id=1, replica_groups=mesh['dap'=8,'dp'=32] {'dap'}, dimensions={0} | all-to-all | bytes 786432 | tf_op jit(solution)/shard_map/all_to_all | solution.py:513
  39.4 0.4 cotangent_rows.1
  39.9 4.5 %second_module.1 = (bf16[8,192,128]{2,1,0:T(8,128)(2,1)S(1)}, f32[24,128]{1,0:T(8,128)S(1)}, bf16[1152,128]{1,0:T(8,128)(2,1)S(1)}, bf16[1152,512]{1,0:T(8,128)(2,1)S(1)}, bf16[1152,128]{1,0:T(8,128)(2,1)S(1)}) custom-call(bf16[8,192,128]{2,1,0:T(8,128)(2,1)S(1)} %all_to_all.25.recv_ref, s32[1,96]{1,0:T(1,128)S(1)} %bitcast.8, ...), custom_call_target="tpu_custom_call" | custom-call | flops 100000000 | bytes 2000000 | tf_op jit(solution)/shard_map/second_module/pallas_call | solution.py:494
  44.4 14.9 %all_to_all.26.recv_ref = bf16[8,192,128]{2,1,0:T(8,128)(2,1)S(1)} all-to-all(bf16[8,192,128]{2,1,0:T(8,128)(2,1)S(1)} %get-tuple-element.53), channel_id=1, replica_groups=mesh['dap'=8,'dp'=32] {'dap'}, dimensions={0} | all-to-all | bytes 786432 | tf_op jit(solution)/shard_map/all_to_all | solution.py:513
  59.4 0.0 copy-done.2
  59.4 3.8 %back_first.1 = (bf16[12,96,128]{2,1,0:T(8,128)(2,1)S(1)}, f32[12,96,128]{2,1,0:T(8,128)S(1)}, bf16[8,208,128]{2,1,0:T(8,128)(2,1)S(1)}, f32[16,128]{1,0:T(8,128)S(1)}) custom-call(bf16[8,192,128]{2,1,0:T(8,128)(2,1)S(1)} %all_to_all.26.recv_ref, bf16[12,96,128]{2,1,0:T(8,128)(2,1)S(1)} %copy-done.2, bf16[12,96,128]{2,1,0:T(8,128)(2,1)S(1)} %get-tuple-element.46.q_ref, ...), custom_call_target="tpu_custom_call" | custom-call | flops 100000000 | bytes 2000000 | tf_op jit(solution)/shard_map/back_first/pallas_call | solution.py:494
  63.2 15.7 %all_to_all.27.recv_ref = bf16[8,208,128]{2,1,0:T(8,128)(2,1)S(1)} all-to-all(bf16[8,208,128]{2,1,0:T(8,128)(2,1)S(1)} %get-tuple-element.67), channel_id=1, replica_groups=mesh['dap'=8,'dp'=32] {'dap'}, dimensions={0} | all-to-all | bytes 851968 | tf_op jit(solution)/shard_map/all_to_all | solution.py:513
  78.9 0.6 grad_sums.1
  79.5 14.3 %all_to_all.28.recv_ref = bf16[8,176,128]{2,1,0:T(8,128)(2,1)S(1)} all-to-all(bf16[8,176,128]{2,1,0:T(8,128)(2,1)S(1)} %get-tuple-element.72), channel_id=1, replica_groups=mesh['dap'=8,'dp'=32] {'dap'}, dimensions={0} | all-to-all | bytes 720896 | tf_op jit(solution)/shard_map/all_to_all | solution.py:513
  93.9 1.1 %grad_pair.1 = bf16[12,96,128]{2,1,0:T(8,128)(2,1)} custom-call(f32[12,96,128]{2,1,0:T(8,128)S(1)} %get-tuple-element.73.full_ref, f32[12,96,128]{2,1,0:T(8,128)S(1)} %get-tuple-element.68.norm_ref, f32[12,96,128]{2,1,0:T(8,128)S(1)} %copy-done.6, bf16[12,96,128]{2,1,0:T(8,128)(2,1)S(1)} %get-tuple-element.75.up_ref, f32[2,128]{1,0:T(2,128)S(1)} %copy-done.10), custom_call_target="tpu_custom_call" | custom-call | flops 100000000 | bytes 2000000 | tf_op jit(solution)/shard_map/grad_pair/pallas_call | solution.py:494
  95.0 0.9 weight_sums.1
  (17 shorter events, 0.0 us)
Async XLA Ops:
  0.6 21.7 %copy-start.10 = (f32[2,128]{1,0:T(2,128)S(1)}, f32[2,128]{1,0:T(2,128)}, u32[]{:S(2)}) copy-start(f32[2,128]{1,0:T(2,128)} %gain_ref.9) | copy-start | bytes 3076
  0.6 21.7 %copy-start.12 = (f32[2,128]{1,0:T(2,128)S(1)}, f32[2,128]{1,0:T(2,128)}, u32[]{:S(2)}) copy-start(f32[2,128]{1,0:T(2,128)} %shift_ref.5) | copy-start | bytes 3076
  0.7 21.7 %copy-start.1 = (bf16[12,96,128]{2,1,0:T(8,128)(2,1)S(1)}, bf16[12,96,128]{2,1,0:T(8,128)(2,1)}, u32[]{:S(2)}) copy-start(bf16[12,96,128]{2,1,0:T(8,128)(2,1)} %x_ref.3) | copy-start | bytes 884740
  0.7 21.6 %copy-start.8 = (bf16[2,128,4]{1,2,0:T(4,128)(2,1)S(1)}, bf16[2,128,4]{1,2,0:T(4,128)(2,1)}, u32[]{:S(2)}) copy-start(bf16[2,128,4]{1,2,0:T(4,128)(2,1)} %param.16) | copy-start | bytes 6148
  0.7 21.6 %copy-start.7 = (bf16[2,128,128]{2,1,0:T(8,128)(2,1)S(1)}, bf16[2,128,128]{2,1,0:T(8,128)(2,1)}, u32[]{:S(2)}) copy-start(bf16[2,128,128]{2,1,0:T(8,128)(2,1)} %wo_ref.5) | copy-start | bytes 196612
  0.7 21.6 %copy-start.14 = (f32[2,128]{1,0:T(2,128)S(1)}, f32[2,128]{1,0:T(2,128)}, u32[]{:S(2)}) copy-start(f32[2,128]{1,0:T(2,128)} %ob_ref.1) | copy-start | bytes 3076
  0.7 21.6 %copy-start.13 = (s32[96]{0:T(128)S(1)}, s32[96]{0:T(128)}, u32[]{:S(2)}) copy-start(s32[96]{0:T(128)} %param.12) | copy-start | bytes 1156
  3.2 19.1 %all-to-all-start = ((bf16[8,192,128]{2,1,0:T(8,128)(2,1)}), bf16[8,192,128]{2,1,0:T(8,128)(2,1)S(1)}, u32[]{:S(2)}, u32[]{:S(2)}) async-start(bf16[8,192,128]{2,1,0:T(8,128)(2,1)} %norm_first.1), calls=%async_computation | async-start | bytes 786432 | tf_op jit(solution)/shard_map/all_to_all | solution.py:513
  10.6 1.0 %copy-start = (bf16[12,96,128]{2,1,0:T(8,128)(2,1)S(1)}, bf16[12,96,128]{2,1,0:T(8,128)(2,1)}, u32[]{:S(2)}) copy-start(bf16[12,96,128]{2,1,0:T(8,128)(2,1)} %x_ref.3) | copy-start | bytes 884740
  11.6 0.9 copy-start.3
  12.5 0.7 copy-start.9
  13.2 0.7 copy-start.11
  13.9 0.7 copy-start.15
  14.6 25.3 %copy-start.4 = (bf16[2,128,512]{2,1,0:T(8,128)(2,1)S(1)}, bf16[2,128,512]{2,1,0:T(8,128)(2,1)}, u32[]{:S(2)}) copy-start(bf16[2,128,512]{2,1,0:T(8,128)(2,1)} %wp_ref.5) | copy-start | bytes 786436
  14.6 25.3 %copy-start.16 = (f32[2,128]{1,0:T(2,128)S(1)}, f32[2,128]{1,0:T(2,128)}, u32[]{:S(2)}) copy-start(f32[2,128]{1,0:T(2,128)} %gb_ref.3) | copy-start | bytes 3076
  15.6 0.8 copy-start.5
  24.4 35.0 %copy-start.2 = (bf16[12,96,128]{2,1,0:T(8,128)(2,1)S(1)}, bf16[12,96,128]{2,1,0:T(8,128)(2,1)}, u32[]{:S(2)}) copy-start(bf16[12,96,128]{2,1,0:T(8,128)(2,1)} %cot_ref.1) | copy-start | bytes 884740
  63.2 30.7 %copy-start.6 = (f32[12,96,128]{2,1,0:T(8,128)S(1)}, f32[12,96,128]{2,1,0:T(8,128)}, u32[]{:S(2)}) copy-start(f32[12,96,128]{2,1,0:T(8,128)} %copy-done.5) | copy-start | bytes 1769476

commit v6 on v5

--- a/solution.py
+++ b/solution.py
@@ -459,7 +459,11 @@
         out_ref[i] = (up_ref[i].astype(F32) + back).astype(BF16)
 
 
-def k6_body(recv_ref, sums1_ref, gain_ref, shift_ref, proj_ref, wb_ref, gate_ref, ow_ref, ob_ref):
+def k6_body(
+    recv_ref, sums1_ref, full_ref, norm_ref, inv_ref, up_ref, ln_gain_ref,
+    out_ref, gain_ref, shift_ref, proj_ref, wb_ref, gate_ref, ow_ref, ob_ref,
+):
+    k5b_body(full_ref, norm_ref, inv_ref, up_ref, ln_gain_ref, out_ref)
     small = jnp.zeros((8, CH), F32)
     for d in range(GROUP):
         for m in range(2):
@@ -580,16 +584,15 @@
         "grad_sums",
     )(recv3, norm0, gn, nx0, small, w_bias)
     recv4 = swap(msg4)
-    (grad_pair,) = call(k5b_body, [rows_b], [], "grad_pair")(after(full, recv4), norm0, inv0, up, ln_gain)
-    grad_gain, grad_shift, grad_proj, grad_bias_w, grad_gate, grad_out_w, grad_out_bias = call(
+    grad_pair, grad_gain, grad_shift, grad_proj, grad_bias_w, grad_gate, grad_out_w, grad_out_bias = call(
         k6_body,
         [
-            ((2, CH), F32), ((2, CH), F32), ((2, CH, 4 * CH), F32), ((2, HEADS, CH), F32),
+            rows_b, ((2, CH), F32), ((2, CH), F32), ((2, CH, 4 * CH), F32), ((2, HEADS, CH), F32),
             ((2, CH), F32), ((2, CH, CH), F32), ((2, CH), F32),
         ],
         [],
         "weight_sums",
-    )(recv4, sums1)
+    )(recv4, sums1, full, norm0, inv0, up, ln_gain)
     return (
         grad_pair, grad_gain, grad_shift, grad_proj, jnp.swapaxes(grad_bias_w, 1, 2), grad_gate,
         grad_out_w, grad_out_bias,

time: 96.3 us -> 95.6 us (level)
    pallas_call x9 -> x8, Pallas kernels: 16.9 us -> 16.2 us  [run(): pl.pallas_call(body, in_specs=[far_spec if n in far else near_spec for n...]
where the time goes in v6:
time: 95.6 us; the launch traced here: 95.2 us
  blocking collectives  60.1 us (63%)
  Pallas kernels  16.2 us (17%)
  starting transfers between devices  7.41 us (8%)
  waiting for transfers between devices  5.85 us (6%)
  local copies, waits for them, and re-layouts  4.83 us (5%)
    all_to_all x4, blocking collectives, swap(): return lax.all_to_all(x, 'dap', 0, 0, tiled=True)  60.1 us
    pallas_call x8, Pallas kernels, run(): pl.pallas_call(body, in_specs=[far_spec if n in far else near_spec for n...  16.2 us
    all_to_all x1, starting transfers between devices, swap(): return lax.all_to_all(x, 'dap', 0, 0, tiled=True)  7.41 us
    all_to_all x1, waiting for transfers between devices, swap(): return lax.all_to_all(x, 'dap', 0, 0, tiled=True)  5.85 us
    unnamed x34, local copies, waits for them, and re-layouts  4.83 us
  transfers between devices with their start and end apart: 1, of which 1 were waited for; matrix products, arithmetic and copies ran while one was open for 0% of the time, Pallas kernels for 1%

profile of v6, /device:TPU:1, one launch (start us, length us, event | category | flops | bytes accessed | tf_op | source)
XLA Modules:
  0.0 95.2 jit_solution(16364211987158359550)
XLA Ops:
  0.6 0.0 copy-start.10
  0.6 0.0 copy-start.12
  0.7 0.0 copy-start.1
  0.7 0.0 copy-start.8
  0.7 0.0 copy-start.7
  0.7 0.0 copy-start.14
  0.7 0.0 copy-start.13
  0.7 2.5 %norm_first.1 = bf16[8,192,128]{2,1,0:T(8,128)(2,1)} custom-call(bf16[12,96,128]{2,1,0:T(8,128)(2,1)} %x_ref.3, bf16[12,96,128]{2,1,0:T(8,128)(2,1)} %cot_ref.1, f32[2,128]{1,0:T(2,128)} %ln_gain_ref.1, f32[2,128]{1,0:T(2,128)} %shift_ref.5, bf16[2,4,128]{2,1,0:T(4,128)(2,1)} %bitcast.3), custom_call_target="tpu_custom_call" | custom-call | flops 100000000 | bytes 2000000 | tf_op jit(solution)/shard_map/norm_first/pallas_call | solution.py:498
  3.2 7.4 %all-to-all-start = ((bf16[8,192,128]{2,1,0:T(8,128)(2,1)}), bf16[8,192,128]{2,1,0:T(8,128)(2,1)S(1)}, u32[]{:S(2)}, u32[]{:S(2)}) async-start(bf16[8,192,128]{2,1,0:T(8,128)(2,1)} %norm_first.1), calls=%async_computation | async-start | bytes 786432 | tf_op jit(solution)/shard_map/all_to_all | solution.py:517
  10.6 1.0 %copy-done = bf16[12,96,128]{2,1,0:T(8,128)(2,1)S(1)} copy-done((bf16[12,96,128]{2,1,0:T(8,128)(2,1)S(1)}, bf16[12,96,128]{2,1,0:T(8,128)(2,1)}, u32[]{:S(2)}) %copy-start) | copy-done | bytes 294936
  11.6 0.9 copy-done.3
  12.5 0.7 copy-done.9
  13.2 0.7 copy-done.11
  13.9 0.7 copy-done.15
  14.6 1.0 %project_first.1 = (bf16[12,96,128]{2,1,0:T(8,128)(2,1)S(1)}, bf16[12,96,128]{2,1,0:T(8,128)(2,1)S(1)}, bf16[12,96,128]{2,1,0:T(8,128)(2,1)S(1)}, f32[12,96,128]...) custom-call(bf16[12,96,128]{2,1,0:T(8,128)(2,1)S(1)} %copy-done, ...), custom_call_target="tpu_custom_call" | custom-call | flops 100000000 | bytes 2000000 | tf_op jit(solution)/shard_map/project_first/pallas_call | solution.py:498
  15.6 0.0 copy-start.5
  15.6 0.8 copy-done.5
  16.5 5.8 %all-to-all-done.recv_ref = bf16[8,192,128]{2,1,0:T(8,128)(2,1)S(1)} async-done(((bf16[8,192,128]{2,1,0:T(8,128)(2,1)}), bf16[8,192,128]{2,1,0:T(8,128)(2,1)S(1)}, u32[]{:S(2)}, u32[]{:S(2)}) %all-to-all-start) | async-done | bytes 393248 | tf_op jit(solution)/shard_map/all_to_all | solution.py:517
  22.3 0.0 copy-done.10
  22.3 0.0 copy-done.12
  22.3 0.0 copy-done.1
  22.3 0.0 copy-done.8
  22.4 2.0 %attend_first.1 = (f32[12,96,128]{2,1,0:T(8,128)S(1)}, bf16[1152,128]{1,0:T(8,128)(2,1)S(1)}, f32[12,4,96,96]{3,2,1,0:T(8,128)S(1)}, bf16[12,96,128]{2,1,0:T(8,1...) custom-call(bf16[12,96,128]{2,1,0:T(8,128)(2,1)S(1)} %copy-done.1, ...), custom_call_target="tpu_custom_call" | custom-call | flops 100000000 | bytes 2000000 | tf_op jit(solution)/shard_map/attend_first/pallas_call | solution.py:498
  24.4 15.1 %all_to_all.25.recv_ref = bf16[8,192,128]{2,1,0:T(8,128)(2,1)S(1)} all-to-all(bf16[8,192,128]{2,1,0:T(8,128)(2,1)S(1)} %get-tuple-element.50), channel_id=1, replica_groups=mesh['dap'=8,'dp'=32] {'dap'}, dimensions={0} | all-to-all | bytes 786432 | tf_op jit(solution)/shard_map/all_to_all | solution.py:517
  39.4 0.4 cotangent_rows.1
  39.9 4.5 %second_module.1 = (bf16[8,192,128]{2,1,0:T(8,128)(2,1)S(1)}, f32[24,128]{1,0:T(8,128)S(1)}, bf16[1152,128]{1,0:T(8,128)(2,1)S(1)}, bf16[1152,512]{1,0:T(8,128)(2,1)S(1)}, bf16[1152,128]{1,0:T(8,128)(2,1)S(1)}) custom-call(bf16[8,192,128]{2,1,0:T(8,128)(2,1)S(1)} %all_to_all.25.recv_ref, s32[1,96]{1,0:T(1,128)S(1)} %bitcast.8, ...), custom_call_target="tpu_custom_call" | custom-call | flops 100000000 | bytes 2000000 | tf_op jit(solution)/shard_map/second_module/pallas_call | solution.py:498
  44.4 14.9 %all_to_all.26.recv_ref = bf16[8,192,128]{2,1,0:T(8,128)(2,1)S(1)} all-to-all(bf16[8,192,128]{2,1,0:T(8,128)(2,1)S(1)} %get-tuple-element.53), channel_id=1, replica_groups=mesh['dap'=8,'dp'=32] {'dap'}, dimensions={0} | all-to-all | bytes 786432 | tf_op jit(solution)/shard_map/all_to_all | solution.py:517
  59.4 3.8 %back_first.1 = (bf16[12,96,128]{2,1,0:T(8,128)(2,1)S(1)}, f32[12,96,128]{2,1,0:T(8,128)S(1)}, bf16[8,208,128]{2,1,0:T(8,128)(2,1)S(1)}, f32[16,128]{1,0:T(8,128)S(1)}) custom-call(bf16[8,192,128]{2,1,0:T(8,128)(2,1)S(1)} %all_to_all.26.recv_ref, bf16[12,96,128]{2,1,0:T(8,128)(2,1)S(1)} %copy-done.2, bf16[12,96,128]{2,1,0:T(8,128)(2,1)S(1)} %get-tuple-element.46.q_ref, ...), custom_call_target="tpu_custom_call" | custom-call | flops 100000000 | bytes 2000000 | tf_op jit(solution)/shard_map/back_first/pallas_call | solution.py:498
  63.2 15.7 %all_to_all.27.recv_ref = bf16[8,208,128]{2,1,0:T(8,128)(2,1)S(1)} all-to-all(bf16[8,208,128]{2,1,0:T(8,128)(2,1)S(1)} %get-tuple-element.67), channel_id=1, replica_groups=mesh['dap'=8,'dp'=32] {'dap'}, dimensions={0} | all-to-all | bytes 851968 | tf_op jit(solution)/shard_map/all_to_all | solution.py:517
  78.9 0.6 grad_sums.1
  79.5 14.3 %all_to_all.28.recv_ref = bf16[8,176,128]{2,1,0:T(8,128)(2,1)S(1)} all-to-all(bf16[8,176,128]{2,1,0:T(8,128)(2,1)S(1)} %get-tuple-element.71), channel_id=1, replica_groups=mesh['dap'=8,'dp'=32] {'dap'}, dimensions={0} | all-to-all | bytes 720896 | tf_op jit(solution)/shard_map/all_to_all | solution.py:517
  93.8 1.3 %weight_sums.1 = (bf16[12,96,128]{2,1,0:T(8,128)(2,1)}, f32[2,128]{1,0:T(2,128)}, f32[2,128]{1,0:T(2,128)}, f32[2,128,512]{2,1,0:T(8,128)}, f32[2,4,128]{2,1,0:T...) custom-call(bf16[8,176,128]{2,1,0:T(8,128)(2,1)S(1)} %all_to_all.28.recv_ref, ...), custom_call_target="tpu_custom_call" | custom-call | flops 100000000 | bytes 2000000 | tf_op jit(solution)/shard_map/weight_sums/pallas_call | solution.py:498
  (16 shorter events, 0.0 us)
Async XLA Ops:
  0.6 21.7 %copy-start.10 = (f32[2,128]{1,0:T(2,128)S(1)}, f32[2,128]{1,0:T(2,128)}, u32[]{:S(2)}) copy-start(f32[2,128]{1,0:T(2,128)} %ln_gain_ref.1) | copy-start | bytes 3076
  0.6 21.7 %copy-start.12 = (f32[2,128]{1,0:T(2,128)S(1)}, f32[2,128]{1,0:T(2,128)}, u32[]{:S(2)}) copy-start(f32[2,128]{1,0:T(2,128)} %shift_ref.5) | copy-start | bytes 3076
  0.7 21.7 %copy-start.1 = (bf16[12,96,128]{2,1,0:T(8,128)(2,1)S(1)}, bf16[12,96,128]{2,1,0:T(8,128)(2,1)}, u32[]{:S(2)}) copy-start(bf16[12,96,128]{2,1,0:T(8,128)(2,1)} %x_ref.3) | copy-start | bytes 884740
  0.7 21.6 %copy-start.8 = (bf16[2,128,4]{1,2,0:T(4,128)(2,1)S(1)}, bf16[2,128,4]{1,2,0:T(4,128)(2,1)}, u32[]{:S(2)}) copy-start(bf16[2,128,4]{1,2,0:T(4,128)(2,1)} %param.16) | copy-start | bytes 6148
  0.7 21.6 %copy-start.7 = (bf16[2,128,128]{2,1,0:T(8,128)(2,1)S(1)}, bf16[2,128,128]{2,1,0:T(8,128)(2,1)}, u32[]{:S(2)}) copy-start(bf16[2,128,128]{2,1,0:T(8,128)(2,1)} %wo_ref.5) | copy-start | bytes 196612
  0.7 21.6 %copy-start.14 = (f32[2,128]{1,0:T(2,128)S(1)}, f32[2,128]{1,0:T(2,128)}, u32[]{:S(2)}) copy-start(f32[2,128]{1,0:T(2,128)} %ob_ref.1) | copy-start | bytes 3076
  0.7 21.6 %copy-start.13 = (s32[96]{0:T(128)S(1)}, s32[96]{0:T(128)}, u32[]{:S(2)}) copy-start(s32[96]{0:T(128)} %param.12) | copy-start | bytes 1156
  3.2 19.1 %all-to-all-start = ((bf16[8,192,128]{2,1,0:T(8,128)(2,1)}), bf16[8,192,128]{2,1,0:T(8,128)(2,1)S(1)}, u32[]{:S(2)}, u32[]{:S(2)}) async-start(bf16[8,192,128]{2,1,0:T(8,128)(2,1)} %norm_first.1), calls=%async_computation | async-start | bytes 786432 | tf_op jit(solution)/shard_map/all_to_all | solution.py:517
  10.6 1.0 %copy-start = (bf16[12,96,128]{2,1,0:T(8,128)(2,1)S(1)}, bf16[12,96,128]{2,1,0:T(8,128)(2,1)}, u32[]{:S(2)}) copy-start(bf16[12,96,128]{2,1,0:T(8,128)(2,1)} %x_ref.3) | copy-start | bytes 884740
  11.6 0.9 copy-start.3
  12.5 0.7 copy-start.9
  13.2 0.7 copy-start.11
  13.9 0.7 copy-start.15
  14.6 25.3 %copy-start.4 = (bf16[2,128,512]{2,1,0:T(8,128)(2,1)S(1)}, bf16[2,128,512]{2,1,0:T(8,128)(2,1)}, u32[]{:S(2)}) copy-start(bf16[2,128,512]{2,1,0:T(8,128)(2,1)} %wp_ref.5) | copy-start | bytes 786436
  14.6 25.3 %copy-start.16 = (f32[2,128]{1,0:T(2,128)S(1)}, f32[2,128]{1,0:T(2,128)}, u32[]{:S(2)}) copy-start(f32[2,128]{1,0:T(2,128)} %gb_ref.3) | copy-start | bytes 3076
  15.6 0.8 copy-start.5
  24.4 35.0 %copy-start.2 = (bf16[12,96,128]{2,1,0:T(8,128)(2,1)S(1)}, bf16[12,96,128]{2,1,0:T(8,128)(2,1)}, u32[]{:S(2)}) copy-start(bf16[12,96,128]{2,1,0:T(8,128)(2,1)} %cot_ref.1) | copy-start | bytes 884740
  63.2 30.7 %copy-start.6 = (f32[12,96,128]{2,1,0:T(8,128)S(1)}, f32[12,96,128]{2,1,0:T(8,128)}, u32[]{:S(2)}) copy-start(f32[12,96,128]{2,1,0:T(8,128)} %copy-done.5) | copy-start | bytes 1769476

commit v7 on v6

--- a/solution.py
+++ b/solution.py
@@ -289,10 +289,11 @@
 
 
 def k3_body(
-    recv_ref, mask_ref, gm_ref, gain_ref, shift_ref, wp_ref, gb_ref,
-    msg_ref, small_ref, nx_ref, joint_ref, mixed_ref,
-    flat_s, x_s, raw_s, bias_s, sum_s, norm_s, inv_s, q_s, k_s, v_s, gate_s, att_s, probs_s, grad_s, scores_s,
-):
+    recv_ref, recv0_ref, mask_ref, wo_ref, gain_ref, shift_ref, wp_ref, gb_ref,
+    msg_ref, small_ref, nx_ref, joint_ref, mixed_ref, up_ref, total_ref,
+    flat_s, x_s, raw_s, bias_s, sum_s, norm_s, inv_s, q_s, k_s, v_s, gate_s, att_s, probs_s, grad_s, scores_s, gm_ref,
+):
+    k2b_body(recv0_ref, wo_ref, up_ref, gm_ref, total_ref, flat_s, x_s)
     key = key_column(mask_ref)
     for d in range(GROUP):
         raw_s[d * BROWS : (d + 1) * BROWS] = recv_ref[d, BLOCK:PACK].astype(F32)
@@ -556,16 +557,13 @@
         "attend_first",
     )(pair_rep, q, k, v, gate, recv0, mask, w_out, out_bias, ln_gain, ln_shift, w_bias)
     recv1 = swap(msg1)
-    up1, gm1, total1 = call(
-        k2b_body, [flat_b, rows_f, ((8, CH), F32)], [flat_f, rows_f], "cotangent_rows"
-    )(after(recv0, recv1), w_out)
-    msg2, small1, nxw, joint1, mixed1 = call(
+    msg2, small1, nxw, joint1, mixed1, up1, total1 = call(
         k3_body,
-        [pack, ((24, CH), F32), flat_b, joint_b, flat_b],
+        [pack, ((24, CH), F32), flat_b, joint_b, flat_b, flat_b, ((8, CH), F32)],
         [flat_f, rows_f, raw, mats, mats, rows_f, rows_f]
-        + [rows_b, rows_b, rows_b, rows_f, rows_f, probs, rows_b, ((ROWS, HEADS, N, N), BF16)],
+        + [rows_b, rows_b, rows_b, rows_f, rows_f, probs, rows_b, ((ROWS, HEADS, N, N), BF16), rows_f],
         "second_module",
-    )(recv1, mask, gm1, ln_gain, ln_shift, w_proj, gate_bias)
+    )(recv1, recv0, mask, w_out, ln_gain, ln_shift, w_proj, gate_bias)
     recv2 = swap(msg2)
     up, gn, msg3, small = call(
         k4_body,

time: 95.6 us -> 95.3 us (level)
    pallas_call x8 -> x7, Pallas kernels: 16.2 us -> 15.9 us  [run(): pl.pallas_call(body, in_specs=[far_spec if n in far else near_spec for n...]
where the time goes in v7:
time: 95.3 us; the launch traced here: 94.9 us
  blocking collectives  59.9 us (63%)
  Pallas kernels  15.9 us (17%)
  starting transfers between devices  7.54 us (8%)
  waiting for transfers between devices  5.87 us (6%)
  local copies, waits for them, and re-layouts  4.83 us (5%)
    all_to_all x4, blocking collectives, swap(): return lax.all_to_all(x, 'dap', 0, 0, tiled=True)  59.9 us
    pallas_call x7, Pallas kernels, run(): pl.pallas_call(body, in_specs=[far_spec if n in far else near_spec for n...  15.9 us
    all_to_all x1, starting transfers between devices, swap(): return lax.all_to_all(x, 'dap', 0, 0, tiled=True)  7.54 us
    all_to_all x1, waiting for transfers between devices, swap(): return lax.all_to_all(x, 'dap', 0, 0, tiled=True)  5.87 us
    unnamed x34, local copies, waits for them, and re-layouts  4.83 us
  transfers between devices with their start and end apart: 1, of which 1 were waited for; matrix products, arithmetic and copies ran while one was open for 0% of the time, Pallas kernels for 1%

profile of v7, /device:TPU:1, one launch (start us, length us, event | category | flops | bytes accessed | tf_op | source)
XLA Modules:
  0.0 94.9 jit_solution(1229491223434097325)
XLA Ops:
  0.6 0.0 copy-start.10
  0.6 0.0 copy-start.12
  0.7 0.0 copy-start.1
  0.7 0.0 copy-start.8
  0.7 0.0 copy-start.5
  0.7 0.0 copy-start.14
  0.7 0.0 copy-start.13
  0.7 2.5 %norm_first.1 = bf16[8,192,128]{2,1,0:T(8,128)(2,1)} custom-call(bf16[12,96,128]{2,1,0:T(8,128)(2,1)} %x_ref.3, bf16[12,96,128]{2,1,0:T(8,128)(2,1)} %cot_ref.1, f32[2,128]{1,0:T(2,128)} %ln_gain_ref.1, f32[2,128]{1,0:T(2,128)} %shift_ref.5, bf16[2,4,128]{2,1,0:T(4,128)(2,1)} %bitcast.3), custom_call_target="tpu_custom_call" | custom-call | flops 100000000 | bytes 2000000 | tf_op jit(solution)/shard_map/norm_first/pallas_call | solution.py:499
  3.2 0.0 copy-start.4
  3.2 0.0 copy-start.16
  3.2 7.5 %all-to-all-start = ((bf16[8,192,128]{2,1,0:T(8,128)(2,1)}), bf16[8,192,128]{2,1,0:T(8,128)(2,1)S(1)}, u32[]{:S(2)}, u32[]{:S(2)}) async-start(bf16[8,192,128]{2,1,0:T(8,128)(2,1)} %norm_first.1), calls=%async_computation | async-start | bytes 786432 | tf_op jit(solution)/shard_map/all_to_all | solution.py:518
  10.8 1.0 %copy-done = bf16[12,96,128]{2,1,0:T(8,128)(2,1)S(1)} copy-done((bf16[12,96,128]{2,1,0:T(8,128)(2,1)S(1)}, bf16[12,96,128]{2,1,0:T(8,128)(2,1)}, u32[]{:S(2)}) %copy-start) | copy-done | bytes 294936
  11.7 0.9 copy-done.3
  12.7 0.7 copy-done.9
  13.4 0.7 copy-done.11
  14.1 0.7 copy-done.15
  14.7 1.0 %project_first.1 = (bf16[12,96,128]{2,1,0:T(8,128)(2,1)S(1)}, bf16[12,96,128]{2,1,0:T(8,128)(2,1)S(1)}, bf16[12,96,128]{2,1,0:T(8,128)(2,1)S(1)}, f32[12,96,128]...) custom-call(bf16[12,96,128]{2,1,0:T(8,128)(2,1)S(1)} %copy-done, ...), custom_call_target="tpu_custom_call" | custom-call | flops 100000000 | bytes 2000000 | tf_op jit(solution)/shard_map/project_first/pallas_call | solution.py:499
  15.8 0.0 copy-start.6
  15.8 0.8 copy-done.6
  16.6 5.9 %all-to-all-done.recv_ref.recv0_ref = bf16[8,192,128]{2,1,0:T(8,128)(2,1)S(1)} async-done(((bf16[8,192,128]{2,1,0:T(8,128)(2,1)}), bf16[8,192,128]{2,1,0:T(8,128)(2,1)S(1)}, u32[]{:S(2)}, u32[]{:S(2)}) %all-to-all-start) | async-done | bytes 393248 | tf_op jit(solution)/shard_map/all_to_all | solution.py:518
  22.5 0.0 copy-done.10
  22.5 0.0 copy-start.2
  22.5 2.0 %attend_first.1 = (f32[12,96,128]{2,1,0:T(8,128)S(1)}, bf16[1152,128]{1,0:T(8,128)(2,1)S(1)}, f32[12,4,96,96]{3,2,1,0:T(8,128)S(1)}, bf16[12,96,128]{2,1,0:T(8,1...) custom-call(bf16[12,96,128]{2,1,0:T(8,128)(2,1)S(1)} %copy-done.1, ...), custom_call_target="tpu_custom_call" | custom-call | flops 100000000 | bytes 2000000 | tf_op jit(solution)/shard_map/attend_first/pallas_call | solution.py:499
  24.5 14.9 %all_to_all.25.recv_ref = bf16[8,192,128]{2,1,0:T(8,128)(2,1)S(1)} all-to-all(bf16[8,192,128]{2,1,0:T(8,128)(2,1)S(1)} %get-tuple-element.48), channel_id=1, replica_groups=mesh['dap'=8,'dp'=32] {'dap'}, dimensions={0} | all-to-all | bytes 786432 | tf_op jit(solution)/shard_map/all_to_all | solution.py:518
  39.5 0.0 copy-done.16
  39.5 4.6 %second_module.1 = (bf16[8,192,128]{2,1,0:T(8,128)(2,1)S(1)}, f32[24,128]{1,0:T(8,128)S(1)}, bf16[1152,128]{1,0:T(8,128)(2,1)S(1)}, bf16[1152,512]{1,0:T(8,128)(...) custom-call(bf16[8,192,128]{2,1,0:T(8,128)(2,1)S(1)} %all_to_all.25.recv_ref, ...), custom_call_target="tpu_custom_call" | custom-call | flops 100000000 | bytes 2000000 | tf_op jit(solution)/shard_map/second_module/pallas_call | solution.py:499
  44.1 14.9 %all_to_all.26.recv_ref = bf16[8,192,128]{2,1,0:T(8,128)(2,1)S(1)} all-to-all(bf16[8,192,128]{2,1,0:T(8,128)(2,1)S(1)} %get-tuple-element.49), channel_id=1, replica_groups=mesh['dap'=8,'dp'=32] {'dap'}, dimensions={0} | all-to-all | bytes 786432 | tf_op jit(solution)/shard_map/all_to_all | solution.py:518
  59.1 3.8 %back_first.1 = (bf16[12,96,128]{2,1,0:T(8,128)(2,1)S(1)}, f32[12,96,128]{2,1,0:T(8,128)S(1)}, bf16[8,208,128]{2,1,0:T(8,128)(2,1)S(1)}, f32[16,128]{1,0:T(8,128)S(1)}) custom-call(bf16[8,192,128]{2,1,0:T(8,128)(2,1)S(1)} %all_to_all.26.recv_ref, bf16[12,96,128]{2,1,0:T(8,128)(2,1)S(1)} %copy-done.2, bf16[12,96,128]{2,1,0:T(8,128)(2,1)S(1)} %get-tuple-element.44.q_ref, ...), custom_call_target="tpu_custom_call" | custom-call | flops 100000000 | bytes 2000000 | tf_op jit(solution)/shard_map/back_first/pallas_call | solution.py:499
  62.9 15.7 %all_to_all.27.recv_ref = bf16[8,208,128]{2,1,0:T(8,128)(2,1)S(1)} all-to-all(bf16[8,208,128]{2,1,0:T(8,128)(2,1)S(1)} %get-tuple-element.63), channel_id=1, replica_groups=mesh['dap'=8,'dp'=32] {'dap'}, dimensions={0} | all-to-all | bytes 851968 | tf_op jit(solution)/shard_map/all_to_all | solution.py:518
  78.6 0.6 grad_sums.1
  79.2 14.3 %all_to_all.28.recv_ref = bf16[8,176,128]{2,1,0:T(8,128)(2,1)S(1)} all-to-all(bf16[8,176,128]{2,1,0:T(8,128)(2,1)S(1)} %get-tuple-element.67), channel_id=1, replica_groups=mesh['dap'=8,'dp'=32] {'dap'}, dimensions={0} | all-to-all | bytes 720896 | tf_op jit(solution)/shard_map/all_to_all | solution.py:518
  93.5 1.3 %weight_sums.1 = (bf16[12,96,128]{2,1,0:T(8,128)(2,1)}, f32[2,128]{1,0:T(2,128)}, f32[2,128]{1,0:T(2,128)}, f32[2,128,512]{2,1,0:T(8,128)}, f32[2,4,128]{2,1,0:T...) custom-call(bf16[8,176,128]{2,1,0:T(8,128)(2,1)S(1)} %all_to_all.28.recv_ref, ...), custom_call_target="tpu_custom_call" | custom-call | flops 100000000 | bytes 2000000 | tf_op jit(solution)/shard_map/weight_sums/pallas_call | solution.py:499
  (15 shorter events, 0.0 us)
Async XLA Ops:
  0.6 21.8 %copy-start.10 = (f32[2,128]{1,0:T(2,128)S(1)}, f32[2,128]{1,0:T(2,128)}, u32[]{:S(2)}) copy-start(f32[2,128]{1,0:T(2,128)} %ln_gain_ref.1) | copy-start | bytes 3076
  0.6 21.8 %copy-start.12 = (f32[2,128]{1,0:T(2,128)S(1)}, f32[2,128]{1,0:T(2,128)}, u32[]{:S(2)}) copy-start(f32[2,128]{1,0:T(2,128)} %shift_ref.5) | copy-start | bytes 3076
  0.7 21.8 %copy-start.1 = (bf16[12,96,128]{2,1,0:T(8,128)(2,1)S(1)}, bf16[12,96,128]{2,1,0:T(8,128)(2,1)}, u32[]{:S(2)}) copy-start(bf16[12,96,128]{2,1,0:T(8,128)(2,1)} %x_ref.3) | copy-start | bytes 884740
  0.7 21.8 %copy-start.8 = (bf16[2,128,4]{1,2,0:T(4,128)(2,1)S(1)}, bf16[2,128,4]{1,2,0:T(4,128)(2,1)}, u32[]{:S(2)}) copy-start(bf16[2,128,4]{1,2,0:T(4,128)(2,1)} %param.16) | copy-start | bytes 6148
  0.7 21.8 %copy-start.5 = (bf16[2,128,128]{2,1,0:T(8,128)(2,1)S(1)}, bf16[2,128,128]{2,1,0:T(8,128)(2,1)}, u32[]{:S(2)}) copy-start(bf16[2,128,128]{2,1,0:T(8,128)(2,1)} %wo_ref.5) | copy-start | bytes 196612
  0.7 21.8 %copy-start.14 = (f32[2,128]{1,0:T(2,128)S(1)}, f32[2,128]{1,0:T(2,128)}, u32[]{:S(2)}) copy-start(f32[2,128]{1,0:T(2,128)} %ob_ref.1) | copy-start | bytes 3076
  0.7 21.8 %copy-start.13 = (s32[96]{0:T(128)S(1)}, s32[96]{0:T(128)}, u32[]{:S(2)}) copy-start(s32[96]{0:T(128)} %param.12) | copy-start | bytes 1156
  3.2 36.3 %copy-start.4 = (bf16[2,128,512]{2,1,0:T(8,128)(2,1)S(1)}, bf16[2,128,512]{2,1,0:T(8,128)(2,1)}, u32[]{:S(2)}) copy-start(bf16[2,128,512]{2,1,0:T(8,128)(2,1)} %wp_ref.5) | copy-start | bytes 786436
  3.2 36.3 %copy-start.16 = (f32[2,128]{1,0:T(2,128)S(1)}, f32[2,128]{1,0:T(2,128)}, u32[]{:S(2)}) copy-start(f32[2,128]{1,0:T(2,128)} %gb_ref.3) | copy-start | bytes 3076
  3.2 19.2 %all-to-all-start = ((bf16[8,192,128]{2,1,0:T(8,128)(2,1)}), bf16[8,192,128]{2,1,0:T(8,128)(2,1)S(1)}, u32[]{:S(2)}, u32[]{:S(2)}) async-start(bf16[8,192,128]{2,1,0:T(8,128)(2,1)} %norm_first.1), calls=%async_computation | async-start | bytes 786432 | tf_op jit(solution)/shard_map/all_to_all | solution.py:518
  10.8 1.0 %copy-start = (bf16[12,96,128]{2,1,0:T(8,128)(2,1)S(1)}, bf16[12,96,128]{2,1,0:T(8,128)(2,1)}, u32[]{:S(2)}) copy-start(bf16[12,96,128]{2,1,0:T(8,128)(2,1)} %x_ref.3) | copy-start | bytes 884740
  11.7 0.9 %copy-start.3 = (bf16[2,128,512]{2,1,0:T(8,128)(2,1)S(1)}, bf16[2,128,512]{2,1,0:T(8,128)(2,1)}, u32[]{:S(2)}) copy-start(bf16[2,128,512]{2,1,0:T(8,128)(2,1)} %wp_ref.5) | copy-start | bytes 786436
  12.7 0.7 copy-start.9
  13.4 0.7 copy-start.11
  14.0 0.7 copy-start.15
  15.8 0.8 copy-start.6
  22.5 36.6 %copy-start.2 = (bf16[12,96,128]{2,1,0:T(8,128)(2,1)S(1)}, bf16[12,96,128]{2,1,0:T(8,128)(2,1)}, u32[]{:S(2)}) copy-start(bf16[12,96,128]{2,1,0:T(8,128)(2,1)} %cot_ref.1) | copy-start | bytes 884740
  62.9 30.7 %copy-start.7 = (f32[12,96,128]{2,1,0:T(8,128)S(1)}, f32[12,96,128]{2,1,0:T(8,128)}, u32[]{:S(2)}) copy-start(f32[12,96,128]{2,1,0:T(8,128)} %copy-done.6) | copy-start | bytes 1769476
